TPU v7x, 256 devices: a whole 4x4x8 slice. The times are simulated.
256 devices in a mesh: blk: 64 (over y, z_hi, x, core), rep: 4 (over z_lo).
Axes of the slice: x: 4, y: 4, z: 8 (z_hi: 2, z_lo: 4; z = z_hi * 4 + z_lo), core: 2. Of those that a mesh axis runs over, the one named last changes fastest.
Arguments:
- factors_in: float32 [16384, 256], P('blk', 'rep'), may hold values from -6 to 6
- items: float32 [8192, 256], P('blk', 'rep'), may hold values from -0.0625 to 0.0625
- tile_user: int32 [64, 128], P('blk', 'rep'), may hold values from 0 to 1
- levels: int32 [64, 128, 128, 128], P('blk', 'rep'), may hold values from 0 to 15
Outputs:
- factors: float32 [16384, 256], P('blk', 'rep')
- item_rhs: float32 [8192, 256], P('blk', 'rep')
All inputs are finite; a program needn't handle non-finite values.
Results may differ from a plain program's by a relative error of at most 0.0003.
Values sent between devices are 32-bit elements; how exact they have to be, the bound alone decides.
No kernel may reach another device: no remote copies, remote signals or barrier semaphores. Data moves between devices by JAX's collectives and lax.ppermute only.
A program may use at most 128 MiB of HBM per device.

v0:
```python
import jax
import jax.numpy as jnp
from jax import lax
from jax.sharding import PartitionSpec as P

ITERS = 2


precise = lax.Precision.HIGHEST
conf_scale = 0.1
ridge_term = 0.1


def per_device(factors_in, items, tile_user, levels):
    rep_count = lax.axis_size("rep")
    owners = lax.axis_size("blk")
    levels_dev = levels[0]
    users = tile_user[0]
    tile_size = levels_dev.shape[-1]
    half_count = levels_dev.shape[0]
    cols = items.shape[1]
    rank = cols * rep_count
    user_rows = factors_in.shape[0]
    blocks = user_rows // tile_size
    weight = conf_scale * levels_dev.astype(jnp.float32)
    target = jnp.where(levels_dev > 0, 1.0 + weight, 0.0)
    onehot = (users[:, None] == jnp.arange(blocks, dtype=jnp.int32)[None, :]).astype(jnp.float32)
    column_start = lax.axis_index("rep") * cols
    half_start = lax.axis_index("rep") % 2 * half_count
    scale = (rep_count // 2 * owners * tile_size) ** (-0.5)

    def local_tiles(first, count):
        local_index = first - half_start + jnp.arange(count, dtype=jnp.int32)
        inside = jnp.logical_and(local_index >= 0, local_index < half_count)
        clipped = jnp.clip(local_index, 0, half_count - 1)
        return (clipped, inside.astype(jnp.float32)[:, None, None])

    panel = lax.all_gather(items, "rep", axis=1, tiled=True)
    x_full = lax.all_gather(factors_in, "rep", axis=1, tiled=True)
    x_blocks = x_full.reshape(blocks, tile_size, rank)
    piece = lax.all_gather(panel, "blk", axis=0, tiled=True)
    gram = jnp.zeros((rank, rank), jnp.float32)
    count = piece.shape[0] // tile_size
    first = jnp.int32(0) // tile_size
    clipped, inside = local_tiles(first, count)
    part_panels = piece.reshape(count, tile_size, rank)
    part_rows = jnp.take(x_blocks, jnp.take(users, clipped, axis=0), axis=0)
    scores = jnp.einsum("ntr,nir->nti", part_rows, part_panels, precision=precise)
    mixed = (
        jnp.take(target, clipped, axis=0) - jnp.take(weight, clipped, axis=0) * scores
    ) * inside
    terms = jnp.einsum("nti,nir->ntr", mixed, part_panels, precision=precise)
    total = jnp.einsum("nb,ntr->btr", jnp.take(onehot, clipped, axis=0), terms, precision=precise)
    store = piece
    total, store, gram = (total, store, gram)
    local_gram = jnp.dot(panel.T, panel, precision=precise, preferred_element_type=jnp.float32)
    gram = lax.psum(local_gram, "blk")
    shifted = gram + ridge_term * jnp.eye(rank, dtype=jnp.float32)
    own_panels = lax.dynamic_slice_in_dim(
        store.reshape(owners, tile_size, rank), half_start, half_count, 0
    )
    start_terms = total.reshape(user_rows, rank)

    def combine_tiles(partial_value):
        return lax.psum(partial_value, "rep")

    resid = combine_tiles(start_terms) - jnp.dot(
        x_full, shifted, precision=precise, preferred_element_type=jnp.float32
    )
    solution = x_full
    direc = resid
    rho = jnp.sum(resid * resid, axis=1, keepdims=True)
    for step in range(ITERS):
        picked = jnp.take(direc.reshape(blocks, tile_size, rank), users, axis=0)
        tile_scores = jnp.einsum("ntr,nir->nti", picked, own_panels, precision=precise)
        tile_terms = jnp.einsum("nti,nir->ntr", weight * tile_scores, own_panels, precision=precise)
        image = combine_tiles(
            jnp.einsum("nb,ntr->btr", onehot, tile_terms, precision=precise).reshape(
                user_rows, rank
            )
        ) + jnp.dot(direc, shifted, precision=precise, preferred_element_type=jnp.float32)
        alpha = rho / jnp.sum(direc * image, axis=1, keepdims=True)
        solution = solution + alpha * direc
        resid = resid - alpha * image
        rho_next = jnp.sum(resid * resid, axis=1, keepdims=True)
        direc = resid + rho_next / rho * direc
        rho = rho_next
    factors = lax.dynamic_slice_in_dim(solution, column_start, cols, 1)
    final_blocks = solution.reshape(blocks, tile_size, rank)
    number = lax.axis_size("blk") * tile_size // tile_size
    first = jnp.int32(0) // tile_size
    clipped, inside = local_tiles(first, number)
    part_rows = jnp.take(final_blocks, jnp.take(users, clipped, axis=0), axis=0)
    part_target = jnp.take(target, clipped, axis=0) * inside
    summed = lax.psum_scatter(
        jnp.einsum("nti,ntr->nir", part_target, part_rows, precision=precise).reshape(
            lax.axis_size("blk") * tile_size, rank
        ),
        "blk",
        scatter_dimension=0,
        tiled=True,
    )
    item_rhs = lax.psum_scatter(summed, "rep", scatter_dimension=1, tiled=True) * scale
    return (factors, item_rhs)


def solution(mesh):
    placed = (P("blk", "rep"), P("blk", "rep"), P("blk", "rep"), P("blk", "rep", None, None))
    return jax.shard_map(
        per_device,
        mesh=mesh,
        in_specs=placed,
        out_specs=(P("blk", "rep"), P("blk", "rep")),
        check_vma=False,
    )
```

profile of v0, /device:TPU:6, one launch (start us, length us, event | category | flops | bytes accessed | tf_op | source)
XLA Modules:
  0.0 1566.1 jit_solution(5625363031460554414)
XLA Ops:
  7.2 16.6 %all_gather.10 = f32[128,256]{0,1:T(8,128)} all-gather(f32[128,64]{0,1:T(8,128)} %param.13), channel_id=1, replica_groups=mesh['blk'=64,'rep'=4] {'rep'}, dimensions={1}, use_global_device_ids=true | all-gather | bytes 163840 | tf_op jit(solution)/shard_map/all_gather | solution.py:38
  23.9 2.1 fusion.80
  26.1 4.2 add_select_fusion
  30.3 1.7 multiply_bitcast_fusion
  32.9 14.1 all_gather.9
  47.2 4.3 gather_fusion.1
  51.5 4.4 gather_fusion.2
  56.0 4.3 gather_fusion.4
  60.9 91.3 %all-gather.2.cloned.1.call-done = f32[8192,256]{0,1:T(8,128)} async-done(((f32[128,256]{0,1:T(8,128)}), f32[8192,256]{0,1:T(8,128)}) %all-gather.2.cloned.1.call-update) | async-done | bytes 8388624 | tf_op jit(solution)/shard_map/all_gather | solution.py:41
  152.3 9.2 copy.60
  161.4 15.8 %fusion.4 = f32[64,128,128]{2,1,0:T(8,128)} fusion(f32[64,128,256]{2,1,0:T(8,128)} %bitcast.52, f32[64,128,256]{2,1,0:T(8,128)} %gather_fusion.4, pred[64]{0:T(512)(128)(4,1)S(1)} %get-tuple-element.18), kind=kOutput, calls=%fused_computation.12 | convolution fusion | flops 3223322624 | bytes 20971584 | tf_op jit(solution)/shard_map/ntr,nir->nti/dot_general | solution.py:48
  177.2 18.8 %fusion.18 = f32[64,128,256]{2,1,0:T(8,128)} fusion(f32[64,128,256]{2,1,0:T(8,128)} %bitcast.53, f32[64,128,128]{2,1,0:T(8,128)} %fusion.4, f32[64,128,128]{2,1,0:T(8,128)} %gather_fusion.2, f32[64,128,128]{2,1,0:T(8,128)} %gather_fusion.1, f32[64]{0:T(128)S(1)} %and_convert_fusion, pred[64]{0:T(512)(128)(4,1)S(1)} %compare_and_fusion.2), kind=kOutput, calls=%fused_computation.27 | convolution fusion | flops 3226468352 | bytes 29360448 | tf_op jit(solution)/shard_map/nti,nir->ntr/dot_general | solution.py:52
  196.0 12.5 fusion
  209.4 661.9 %all-reduce.7.cloned.1.call-done = f32[256,256]{1,0:T(8,128)} async-done(((f32[256,256]{1,0:T(8,128)}), f32[256,256]{1,0:T(8,128)}) %all-reduce.7.cloned.1.call-update) | async-done | bytes 262160 | tf_op jit(solution)/shard_map/psum | solution.py:57
  871.3 66.3 %all-reduce.5.cloned.1.call-done = f32[256,256]{1,0:T(8,128)} async-done(((f32[256,256]{1,0:T(8,128)}), f32[256,256]{1,0:T(8,128)}) %all-reduce.5.cloned.1.call-update) | async-done | bytes 262160 | tf_op jit(solution)/shard_map/psum | solution.py:65
  937.6 1.6 fusion.44
  939.3 2.7 gather_fusion.5
  942.0 7.8 fusion.12
  949.8 5.7 fusion.28
  955.5 3.8 fusion.8
  960.4 48.0 %all-reduce.9.cloned.1.call-done = f32[256,256]{1,0:T(8,128)} async-done(((f32[256,256]{1,0:T(8,128)}), f32[256,256]{1,0:T(8,128)}) %all-reduce.9.cloned.1.call-update) | async-done | bytes 262160 | tf_op jit(solution)/shard_map/psum | solution.py:65
  1008.4 1.5 multiply_reduce_fusion.1
  1010.2 2.7 gather_fusion.6
  1012.9 7.8 fusion.10
  1020.8 5.7 fusion.25
  1026.5 3.8 fusion.6
  1031.3 47.9 %all-reduce.11.cloned.1.call-done = f32[256,256]{1,0:T(8,128)} async-done(((f32[256,256]{1,0:T(8,128)}), f32[256,256]{1,0:T(8,128)}) %all-reduce.11.cloned.1.call-update) | async-done | bytes 262160 | tf_op jit(solution)/shard_map/psum | solution.py:65
  1080.9 4.3 gather_fusion.7
  1085.1 16.1 %fusion.2 = f32[64,128,256]{2,1,0:T(8,128)} fusion(f32[64,128,256]{2,1,0:T(8,128)} %gather_fusion.7, pred[64]{0:T(512)(128)(4,1)S(1)} %get-tuple-element.18, f32[64,128,128]{2,1,0:T(8,128)} %gather_fusion.1, f32[64]{0:T(128)S(1)} %and_convert_fusion, pred[64]{0:T(512)(128)(4,1)S(1)} %compare_and_fusion.2), kind=kOutput, calls=%fused_computation.10 | convolution fusion | flops 3225419776 | bytes 20971904 | tf_op jit(solution)/shard_map/nti,ntr->nir/dot_general | solution.py:96
  1101.3 8.9 copy.71
  1110.3 397.4 %reduce-scatter.3.cloned.1.call-done = f32[128,256]{0,1:T(8,128)} async-done(((f32[8192,256]{0,1:T(8,128)}), f32[128,256]{0,1:T(8,128)}) %reduce-scatter.3.cloned.1.call-update) | async-done | bytes 131088 | tf_op jit(solution)/shard_map/reduce_scatter | solution.py:95
  1508.5 49.0 %reduce-scatter.5.cloned.1.call-done = f32[128,64]{0,1:T(8,128)} async-done(((f32[128,256]{0,1:T(8,128)}), f32[128,64]{0,1:T(8,128)}) %reduce-scatter.5.cloned.1.call-update) | async-done | bytes 32784 | tf_op jit(solution)/shard_map/reduce_scatter | solution.py:103
  (51 shorter events, 9.0 us)
Async XLA Ops:
  7.2 23.2 %copy-start.1 = (s32[1,32,128,128]{3,2,1,0:T(8,128)S(1)}, s32[1,32,128,128]{3,2,1,0:T(8,128)}, u32[]{:S(2)}) copy-start(s32[1,32,128,128]{3,2,1,0:T(8,128)} %param.15) | copy-start | bytes 6291460
  7.2 145.1 %all-gather.2.cloned.1.call-start = ((), (), s32[]{:S(2)}) async-start(), calls=%async_computation.2 | async-start | bytes 8519680 | tf_op jit(solution)/shard_map/all_gather | solution.py:41
  23.9 847.5 %all-reduce.7.cloned.1.call-start = ((), (), s32[]{:S(2)}) async-start(), calls=%async_computation.4 | async-start | bytes 524288 | tf_op jit(solution)/shard_map/psum | solution.py:57
  26.0 911.6 %all-reduce.5.cloned.1.call-start = ((), (), s32[]{:S(2)}) async-start(), calls=%async_computation.3 | async-start | bytes 524288 | tf_op jit(solution)/shard_map/psum | solution.py:65
  26.1 6.0 copy-start
  26.1 6.8 copy-start.3
  209.2 799.2 %all-reduce.9.cloned.1.call-start = ((), (), s32[]{:S(2)}) async-start(), calls=%async_computation.5 | async-start | bytes 524288 | tf_op jit(solution)/shard_map/psum | solution.py:65
  955.5 52.8 %copy-start.2 = (f32[256,256]{1,0:T(8,128)S(1)}, f32[256,256]{1,0:T(8,128)}, u32[]{:S(2)}) copy-start(f32[256,256]{1,0:T(8,128)} %all-reduce.7.cloned.1.call-done) | copy-start | bytes 786436
  960.1 119.2 %all-reduce.11.cloned.1.call-start = ((), (), s32[]{:S(2)}) async-start(), calls=%async_computation.6 | async-start | bytes 524288 | tf_op jit(solution)/shard_map/psum | solution.py:65
  1031.0 476.7 %reduce-scatter.3.cloned.1.call-start = ((), (), s32[]{:S(2)}) async-start(), calls=%async_computation.7 | async-start | bytes 8519680 | tf_op jit(solution)/shard_map/reduce_scatter | solution.py:95
  1110.2 447.3 %reduce-scatter.5.cloned.1.call-start = ((), (), s32[]{:S(2)}) async-start(), calls=%async_computation.8 | async-start | bytes 163840 | tf_op jit(solution)/shard_map/reduce_scatter | solution.py:103
Sparse Core Ops, SparseCore 0:
  24.0 128.2 all-gather.1
  154.9 716.4 all-reduce.6
  874.2 63.4 all-reduce.4
  960.2 48.0 all-reduce.8
  1031.1 48.0 all-reduce.10
  1110.3 397.3 reduce-scatter.2
  1510.2 47.2 reduce-scatter.4
where the time goes:
time: 1570 us
  waiting for transfers between devices  1360 us (87%)
  matrix products  104 us (7%)
  local copies, waits for them, and re-layouts  45.5 us (3%)
  blocking collectives  30.7 us (2%)
    psum x1, waiting for transfers between devices, per_device(): gram = lax.psum(local_gram, 'blk')  662 us
    reduce_scatter x1, waiting for transfers between devices, per_device(): lax.psum_scatter(jnp.einsum('nti,ntr->nir', part_target, part_rows, preci...  397 us
    psum x3, waiting for transfers between devices, combine_tiles(): return lax.psum(partial_value, 'rep')  162 us
    all_gather x1, waiting for transfers between devices, per_device(): piece = lax.all_gather(panel, 'blk', axis=0, tiled=True)  91.3 us
    reduce_scatter x1, waiting for transfers between devices, per_device(): lax.psum_scatter(summed, 'rep', scatter_dimension=1, tiled=True) * scale  49 us
  transfers between devices with their start and end apart: 7, of which 7 were waited for; matrix products, arithmetic and copies ran while one was open for 5% of the time, Pallas kernels for 0%

commit v1 on v0

v1 whole, which is shorter than its diff:
```python
import functools

import jax
import jax.numpy as jnp
import numpy as np
from jax import lax
from jax.experimental import pallas as pl
from jax.experimental.pallas import tpu as pltpu
from jax.sharding import Mesh, PartitionSpec as P

ITERS = 2
AXES = ("y", "zh", "x", "core", "rep")
SIZES = (4, 2, 4, 2, 4)
BLK = ("y", "zh", "x", "core")
RANK = 256
TILE = 128
HALF = TILE // 2
GROUPS = 8
WIDE = 4 * TILE
RIDGE = 0.1
STEP = 0.1
VMEM = 48 * 1024 * 1024
f32 = jnp.float32
bf16 = jnp.bfloat16


def split(value):
    high = value.astype(bf16)
    low = (value - high.astype(f32)).astype(bf16)
    return high, low


def dot(a, b):
    return lax.dot_general(a, b, (((1,), (0,)), ((), ())), preferred_element_type=f32)


def dot_t(a, b):
    return lax.dot_general(a, b, (((1,), (1,)), ((), ())), preferred_element_type=f32)


def scores_of(stacked, panel_hi, panel_lo):
    both = dot(stacked, panel_hi)
    return both[:TILE] + both[TILE:] + dot(stacked[:TILE], panel_lo)


def project(mixed, panel_hi, panel_lo):
    high, low = split(mixed)
    both = dot_t(jnp.concatenate([high, low], axis=0), panel_hi)
    return both[:TILE] + both[TILE:] + dot_t(high, panel_lo)


def store_split(vectors, stacked):
    high, low = split(vectors)
    stacked[:TILE] = high
    stacked[TILE:] = low


def first_kernel(scal, x0, panels, lev_a, lev_b, hi, lo, weight, target, part, stacked):
    i = pl.program_id(0)

    @pl.when(i == 0)
    def _():
        store_split(x0[...], stacked)
        part[...] = jnp.zeros_like(part)

    for j in range(4):
        cols = slice(j * TILE, (j + 1) * TILE)
        tile = j * GROUPS + i
        a1 = scal[1 + tile].astype(f32)
        b1 = scal[33 + tile].astype(f32)
        a0, b0 = 1.0 - a1, 1.0 - b1
        la = lev_a[j, 0, 0].astype(f32)
        lb = lev_b[j, 0].astype(f32)
        ta = la + jnp.where(la > 0, 10.0, 0.0)
        tb = lb + jnp.where(lb > 0, 10.0, 0.0)
        weight[0, :HALF, cols] = (10.0 + a0 * la + b0 * lb).astype(bf16)
        weight[0, HALF:, cols] = (10.0 + a1 * la + b1 * lb).astype(bf16)
        target[0, :HALF, cols] = a0 * ta + b0 * tb
        target[0, HALF:, cols] = a1 * ta + b1 * tb
        high, low = split(panels[0, j])
        hi[0, :, cols] = high
        lo[0, :, cols] = low
    scores = scores_of(stacked[...], hi[0], lo[0])
    mixed = STEP * (target[0] - weight[0].astype(f32) * scores)
    part[...] += project(mixed, hi[0], lo[0])


def apply_step(hi, lo, weight, part, stacked):
    scores = scores_of(stacked[...], hi[0], lo[0])
    mixed = STEP * (weight[0].astype(f32) * scores)
    part[...] += project(mixed, hi[0], lo[0])


def second_kernel(pa, pb, x0, hi, lo, weight, resid, part, stacked):
    @pl.when(pl.program_id(0) == 0)
    def _():
        start = pa[...] + pb[...] - RIDGE * x0[...]
        resid[...] = start
        store_split(start, stacked)
        part[...] = jnp.zeros_like(part)

    apply_step(hi, lo, weight, part, stacked)


def third_kernel(pa, pb, resid, x0, hi, lo, weight, x1, resid1, direc1, part, stacked):
    @pl.when(pl.program_id(0) == 0)
    def _():
        direc = resid[...]
        image = pa[...] + pb[...] + RIDGE * direc
        rho = jnp.sum(direc * direc, axis=1, keepdims=True)
        alpha = rho / jnp.sum(direc * image, axis=1, keepdims=True)
        x1[...] = x0[...] + alpha * direc
        after = direc - alpha * image
        resid1[...] = after
        rho_next = jnp.sum(after * after, axis=1, keepdims=True)
        ahead = after + (rho_next / rho) * direc
        direc1[...] = ahead
        store_split(ahead, stacked)
        part[...] = jnp.zeros_like(part)

    apply_step(hi, lo, weight, part, stacked)


def last_kernel(pa, pb, resid, direc, x1, out):
    image = pa[...] + pb[...] + RIDGE * direc[...]
    rho = jnp.sum(resid[...] * resid[...], axis=1, keepdims=True)
    alpha = rho / jnp.sum(direc[...] * image, axis=1, keepdims=True)
    out[...] = x1[...] + alpha * direc[...]


def rhs_kernel(scal, vectors, own, got, t1, t2, t3, out, total):
    x, core = scal[0], scal[1]
    for k in range(4):
        source = lax.rem(x + 4 - k, 4)
        for slot in range(2):
            src_core = core if slot == 0 else 1 - core
            chunk = vectors[source * 2 + src_core]
            if k == 0:
                tile = (own, got)[slot][x]
            else:
                tile = (t1, t2, t3)[k - 1][slot]
            tile = tile.astype(bf16)
            high, low = split(chunk.T)
            both = jnp.concatenate([high, low], axis=1)
            term = dot(both, jnp.concatenate([tile, tile], axis=0))
            if k == 0 and slot == 0:
                total[...] = term
            else:
                total[...] += term
    for j in range(4):
        out[j] = total[:, j * TILE : (j + 1) * TILE]


def spec(shape, index=None):
    if index is None:
        zeros = (0,) * len(shape)
        return pl.BlockSpec(shape, lambda *_: zeros)
    return pl.BlockSpec(shape, index)


def params():
    return pltpu.CompilerParams(vmem_limit_bytes=VMEM)


def cost(flops, moved):
    return pl.CostEstimate(flops=flops, bytes_accessed=moved, transcendentals=0)


APPLY_COST = 6 * 2 * TILE * GROUPS * WIDE * RANK


def panel_specs():
    return [
        spec((1, RANK, WIDE), lambda i, *_: (i, 0, 0)),
        spec((1, RANK, WIDE), lambda i, *_: (i, 0, 0)),
        spec((1, TILE, WIDE), lambda i, *_: (i, 0, 0)),
    ]


def shaped(*shape, dtype=f32):
    return jax.ShapeDtypeStruct(shape, dtype)


def first_apply(scal, x0, panels, lev_a, lev_b):
    whole = (TILE, RANK)
    return pl.pallas_call(
        first_kernel,
        grid_spec=pltpu.PrefetchScalarGridSpec(
            num_scalar_prefetch=1,
            grid=(GROUPS,),
            in_specs=[
                spec(whole),
                spec((1, 4, RANK, TILE), lambda i, s: (i, 0, 0, 0)),
                spec((4, 1, 1, HALF, TILE), lambda i, s: (0, i, s[0], 0, 0)),
                spec((4, 1, HALF, TILE), lambda i, s: (0, i, 0, 0)),
            ],
            out_specs=panel_specs()
            + [spec((1, TILE, WIDE), lambda i, s: (i, 0, 0)), spec(whole)],
            scratch_shapes=[pltpu.VMEM((2 * TILE, RANK), bf16)],
        ),
        out_shape=[
            shaped(GROUPS, RANK, WIDE, dtype=bf16),
            shaped(GROUPS, RANK, WIDE, dtype=bf16),
            shaped(GROUPS, TILE, WIDE, dtype=bf16),
            shaped(GROUPS, TILE, WIDE),
            shaped(*whole),
        ],
        compiler_params=params(),
        cost_estimate=cost(APPLY_COST, 14 << 20),
        name="first_apply",
    )(scal, x0, panels, lev_a, lev_b)


def next_apply(kernel, vectors, panels, outs, name):
    whole = (TILE, RANK)
    return pl.pallas_call(
        kernel,
        grid=(GROUPS,),
        in_specs=[spec(whole)] * len(vectors) + panel_specs(),
        out_specs=[spec(whole)] * outs,
        out_shape=[shaped(*whole)] * outs,
        scratch_shapes=[pltpu.VMEM((2 * TILE, RANK), bf16)],
        compiler_params=params(),
        cost_estimate=cost(APPLY_COST, 6 << 20),
        name=name,
    )(*vectors, *panels)


def shift(value, axis, size, by):
    return lax.ppermute(value, axis, [(i, (i + by) % size) for i in range(size)])


def flip(value, axis, size, bit):
    return lax.ppermute(value, axis, [(i, i ^ bit) for i in range(size)])


def pick(value, index, axis=0):
    return lax.dynamic_index_in_dim(value, index, axis, keepdims=False)


def per_device(factors_in, items, tile_user, levels):
    y, zh, x, core, rep = (lax.axis_index(name) for name in AXES)
    half, parity = rep // 2, rep % 2
    strip = RANK // 4

    packed = jnp.concatenate(
        [items.T[None], factors_in.T.reshape(strip, 2, TILE).transpose(1, 0, 2)], axis=0
    )
    column = lax.all_gather(packed, ("zh", "rep"), axis=0, tiled=False)
    lev = levels[0].reshape(32, 2, HALF, TILE)
    other = pick(lev, 1 - half, 1)
    other, column = lax.optimization_barrier((other, column))
    lev_b = flip(other, "rep", 4, 2)
    user_b = flip(tile_user, "rep", 4, 2)
    scal = jnp.concatenate([half[None].astype(jnp.int32), tile_user[0], user_b[0]])

    mine = lax.dynamic_slice(column, (zh * 4, 1, 0, half * HALF), (4, 2, strip, HALF))
    x0 = mine.transpose(1, 3, 0, 2).reshape(TILE, RANK)

    panel = column[:, 0].reshape(2, RANK, TILE)
    panel = lax.all_gather(panel, "y", axis=0, tiled=False)
    panel = lax.dynamic_slice_in_dim(panel, 2 * parity, 2, 0).reshape(4, RANK, TILE)
    panels = lax.all_gather(panel, ("x", "core"), axis=0, tiled=False)

    hi, lo, weight, target, part = first_apply(
        scal,
        x0,
        panels,
        lev.reshape(4, GROUPS, 2, HALF, TILE),
        lev_b.reshape(4, GROUPS, HALF, TILE),
    )
    shared = (hi, lo, weight)
    part_b = flip(part, "rep", 4, 1)

    target = target.reshape(4, 2, TILE, WIDE)
    own = pick(target, core, 1)
    got = flip(pick(target, 1 - core, 1), "core", 2, 1)
    moved = []
    for k in (1, 2, 3):
        to = (x + k) % 4
        moved.append(shift(jnp.stack([pick(own, to), pick(got, to)]), "x", 4, k))

    resid, part = next_apply(second_kernel, (part, part_b, x0), shared, 2, "second_apply")
    part_b = flip(part, "rep", 4, 1)
    x1, resid1, direc1, part = next_apply(
        third_kernel, (part, part_b, resid, x0), shared, 4, "third_apply"
    )
    part_b = flip(part, "rep", 4, 1)
    solved = pl.pallas_call(
        last_kernel,
        out_shape=shaped(TILE, RANK),
        compiler_params=params(),
        cost_estimate=cost(TILE * RANK * 10, 6 * TILE * RANK * 4),
        name="last_update",
    )(part, part_b, resid1, direc1, x1)

    vectors = lax.all_gather(solved, ("x", "core"), axis=0, tiled=False)

    strips = solved.reshape(TILE, 4, strip)
    sent = flip(pick(strips, rep ^ 2, 1), "rep", 4, 2)
    kept = pick(strips, rep, 1)
    low = jnp.where(half == 0, kept, sent).reshape(2, HALF, strip)
    high = jnp.where(half == 0, sent, kept).reshape(2, HALF, strip)
    factors = jnp.stack([low, high], axis=1).reshape(2 * TILE, strip)

    smem = pl.BlockSpec(memory_space=pltpu.SMEM)
    vmem = pl.BlockSpec(memory_space=pltpu.VMEM)
    terms = pl.pallas_call(
        rhs_kernel,
        in_specs=[smem] + [vmem] * 6,
        out_shape=shaped(4, RANK, TILE),
        scratch_shapes=[pltpu.VMEM((RANK, WIDE), f32)],
        compiler_params=params(),
        cost_estimate=cost(4 * 1024 * RANK * WIDE, 4 << 20),
        name="rhs_terms",
    )(jnp.stack([x, core]).astype(jnp.int32), vectors, own, got, *moved)

    terms = terms.reshape(2, 2 * RANK, TILE)
    near, far = pick(terms, y % 2), pick(terms, 1 - y % 2)

    def along_y(value, move, inside):
        pairs = [
            (s * 4 + r, move(s) * 4 + r)
            for s in range(4)
            for r in range(4)
            if (s // 2 == r % 2) == inside
        ]
        return lax.ppermute(value, ("y", "rep"), pairs)

    summed = (
        near
        + along_y(far, lambda s: s ^ 1, True)
        + along_y(far, lambda s: 3 - s, False)
        + along_y(near, lambda s: (s + 2) % 4, False)
    )
    pieces = lax.all_to_all(
        summed.reshape(8, strip, TILE), ("zh", "rep"), split_axis=0, concat_axis=0, tiled=True
    )
    chosen = pick(pieces.reshape(2, 2, 2, strip, TILE), y // 2, 2)
    scale = (2 * 64 * TILE) ** -0.5
    item_rhs = jnp.sum(chosen, axis=(0, 1)).T * (scale * STEP)
    return factors, item_rhs


def solution(mesh):
    fine = Mesh(np.asarray(mesh.devices).reshape(SIZES), AXES)
    rows = P(BLK, "rep")
    return jax.shard_map(
        per_device,
        mesh=fine,
        in_specs=(rows, rows, rows, P(BLK, "rep", None, None)),
        out_specs=(rows, rows),
        check_vma=False,
    )
```

time: 1570 us -> 238 us (0.15)
  waiting for transfers between devices: 1360 us -> 125 us
  matrix products: 104 us -> 0 us
  local copies, waits for them, and re-layouts: 45.5 us -> 15.6 us
  starting transfers between devices: 0.93 us -> 25.1 us
  Pallas kernels: 0 us -> 22.1 us
    psum x4 -> x0, waiting for transfers between devices: 824 us -> none  [the longest x1 662 us: per_device(): gram = lax.psum(local_gram, 'blk')]
    reduce_scatter x2 -> x0, waiting for transfers between devices: 446 us -> none  [the longest x1 397 us: per_device(): lax.psum_scatter(jnp.einsum('nti,ntr->nir', part_target, part_rows, preci...]
    dot_general x14 -> x0, matrix products: 104 us -> none  [the longest x1 18.8 us: per_device(): terms = jnp.einsum('nti,nir->ntr', mixed, part_panels, precision=precise)]
    ppermute x0 -> x13, waiting for transfers between devices: none -> 97.1 us  [the longest x7 60.7 us: flip(): return lax.ppermute(value, axis, [(i, i ^ bit) for i in range(size)])]
    all_gather x1 -> x3, waiting for transfers between devices: 91.3 us -> 25.9 us  [the longest x1 25.9 us: per_device(): panel = lax.all_gather(panel, 'y', axis=0, tiled=False)]
    gather x8 -> x0, local copies, waits for them, and re-layouts: 24.2 us -> none  [the longest x2 5.48 us: per_device(): picked = jnp.take(direc.reshape(blocks, tile_size, rank), users, axis=0)]
    pallas_call x0 -> x5, Pallas kernels: none -> 22.1 us  [the longest x2 11.1 us: next_apply(): pl.pallas_call(kernel, grid=(GROUPS,), in_specs=[spec(whole)] * len(vecto...]
    ppermute x0 -> x13, starting transfers between devices: none -> 17.7 us  [the longest x7 8.82 us: flip(): return lax.ppermute(value, axis, [(i, i ^ bit) for i in range(size)])]
  transfers between devices with their start and end apart: 7 -> 17, of which waited for: 7 -> 11; matrix products, arithmetic and copies ran while one was open for 5% -> 3% of each run, Pallas kernels for 0% -> 3%
where the time goes in v1:
time: 238 us; the launch traced here: 236 us
  waiting for transfers between devices  125 us (53%)
  blocking collectives  29.8 us (13%)
  starting transfers between devices  25.1 us (11%)
  Pallas kernels  22.1 us (9%)
  local copies, waits for them, and re-layouts  15.6 us (7%)
  between operations  14 us (6%)
  other arithmetic  4.91 us (2%)
    ppermute x7, waiting for transfers between devices, flip(): return lax.ppermute(value, axis, [(i, i ^ bit) for i in range(size)])  60.7 us
    all_gather x1, blocking collectives, per_device(): column = lax.all_gather(packed, ('zh', 'rep'), axis=0, tiled=False)  29.8 us
    all_gather x1, waiting for transfers between devices, per_device(): panel = lax.all_gather(panel, 'y', axis=0, tiled=False)  25.9 us
    ppermute x3, waiting for transfers between devices, shift(): lax.ppermute(value, axis, [(i, (i + by) % size) for i in range(size)])  23.1 us
    ppermute x3, waiting for transfers between devices, along_y(): return lax.ppermute(value, ('y', 'rep'), pairs)  13.2 us
    pallas_call x2, Pallas kernels, next_apply(): pl.pallas_call(kernel, grid=(GROUPS,), in_specs=[spec(whole)] * len(vecto...  11.1 us
    ppermute x7, starting transfers between devices, flip(): return lax.ppermute(value, axis, [(i, i ^ bit) for i in range(size)])  8.82 us
    pallas_call x1, Pallas kernels, first_apply(): pl.pallas_call(first_kernel, grid_spec=pltpu.PrefetchScalarGridSpec(num_s...  8.35 us
  transfers between devices with their start and end apart: 17, of which 11 were waited for; matrix products, arithmetic and copies ran while one was open for 3% of the time, Pallas kernels for 3%

profile of v1, /device:TPU:6, one launch (start us, length us, event | category | flops | bytes accessed | tf_op | source)
XLA Modules:
  0.0 236.1 jit_solution(14319673430190570954)
XLA Ops:
  8.9 29.8 %all-gather = f32[24,64,128]{2,1,0:T(8,128)S(1)} all-gather(f32[3,64,128]{2,1,0:T(8,128)S(1)} %copy.15), channel_id=2, replica_groups=mesh['y'=4,'zh'=2,'x'=4,'core'=2,'rep'=4] {'zh','rep'}, dimensions={0}, use_global_device_ids=true | all-gather | bytes 884736 | tf_op jit(solution)/shard_map/all_gather | solution.py:249
  38.8 1.3 dynamic-slice_bitcast_fusion.2
  40.9 25.9 %all-gather.6.cloned.1.call-done = f32[4,2,256,128]{3,2,1,0:T(8,128)} async-done(((f32[1,2,256,128]{3,2,1,0:T(8,128)}), f32[4,2,256,128]{3,2,1,0:T(8,128)}) %all-gather.6.cloned.1.call-update) | async-done | bytes 1048592 | tf_op jit(solution)/shard_map/all_gather | solution.py:261
  66.8 1.9 constant_dynamic-slice_fusion.3
  68.7 2.6 %collective-permute-start.1 = (s32[32,64,128]{2,1,0:T(8,128)S(1)}, s32[32,64,128]{2,1,0:T(8,128)S(1)}, u32[]{:S(2)}, u32[]{:S(2)}) collective-permute-start(s32[32,64,128]{2,1,0:T(8,128)S(1)} %dynamic-slice_bitcast_fusion.2), channel_id=1, source_target_pairs={{0,2},{1,3},{2,0},{3,1},{4,6},{5,7},{6,4},{7,5},{8,10},{9,11},{10,... | collective-permute-start | bytes 3145736 | tf_op jit(solution)/shard_map/ppermute | solution.py:234
  72.2 44.0 %collective-permute-done = s32[1,32]{1,0:T(1,128)S(1)} collective-permute-done((s32[1,32]{1,0:T(1,128)S(1)}, s32[1,32]{1,0:T(1,128)S(1)}, u32[]{:S(2)}, u32[]{:S(2)}) %collective-permute-start) | collective-permute-done | bytes 160 | tf_op jit(solution)/shard_map/ppermute | solution.py:234
  116.3 8.3 %first_apply.1 = (bf16[8,256,512]{2,1,0:T(8,128)(2,1)S(1)}, bf16[8,256,512]{2,1,0:T(8,128)(2,1)}, bf16[8,128,512]{2,1,0:T(8,128)(2,1)S(1)}, f32[8,128,512]{2,1,0:T(8,128)}, f32[128,256]{1,0:T(8,128)S(1)}) custom-call(s32[65]{0:T(128)S(1)} %pad_add_fusion.scal, f32[128,256]{1,0:T(8,128)S(1)} %reshape.35.x0, ...), custom_call_target="tpu_custom_call" | custom-call | flops 1610612736 | bytes 14680064 | tf_op jit(solution)/shard_map/first_apply/pallas_call | solution.py:186
  124.7 1.3 copy-done.1
  126.6 4.4 %collective-permute-done.2.pb = f32[128,256]{1,0:T(8,128)S(1)} collective-permute-done((f32[128,256]{1,0:T(8,128)S(1)}, f32[128,256]{1,0:T(8,128)S(1)}, u32[]{:S(2)}, u32[]{:S(2)}) %collective-permute-start.2) | collective-permute-done | bytes 131104 | tf_op jit(solution)/shard_map/ppermute | solution.py:234
  131.0 1.6 copy-done.2
  132.6 1.6 copy-done.4
  134.2 4.3 %second_apply.1 = (f32[128,256]{1,0:T(8,128)S(1)}, f32[128,256]{1,0:T(8,128)S(1)}) custom-call(f32[128,256]{1,0:T(8,128)S(1)} %get-tuple-element.17.pa, f32[128,256]{1,0:T(8,128)S(1)} %collective-permute-done.2.pb, f32[128,256]{1,0:T(8,128)S(1)} %reshape.35.x0, bf16[8,256,512]{2,1,0:T(8,128)(2,1)S(1)} %copy-done.2, bf16[8,256,512]{2,1,0:T(8,128)(2,1)S(1)} %copy-done.4, ...), custom_call_target="tpu_custom_call" | custom-call | flops 1610612736 | bytes 6291456 | tf_op jit(solution)/shard_map/second_apply/pallas_call | solution.py:216
  139.7 1.2 dynamic-slice_bitcast_fusion
  140.9 2.7 %collective-permute-done.3.pb = f32[128,256]{1,0:T(8,128)S(1)} collective-permute-done((f32[128,256]{1,0:T(8,128)S(1)}, f32[128,256]{1,0:T(8,128)S(1)}, u32[]{:S(2)}, u32[]{:S(2)}) %collective-permute-start.3) | collective-permute-done | bytes 131104 | tf_op jit(solution)/shard_map/ppermute | solution.py:234
  143.6 6.8 %third_apply.1 = (f32[128,256]{1,0:T(8,128)S(1)}, f32[128,256]{1,0:T(8,128)S(1)}, f32[128,256]{1,0:T(8,128)S(1)}, f32[128,256]{1,0:T(8,128)S(1)}) custom-call(f32[128,256]{1,0:T(8,128)S(1)} %get-tuple-element.21.pa, f32[128,256]{1,0:T(8,128)S(1)} %collective-permute-done.3.pb, f32[128,256]{1,0:T(8,128)S(1)} %get-tuple-element.22.resid, ...), custom_call_target="tpu_custom_call" | custom-call | flops 1610612736 | bytes 6291456 | tf_op jit(solution)/shard_map/third_apply/pallas_call | solution.py:216
  151.5 3.9 %collective-permute-done.4.pb = f32[128,256]{1,0:T(8,128)S(1)} collective-permute-done((f32[128,256]{1,0:T(8,128)S(1)}, f32[128,256]{1,0:T(8,128)S(1)}, u32[]{:S(2)}, u32[]{:S(2)}) %collective-permute-start.4) | collective-permute-done | bytes 131104 | tf_op jit(solution)/shard_map/ppermute | solution.py:234
  156.3 1.2 dynamic-slice_bitcast_fusion.5
  160.1 1.2 collective-permute-start.8
  162.1 2.1 collective-permute-start.7
  164.2 20.8 %collective-permute-done.9.t3 = f32[2,128,512]{2,1,0:T(8,128)S(1)} collective-permute-done((f32[2,128,512]{2,1,0:T(8,128)}, f32[2,128,512]{2,1,0:T(8,128)S(1)}, u32[]{:S(2)}, u32[]{:S(2)}) %collective-permute-start.9) | collective-permute-done | bytes 524320 | tf_op jit(solution)/shard_map/ppermute | solution.py:230
  185.0 2.3 collective-permute-done.7.t1
  187.3 1.2 copy-done
  188.6 1.8 rhs_terms.1
  190.4 2.2 collective-permute-start.10
  192.6 1.3 collective-permute-start.11
  193.9 1.3 collective-permute-start.12
  196.2 4.5 %collective-permute-done.10 = f32[512,128]{1,0:T(8,128)S(1)} collective-permute-done((f32[512,128]{1,0:T(8,128)S(1)}, f32[512,128]{1,0:T(8,128)S(1)}, u32[]{:S(2)}, u32[]{:S(2)}) %collective-permute-start.10) | collective-permute-done | bytes 262176 | tf_op jit(solution)/shard_map/ppermute | solution.py:328
  200.7 8.8 %collective-permute-done.11 = f32[512,128]{1,0:T(8,128)S(1)} collective-permute-done((f32[512,128]{1,0:T(8,128)S(1)}, f32[512,128]{1,0:T(8,128)S(1)}, u32[]{:S(2)}, u32[]{:S(2)}) %collective-permute-start.11) | collective-permute-done | bytes 262176 | tf_op jit(solution)/shard_map/ppermute | solution.py:328
  210.2 7.3 %all-to-all-start = ((f32[8,64,128]{2,1,0:T(8,128)}), f32[8,64,128]{2,1,0:T(8,128)S(1)}, u32[]{:S(2)}, u32[]{:S(2)}) async-start(f32[8,64,128]{2,1,0:T(8,128)} %bitcast.30), calls=%async_computation | async-start | bytes 524288 | tf_op jit(solution)/shard_map/all_to_all | solution.py:336
  217.5 2.9 %collective-permute-start.5 = (f32[128,64]{0,1:T(8,128)S(1)}, f32[128,64]{0,1:T(8,128)S(1)}, u32[]{:S(2)}, u32[]{:S(2)}) collective-permute-start(f32[128,64]{0,1:T(8,128)S(1)} %dynamic-slice_bitcast_fusion.9), channel_id=1, source_target_pairs={{0,2},{1,3},{2,0},{3,1},{4,6},{5,7},{6,4},{7,5},{8,10},{9,11},{10,... | collective-permute-start | bytes 98312 | tf_op jit(solution)/shard_map/ppermute | solution.py:234
  220.5 5.7 %collective-permute-done.5 = f32[128,64]{0,1:T(8,128)S(1)} collective-permute-done((f32[128,64]{0,1:T(8,128)S(1)}, f32[128,64]{0,1:T(8,128)S(1)}, u32[]{:S(2)}, u32[]{:S(2)}) %collective-permute-start.5) | collective-permute-done | bytes 32800 | tf_op jit(solution)/shard_map/ppermute | solution.py:234
  227.4 1.6 all-to-all-done
  (54 shorter events, 14.3 us)
Async XLA Ops:
  7.2 59.6 %all-gather.6.cloned.1.call-start = ((), (), s32[]{:S(2)}) async-start(), calls=%async_computation.1 | async-start | bytes 1310720 | tf_op jit(solution)/shard_map/all_gather | solution.py:261
  38.8 32.6 %copy-start.6 = (s32[1,32]{1,0:T(1,128)S(1)}, s32[1,32]{1,0:T(1,128)}, u32[]{:S(2)}) copy-start(s32[1,32]{1,0:T(1,128)} %param.6) | copy-start | bytes 388
  40.8 75.5 %all-gather.8.cloned.1.call-start = ((), (), s32[]{:S(2)}) async-start(), calls=%async_computation.2 | async-start | bytes 4718592 | tf_op jit(solution)/shard_map/all_gather | solution.py:263
  68.7 118.7 %all-gather.10.cloned.1.call-start = ((), (), s32[]{:S(2)}) async-start(), calls=%async_computation.3 | async-start | bytes 1179648 | tf_op jit(solution)/shard_map/all_gather | solution.py:297
  68.7 47.6 %collective-permute-start.1 = (s32[32,64,128]{2,1,0:T(8,128)S(1)}, s32[32,64,128]{2,1,0:T(8,128)S(1)}, u32[]{:S(2)}, u32[]{:S(2)}) collective-permute-start(s32[32,64,128]{2,1,0:T(8,128)S(1)} %dynamic-slice_bitcast_fusion.2), channel_id=1, source_target_pairs={{0,2},{1,3},{2,0},{3,1},{4,6},{5,7},{6,4},{7,5},{8,10},{9,11},{10,... | collective-permute-start | bytes 3145736 | tf_op jit(solution)/shard_map/ppermute | solution.py:234
  71.4 44.9 %collective-permute-start = (s32[1,32]{1,0:T(1,128)S(1)}, s32[1,32]{1,0:T(1,128)S(1)}, u32[]{:S(2)}, u32[]{:S(2)}) collective-permute-start(s32[1,32]{1,0:T(1,128)S(1)} %copy-done.6), channel_id=1, source_target_pairs={{0,2},{1,3},{2,0},{3,1},{4,6},{5,7},{6,4},{7,5},{8,10},{9,11},{10,... | collective-permute-start | bytes 392 | tf_op jit(solution)/shard_map/ppermute | solution.py:234
  124.7 1.3 copy-start.1
  126.0 5.0 %collective-permute-start.2 = (f32[128,256]{1,0:T(8,128)S(1)}, f32[128,256]{1,0:T(8,128)S(1)}, u32[]{:S(2)}, u32[]{:S(2)}) collective-permute-start(f32[128,256]{1,0:T(8,128)S(1)} %get-tuple-element.17.pa), channel_id=1, source_target_pairs={{0,1},{1,0},{2,3},{3,2},{4,5},{5,4},{6,7},{7,6},{8,9},{9,8},{10,11... | collective-permute-start | bytes 393224 | tf_op jit(solution)/shard_map/ppermute | solution.py:234
  131.0 1.6 copy-start.2
  132.6 1.6 copy-start.4
  134.2 5.5 %copy-start.5 = (f32[8,128,512]{2,1,0:T(8,128)S(1)}, f32[8,128,512]{2,1,0:T(8,128)}, u32[]{:S(2)}) copy-start(f32[8,128,512]{2,1,0:T(8,128)} %get-tuple-element.27) | copy-start | bytes 6291460
  138.5 5.1 %collective-permute-start.3 = (f32[128,256]{1,0:T(8,128)S(1)}, f32[128,256]{1,0:T(8,128)S(1)}, u32[]{:S(2)}, u32[]{:S(2)}) collective-permute-start(f32[128,256]{1,0:T(8,128)S(1)} %get-tuple-element.21.pa), channel_id=1, source_target_pairs={{0,1},{1,0},{2,3},{3,2},{4,5},{5,4},{6,7},{7,6},{8,9},{9,8},{10,11... | collective-permute-start | bytes 393224 | tf_op jit(solution)/shard_map/ppermute | solution.py:234
  139.7 3.9 %copy-start.3 = (bf16[8,256,512]{2,1,0:T(8,128)(2,1)S(1)}, bf16[8,256,512]{2,1,0:T(8,128)(2,1)}, u32[]{:S(2)}) copy-start(bf16[8,256,512]{2,1,0:T(8,128)(2,1)} %copy-done.1) | copy-start | bytes 6291460
  140.9 16.6 %collective-permute-start.6 = (f32[4,128,512]{2,1,0:T(8,128)}, f32[4,128,512]{2,1,0:T(8,128)S(1)}, u32[]{:S(2)}, u32[]{:S(2)}) collective-permute-start(f32[4,128,512]{2,1,0:T(8,128)} %get-tuple-element.31), channel_id=1, source_target_pairs={{0,4},{4,0},{1,5},{5,1},{2,6},{6,2},{3,7},{7,3},{8,12},{12,8},{9,1... | collective-permute-start | bytes 3145736 | tf_op jit(solution)/shard_map/ppermute | solution.py:234
  150.4 5.1 %collective-permute-start.4 = (f32[128,256]{1,0:T(8,128)S(1)}, f32[128,256]{1,0:T(8,128)S(1)}, u32[]{:S(2)}, u32[]{:S(2)}) collective-permute-start(f32[128,256]{1,0:T(8,128)S(1)} %get-tuple-element.23.pa), channel_id=1, source_target_pairs={{0,1},{1,0},{2,3},{3,2},{4,5},{5,4},{6,7},{7,6},{8,9},{9,8},{10,11... | collective-permute-start | bytes 393224 | tf_op jit(solution)/shard_map/ppermute | solution.py:234
  158.4 26.6 %collective-permute-start.9 = (f32[2,128,512]{2,1,0:T(8,128)}, f32[2,128,512]{2,1,0:T(8,128)S(1)}, u32[]{:S(2)}, u32[]{:S(2)}) collective-permute-start(f32[2,128,512]{2,1,0:T(8,128)} %pad_maximum_fusion.2), channel_id=1, source_target_pairs={{0,24},{8,0},{16,8},{24,16},{1,25},{9,1},{17,9},{25,17},{2,26},{10... | collective-permute-start | bytes 1572872 | tf_op jit(solution)/shard_map/ppermute | solution.py:230
  160.1 24.9 %collective-permute-start.8 = (f32[2,128,512]{2,1,0:T(8,128)}, f32[2,128,512]{2,1,0:T(8,128)S(1)}, u32[]{:S(2)}, u32[]{:S(2)}) collective-permute-start(f32[2,128,512]{2,1,0:T(8,128)} %pad_maximum_fusion.1), channel_id=1, source_target_pairs={{0,16},{8,24},{16,0},{24,8},{1,17},{9,25},{17,1},{25,9},{2,18},{10... | collective-permute-start | bytes 1572872 | tf_op jit(solution)/shard_map/ppermute | solution.py:230
  162.1 25.3 %collective-permute-start.7 = (f32[2,128,512]{2,1,0:T(8,128)}, f32[2,128,512]{2,1,0:T(8,128)}, u32[]{:S(2)}, u32[]{:S(2)}) collective-permute-start(f32[2,128,512]{2,1,0:T(8,128)} %pad_maximum_fusion), channel_id=1, source_target_pairs={{0,8},{8,16},{16,24},{24,0},{1,9},{9,17},{17,25},{25,1},{2,10},{10... | collective-permute-start | bytes 1572872 | tf_op jit(solution)/shard_map/ppermute | solution.py:230
  187.3 1.2 copy-start
  190.4 10.3 %collective-permute-start.10 = (f32[512,128]{1,0:T(8,128)S(1)}, f32[512,128]{1,0:T(8,128)S(1)}, u32[]{:S(2)}, u32[]{:S(2)}) collective-permute-start(f32[512,128]{1,0:T(8,128)S(1)} %get-tuple-element.36), channel_id=1, source_target_pairs={{0,64},{2,66},{64,0},{66,2},{129,193},{131,195},{193,129},{195,131... | collective-permute-start | bytes 786440 | tf_op jit(solution)/shard_map/ppermute | solution.py:328
  192.6 16.8 %collective-permute-start.11 = (f32[512,128]{1,0:T(8,128)S(1)}, f32[512,128]{1,0:T(8,128)S(1)}, u32[]{:S(2)}, u32[]{:S(2)}) collective-permute-start(f32[512,128]{1,0:T(8,128)S(1)} %get-tuple-element.36), channel_id=1, source_target_pairs={{1,193},{3,195},{65,129},{67,131},{128,64},{130,66},{192,0},{194,2... | collective-permute-start | bytes 786440 | tf_op jit(solution)/shard_map/ppermute | solution.py:328
  193.9 15.5 %collective-permute-start.12 = (f32[512,128]{1,0:T(8,128)S(1)}, f32[512,128]{1,0:T(8,128)S(1)}, u32[]{:S(2)}, u32[]{:S(2)}) collective-permute-start(f32[512,128]{1,0:T(8,128)S(1)} %get-tuple-element.37), channel_id=1, source_target_pairs={{1,129},{3,131},{65,193},{67,195},{128,0},{130,2},{192,64},{194,66... | collective-permute-start | bytes 786440 | tf_op jit(solution)/shard_map/ppermute | solution.py:328
  210.2 18.7 %all-to-all-start = ((f32[8,64,128]{2,1,0:T(8,128)}), f32[8,64,128]{2,1,0:T(8,128)S(1)}, u32[]{:S(2)}, u32[]{:S(2)}) async-start(f32[8,64,128]{2,1,0:T(8,128)} %bitcast.30), calls=%async_computation | async-start | bytes 524288 | tf_op jit(solution)/shard_map/all_to_all | solution.py:336
  217.5 8.7 %collective-permute-start.5 = (f32[128,64]{0,1:T(8,128)S(1)}, f32[128,64]{0,1:T(8,128)S(1)}, u32[]{:S(2)}, u32[]{:S(2)}) collective-permute-start(f32[128,64]{0,1:T(8,128)S(1)} %dynamic-slice_bitcast_fusion.9), channel_id=1, source_target_pairs={{0,2},{1,3},{2,0},{3,1},{4,6},{5,7},{6,4},{7,5},{8,10},{9,11},{10,... | collective-permute-start | bytes 98312 | tf_op jit(solution)/shard_map/ppermute | solution.py:234
Sparse Core Ops, SparseCore 0:
  40.9 25.7 all-gather.5
  68.8 33.1 all-gather.7
  156.4 30.8 all-gather.9

commit v2 on v1

v2 whole, which is shorter than its diff:
```python
import functools

import jax
import jax.numpy as jnp
import numpy as np
from jax import lax
from jax.experimental import pallas as pl
from jax.experimental.pallas import tpu as pltpu
from jax.sharding import Mesh, PartitionSpec as P

ITERS = 2
AXES = ("y", "zh", "x", "core", "rep")
SIZES = (4, 2, 4, 2, 4)
BLK = ("y", "zh", "x", "core")
RANK = 256
TILE = 128
HALF = TILE // 2
GROUPS = 8
WIDE = 4 * TILE
RIDGE = 0.1
STEP = 0.1
f32 = jnp.float32
bf16 = jnp.bfloat16


def split(value):
    high = value.astype(bf16)
    low = (value - high.astype(f32)).astype(bf16)
    return high, low


def dot(a, b):
    return lax.dot_general(a, b, (((1,), (0,)), ((), ())), preferred_element_type=f32)


def dot_t(a, b):
    return lax.dot_general(a, b, (((1,), (1,)), ((), ())), preferred_element_type=f32)


def scores_of(stacked, panel_hi, panel_lo):
    both = dot(stacked, panel_hi)
    return both[:TILE] + both[TILE:] + dot(stacked[:TILE], panel_lo)


def project(mixed, panel_hi, panel_lo):
    high, low = split(mixed)
    both = dot_t(jnp.concatenate([high, low], axis=0), panel_hi)
    return both[:TILE] + both[TILE:] + dot_t(high, panel_lo)


def store_split(vectors, stacked):
    high, low = split(vectors)
    stacked[:TILE] = high
    stacked[TILE:] = low


def scores_kernel(
    x0_t, own, far, own_hi, own_lo, far_hi, far_lo, own_scores, far_scores, x0, stacked
):
    @pl.when(pl.program_id(0) == 0)
    def _():
        start = x0_t[...].T
        x0[...] = start
        store_split(start, stacked)

    sides = ((own, own_hi, own_lo, own_scores), (far, far_hi, far_lo, far_scores))
    for panels, hi, lo, scores in sides:
        for j in range(4):
            cols = slice(j * TILE, (j + 1) * TILE)
            high, low = split(panels[0, j])
            hi[0, :, cols] = high
            lo[0, :, cols] = low
        scores[0] = scores_of(stacked[...], hi[0], lo[0])


def first_kernel(scal, *refs):
    (
        own_scores, far_scores, own_hi, own_lo, far_hi, far_lo,
        own_a, own_b, own_c, own_d, far_a, far_b, far_c, far_d,
        own_weight, far_weight, own_target, far_target, part,
    ) = refs
    i = pl.program_id(0)
    core = scal[1]

    @pl.when(i == 0)
    def _():
        part[...] = jnp.zeros_like(part)

    sides = (
        (core, own_scores, own_hi, own_lo, own_a, (own_b, own_c, own_d), own_weight, own_target),
        (1 - core, far_scores, far_hi, far_lo, far_a, (far_b, far_c, far_d), far_weight, far_target),
    )
    for which, scores, hi, lo, lev_a, moved, weight, target in sides:
        for j in range(4):
            cols = slice(j * TILE, (j + 1) * TILE)
            tile = j * GROUPS + i * 2 + which
            a1 = scal[2 + tile].astype(f32)
            b1 = scal[34 + tile].astype(f32)
            a0, b0 = 1.0 - a1, 1.0 - b1
            la = lev_a[j, 0, 0].astype(f32)
            lb = moved[min(j, 2)][max(j - 2, 0), 0].astype(f32)
            ta = la + jnp.where(la > 0, 10.0, 0.0)
            tb = lb + jnp.where(lb > 0, 10.0, 0.0)
            weight[0, :HALF, cols] = (10.0 + a0 * la + b0 * lb).astype(bf16)
            weight[0, HALF:, cols] = (10.0 + a1 * la + b1 * lb).astype(bf16)
            target[0, :HALF, cols] = a0 * ta + b0 * tb
            target[0, HALF:, cols] = a1 * ta + b1 * tb
        mixed = STEP * (target[0] - weight[0].astype(f32) * scores[0])
        part[...] += project(mixed, hi[0], lo[0])


def apply_step(shared, part, stacked):
    own_hi, own_lo, far_hi, far_lo, own_weight, far_weight = shared
    for hi, lo, weight in ((own_hi, own_lo, own_weight), (far_hi, far_lo, far_weight)):
        scores = scores_of(stacked[...], hi[0], lo[0])
        mixed = STEP * (weight[0].astype(f32) * scores)
        part[...] += project(mixed, hi[0], lo[0])


def second_kernel(pa, pb, x0, *refs):
    shared, (resid, part, stacked) = refs[:6], refs[6:]

    @pl.when(pl.program_id(0) == 0)
    def _():
        start = pa[...] + pb[...] - RIDGE * x0[...]
        resid[...] = start
        store_split(start, stacked)
        part[...] = jnp.zeros_like(part)

    apply_step(shared, part, stacked)


def third_kernel(pa, pb, resid, x0, *refs):
    shared, (x1, resid1, direc1, part, stacked) = refs[:6], refs[6:]

    @pl.when(pl.program_id(0) == 0)
    def _():
        direc = resid[...]
        image = pa[...] + pb[...] + RIDGE * direc
        rho = jnp.sum(direc * direc, axis=1, keepdims=True)
        alpha = rho / jnp.sum(direc * image, axis=1, keepdims=True)
        x1[...] = x0[...] + alpha * direc
        after = direc - alpha * image
        resid1[...] = after
        rho_next = jnp.sum(after * after, axis=1, keepdims=True)
        ahead = after + (rho_next / rho) * direc
        direc1[...] = ahead
        store_split(ahead, stacked)
        part[...] = jnp.zeros_like(part)

    apply_step(shared, part, stacked)


def last_kernel(pa, pb, resid, direc, x1, out):
    image = pa[...] + pb[...] + RIDGE * direc[...]
    rho = jnp.sum(resid[...] * resid[...], axis=1, keepdims=True)
    alpha = rho / jnp.sum(direc[...] * image, axis=1, keepdims=True)
    out[...] = x1[...] + alpha * direc[...]


def rhs_kernel(scal, vectors, own, got, t1, t2, t3, out, total):
    x = scal[0]
    for k in range(4):
        source = lax.rem(x + 4 - k, 4)
        for slot in range(2):
            chunk = vectors[source, slot]
            if k == 0:
                tile = (own, got)[slot][x]
            else:
                tile = (t1, t2, t3)[k - 1][slot]
            tile = tile.astype(bf16)
            high, low = split(chunk.T)
            both = jnp.concatenate([high, low], axis=1)
            term = dot(both, jnp.concatenate([tile, tile], axis=0))
            if k == 0 and slot == 0:
                total[...] = term
            else:
                total[...] += term
    for j in range(4):
        out[0, j] = total[:, j * TILE : (j + 1) * TILE]
        out[1, j] = total[:, j * TILE : (j + 1) * TILE]


def spec(shape, index=None):
    if index is None:
        zeros = (0,) * len(shape)
        return pl.BlockSpec(shape, lambda *_: zeros)
    return pl.BlockSpec(shape, index)


def params():
    return pltpu.CompilerParams(vmem_limit_bytes=VMEM)


def cost(flops, moved):
    return pl.CostEstimate(flops=flops, bytes_accessed=moved, transcendentals=0)


APPLY_COST = 6 * 2 * TILE * GROUPS * WIDE * RANK


def shaped(*shape, dtype=f32):
    return jax.ShapeDtypeStruct(shape, dtype)


def group(*shape):
    return spec((1,) + shape, lambda i, *_: (i,) + (0,) * len(shape))


def first_scores(x0_t, own, far):
    half_panel = shaped(4, RANK, WIDE, dtype=bf16)
    return pl.pallas_call(
        scores_kernel,
        grid=(4,),
        in_specs=[spec((RANK, TILE))] + [group(4, RANK, TILE)] * 2,
        out_specs=[group(RANK, WIDE)] * 4 + [group(TILE, WIDE)] * 2 + [spec((TILE, RANK))],
        out_shape=[half_panel] * 4 + [shaped(4, TILE, WIDE)] * 2 + [shaped(TILE, RANK)],
        scratch_shapes=[pltpu.VMEM((2 * TILE, RANK), bf16)],
        compiler_params=params(),
        cost_estimate=cost(APPLY_COST // 2, 10 << 20),
        name="first_scores",
    )(x0_t, own, far)


def first_apply(scal, scores, panels, lev, moved):
    whole = (TILE, RANK)

    def side(i, s, far):
        return i * 2 + (1 - s[1] if far else s[1])

    levels_specs = []
    for far in (False, True):
        levels_specs += [
            spec((4, 1, 1, HALF, TILE), lambda i, s, far=far: (0, side(i, s, far), s[0], 0, 0)),
            *(
                spec((n, 1, HALF, TILE), lambda i, s, far=far: (0, side(i, s, far), 0, 0))
                for n in (1, 1, 2)
            ),
        ]
    return pl.pallas_call(
        first_kernel,
        grid_spec=pltpu.PrefetchScalarGridSpec(
            num_scalar_prefetch=1,
            grid=(4,),
            in_specs=[group(TILE, WIDE)] * 2 + [group(RANK, WIDE)] * 4 + levels_specs,
            out_specs=[group(TILE, WIDE)] * 4 + [spec(whole)],
        ),
        out_shape=[shaped(4, TILE, WIDE, dtype=bf16)] * 2
        + [shaped(4, TILE, WIDE)] * 2
        + [shaped(*whole)],
        compiler_params=params(),
        cost_estimate=cost(APPLY_COST // 2, 12 << 20),
        name="first_apply",
    )(scal, *scores, *panels, lev, *moved, lev, *moved)


def next_apply(kernel, vectors, shared, outs, name):
    whole = (TILE, RANK)
    return pl.pallas_call(
        kernel,
        grid=(4,),
        in_specs=[spec(whole)] * len(vectors) + [group(RANK, WIDE)] * 4 + [group(TILE, WIDE)] * 2,
        out_specs=[spec(whole)] * outs,
        out_shape=[shaped(*whole)] * outs,
        scratch_shapes=[pltpu.VMEM((2 * TILE, RANK), bf16)],
        compiler_params=params(),
        cost_estimate=cost(APPLY_COST, 6 << 20),
        name=name,
    )(*vectors, *shared)


def shift(value, axis, size, by):
    return lax.ppermute(value, axis, [(i, (i + by) % size) for i in range(size)])


def flip(value, axis, size, bit):
    return lax.ppermute(value, axis, [(i, i ^ bit) for i in range(size)])


def pick(value, index, axis=0):
    return lax.dynamic_index_in_dim(value, index, axis, keepdims=False)


VMEM = 16777216


def everyone(value, axis, size):
    copies = jnp.broadcast_to(value[None], (size,) + value.shape)
    return lax.all_to_all(copies, axis, split_axis=0, concat_axis=0, tiled=True)


def per_device(factors_in, items, tile_user, levels):
    y, zh, x, core, rep = (lax.axis_index(name) for name in AXES)
    half, parity = rep // 2, rep % 2
    inside = y // 2 == parity
    strip = RANK // 4
    tie = lax.optimization_barrier

    lev = levels[0].reshape(32, 2, HALF, TILE)
    other = pick(lev, 1 - half, 1)
    chunks = (other[:8], other[8:16], other[16:])
    users = factors_in.T.reshape(strip, 2, TILE)
    kept = lax.dynamic_slice_in_dim(users, half * HALF, HALF, 2).reshape(strip, TILE)
    given = lax.dynamic_slice_in_dim(users, (1 - half) * HALF, HALF, 2).reshape(strip, TILE)
    blocks = jnp.zeros((8, TILE), f32).at[0, :32].set(tile_user[0].astype(f32))
    given = jnp.concatenate([given, blocks])
    panel = items.T
    panel, kept, given, chunks = tie((panel, kept, given, chunks))

    lev_b = flip(chunks[0], "rep", 4, 2)
    panel = everyone(panel, ("zh", "rep"), 8).reshape(2, RANK, TILE)
    panel, given, lev_b, *chunks = tie((panel, given, lev_b, *chunks[1:]))
    lev_c = flip(chunks[0], "rep", 4, 2)
    got = flip(given, "rep", 4, 2)
    user_b = got[strip, :32].astype(jnp.int32)
    scal = jnp.concatenate([jnp.stack([half, core]).astype(jnp.int32), tile_user[0], user_b])
    low = jnp.where(half == 0, kept, got[:strip])
    high = jnp.where(half == 0, got[:strip], kept)
    pair = jnp.stack([low, high])

    panel = everyone(panel, "y", 4).reshape(4, 2, RANK, TILE)
    panel = lax.dynamic_slice_in_dim(panel, 2 * parity, 2, 0).reshape(1, 4, RANK, TILE)
    panel, pair, scal, lev_c, last = tie((panel, pair, scal, lev_c, chunks[1]))
    lev_d = flip(last, "rep", 4, 2)
    next_pair = flip(pair, "rep", 4, 1)
    own_panels = everyone(panel, "x", 4).reshape(4, 4, RANK, TILE)
    own_panels, next_pair, lev_d = tie((own_panels, next_pair, lev_d))
    far_panels = flip(own_panels, "core", 2, 1)
    first = jnp.where(parity == 0, pair, next_pair)
    second = jnp.where(parity == 0, next_pair, pair)
    x0_t = jnp.stack([first, second], axis=1).reshape(RANK, TILE)

    *panels, own_scores, far_scores, x0 = first_scores(x0_t, own_panels, far_panels)
    *weights, target, far_target, part = first_apply(
        scal,
        (own_scores, far_scores),
        panels,
        lev.reshape(4, GROUPS, 2, HALF, TILE),
        [v.reshape(-1, GROUPS, HALF, TILE) for v in (lev_b, lev_c, lev_d)],
    )
    shared = (*panels, *weights)
    part_b = flip(part, "rep", 4, 1)

    got = flip(far_target, "core", 2, 1)
    moved = []
    for k in (1, 2, 3):
        to = (x + k) % 4
        moved.append(shift(jnp.stack([pick(target, to), pick(got, to)]), "x", 4, k))

    resid, part = next_apply(second_kernel, (part, part_b, x0), shared, 2, "second_apply")
    part_b = flip(part, "rep", 4, 1)
    x1, resid1, direc1, part = next_apply(
        third_kernel, (part, part_b, resid, x0), shared, 4, "third_apply"
    )
    part_b = flip(part, "rep", 4, 1)
    part_b, moved = tie((part_b, moved))
    solved = pl.pallas_call(
        last_kernel,
        out_shape=shaped(TILE, RANK),
        compiler_params=params(),
        cost_estimate=cost(TILE * RANK * 10, 6 * TILE * RANK * 4),
        name="last_update",
    )(part, part_b, resid1, direc1, x1)

    pair = jnp.stack([solved, flip(solved, "core", 2, 1)])
    vectors = everyone(pair, "x", 4)

    smem = pl.BlockSpec(memory_space=pltpu.SMEM)
    vmem = pl.BlockSpec(memory_space=pltpu.VMEM)
    terms = pl.pallas_call(
        rhs_kernel,
        in_specs=[smem] + [vmem] * 6,
        out_shape=shaped(2, 4, RANK, TILE),
        scratch_shapes=[pltpu.VMEM((RANK, WIDE), f32)],
        compiler_params=params(),
        cost_estimate=cost(4 * 1024 * RANK * WIDE, 4 << 20),
        name="rhs_terms",
    )(jnp.stack([x, core]).astype(jnp.int32), vectors, target, got, *moved)

    terms, solved = tie((terms, solved))
    strips = solved.reshape(TILE, 4, strip)
    sent = flip(pick(strips, rep ^ 2, 1), "rep", 4, 2)
    kept = pick(strips, rep, 1)
    low = jnp.where(half == 0, kept, sent).reshape(2, HALF, strip)
    high = jnp.where(half == 0, sent, kept).reshape(2, HALF, strip)
    factors = jnp.stack([low, high], axis=1).reshape(2 * TILE, strip)

    summed = lax.all_to_all(
        terms.reshape(4, 8, strip, TILE), "y", split_axis=0, concat_axis=0, tiled=True
    ).sum(axis=0)
    summed, factors = tie((summed, factors))
    pieces = lax.all_to_all(
        summed, ("zh", "rep"), split_axis=0, concat_axis=0, tiled=True
    )
    chosen = pick(pieces.reshape(2, 2, 2, strip, TILE), y // 2, 2)
    scale = (2 * 64 * TILE) ** -0.5
    item_rhs = jnp.sum(chosen, axis=(0, 1)).T * (scale * STEP)
    return factors, item_rhs


def solution(mesh):
    fine = Mesh(np.asarray(mesh.devices).reshape(SIZES), AXES)
    rows = P(BLK, "rep")
    return jax.shard_map(
        per_device,
        mesh=fine,
        in_specs=(rows, rows, rows, P(BLK, "rep", None, None)),
        out_specs=(rows, rows),
        check_vma=False,
    )
```

time: 238 us -> 193 us (0.81)
  blocking collectives: 29.8 us -> 0 us
  starting transfers between devices: 25.1 us -> 46.9 us
  waiting for transfers between devices: 125 us -> 109 us
  between operations: 14 us -> 1.08 us
  Pallas kernels: 22.1 us -> 17.9 us
  other arithmetic: 4.91 us -> 1.8 us
    all_to_all x1 -> x6, waiting for transfers between devices: 1.57 us -> 35.9 us  [the longest x4 17 us: everyone(): return lax.all_to_all(copies, axis, split_axis=0, concat_axis=0, tiled=True)]
    all_gather x1 -> x0, blocking collectives: 29.8 us -> none  [per_device(): column = lax.all_gather(packed, ('zh', 'rep'), axis=0, tiled=False)]
    all_to_all x1 -> x6, starting transfers between devices: 7.31 us -> 33.5 us  [the longest x4 23.7 us: everyone(): return lax.all_to_all(copies, axis, split_axis=0, concat_axis=0, tiled=True)]
    all_gather x3 -> x0, waiting for transfers between devices: 25.9 us -> none  [the longest x1 25.9 us: per_device(): panel = lax.all_gather(panel, 'y', axis=0, tiled=False)]
    ppermute x3, waiting for transfers between devices: 23.1 us -> 3.99 us  [shift(): lax.ppermute(value, axis, [(i, (i + by) % size) for i in range(size)])]
    ppermute x3 -> x0, waiting for transfers between devices: 13.2 us -> none  [along_y(): return lax.ppermute(value, ('y', 'rep'), pairs)]
    ppermute x7 -> x12, waiting for transfers between devices: 60.7 us -> 68.8 us  [flip(): return lax.ppermute(value, axis, [(i, i ^ bit) for i in range(size)])]
    ppermute x3 -> x0, starting transfers between devices: 4.78 us -> none  [along_y(): return lax.ppermute(value, ('y', 'rep'), pairs)]
  transfers between devices with their start and end apart: 17 -> 21, of which waited for: 11 -> 16; matrix products, arithmetic and copies ran while one was open for 3% -> 1% of each run, Pallas kernels for 3% -> 4%
where the time goes in v2:
time: 193 us; the launch traced here: 192 us
  waiting for transfers between devices  109 us (56%)
  starting transfers between devices  46.9 us (24%)
  Pallas kernels  17.9 us (9%)
  local copies, waits for them, and re-layouts  15.6 us (8%)
    ppermute x12, waiting for transfers between devices, flip(): return lax.ppermute(value, axis, [(i, i ^ bit) for i in range(size)])  68.8 us
    all_to_all x4, starting transfers between devices, everyone(): return lax.all_to_all(copies, axis, split_axis=0, concat_axis=0, tiled=True)  23.7 us
    all_to_all x4, waiting for transfers between devices, everyone(): return lax.all_to_all(copies, axis, split_axis=0, concat_axis=0, tiled=True)  17 us
    all_to_all x1, waiting for transfers between devices, per_device(): lax.all_to_all(summed, ('zh', 'rep'), split_axis=0, concat_axis=0, tiled=...  10.5 us
    ppermute x12, starting transfers between devices, flip(): return lax.ppermute(value, axis, [(i, i ^ bit) for i in range(size)])  9.13 us
    all_to_all x1, waiting for transfers between devices, per_device(): lax.all_to_all(terms.reshape(4, 8, strip, TILE), 'y', split_axis=0, conca...  8.37 us
    pallas_call x2, Pallas kernels, next_apply(): pl.pallas_call(kernel, grid=(4,), in_specs=[spec(whole)] * len(vectors) +...  7.91 us
    unnamed x44, local copies, waits for them, and re-layouts  6.4 us
  transfers between devices with their start and end apart: 21, of which 16 were waited for; matrix products, arithmetic and copies ran while one was open for 1% of the time, Pallas kernels for 4%

profile of v2, /device:TPU:6, one launch (start us, length us, event | category | flops | bytes accessed | tf_op | source)
XLA Modules:
  0.0 191.9 jit_solution(12487952540095733617)
XLA Ops:
  1.8 1.9 dynamic-slice_bitcast_fusion
  4.9 8.5 %all-to-all-start = ((f32[8,64,128]{2,1,0:T(8,128)}), f32[8,64,128]{2,1,0:T(8,128)S(1)}, u32[]{:S(2)}, u32[]{:S(2)}) async-start(f32[8,64,128]{2,1,0:T(8,128)} %broadcast_in_dim.10), calls=%async_computation | async-start | bytes 524288 | tf_op jit(solution)/shard_map/all_to_all | solution.py:289
  13.3 2.9 %collective-permute-start = (s32[8,64,128]{2,1,0:T(8,128)S(1)}, s32[8,64,128]{2,1,0:T(8,128)S(1)}, u32[]{:S(2)}, u32[]{:S(2)}) collective-permute-start(s32[8,64,128]{2,1,0:T(8,128)S(1)} %get-tuple-element.61), channel_id=1, source_target_pairs={{0,2},{1,3},{2,0},{3,1},{4,6},{5,7},{6,4},{7,5},{8,10},{9,11},{10,... | collective-permute-start | bytes 786440 | tf_op jit(solution)/shard_map/ppermute | solution.py:277
  16.3 17.2 %collective-permute-done = s32[8,64,128]{2,1,0:T(8,128)S(1)} collective-permute-done((s32[8,64,128]{2,1,0:T(8,128)S(1)}, s32[8,64,128]{2,1,0:T(8,128)S(1)}, u32[]{:S(2)}, u32[]{:S(2)}) %collective-permute-start) | collective-permute-done | bytes 262176 | tf_op jit(solution)/shard_map/ppermute | solution.py:277
  34.5 4.5 %all-to-all-start.1 = ((f32[4,2,256,128]{3,2,1,0:T(8,128)}), f32[4,2,256,128]{3,2,1,0:T(8,128)S(1)}, u32[]{:S(2)}, u32[]{:S(2)}) async-start(f32[4,2,256,128]{3,2,1,0:T(8,128)} %broadcast_in_dim.11), calls=%async_computation.1 | async-start | bytes 2097152 | tf_op jit(solution)/shard_map/all_to_all | solution.py:289
  39.0 2.9 %collective-permute-start.2 = (s32[8,64,128]{2,1,0:T(8,128)S(1)}, s32[8,64,128]{2,1,0:T(8,128)S(1)}, u32[]{:S(2)}, u32[]{:S(2)}) collective-permute-start(s32[8,64,128]{2,1,0:T(8,128)S(1)} %get-tuple-element.67), channel_id=1, source_target_pairs={{0,2},{1,3},{2,0},{3,1},{4,6},{5,7},{6,4},{7,5},{8,10},{9,11},{10,... | collective-permute-start | bytes 786440 | tf_op jit(solution)/shard_map/ppermute | solution.py:277
  41.9 7.5 %collective-permute-done.1 = f32[72,128]{1,0:T(8,128)S(1)} collective-permute-done((f32[72,128]{1,0:T(8,128)S(1)}, f32[72,128]{1,0:T(8,128)S(1)}, u32[]{:S(2)}, u32[]{:S(2)}) %collective-permute-start.1) | collective-permute-done | bytes 36896 | tf_op jit(solution)/shard_map/ppermute | solution.py:277
  49.5 3.5 %all-to-all-done.1 = f32[4,2,256,128]{3,2,1,0:T(8,128)S(1)} async-done(((f32[4,2,256,128]{3,2,1,0:T(8,128)}), f32[4,2,256,128]{3,2,1,0:T(8,128)S(1)}, u32[]{:S(2)}, u32[]{:S(2)}) %all-to-all-start.1) | async-done | bytes 1048608 | tf_op jit(solution)/shard_map/all_to_all | solution.py:289
  53.3 1.6 broadcast_in_dim.13
  54.9 4.8 %all-to-all-start.2 = ((f32[4,1,4,256,128]{4,3,2,1,0:T(8,128)}), f32[4,1,4,256,128]{4,3,2,1,0:T(8,128)S(1)}, u32[]{:S(2)}, u32[]{:S(2)}) async-start(f32[4,1,4,256,128]{4,3,2,1,0:T(8,128)} %broadcast_in_dim.13), calls=%async_computation.2 | async-start | bytes 4194304 | tf_op jit(solution)/shard_map/all_to_all | solution.py:289
  59.6 2.7 %collective-permute-start.3 = (f32[2,64,128]{2,1,0:T(8,128)S(1)}, f32[2,64,128]{2,1,0:T(8,128)S(1)}, u32[]{:S(2)}, u32[]{:S(2)}) collective-permute-start(f32[2,64,128]{2,1,0:T(8,128)S(1)} %pad_maximum_fusion.6), channel_id=1, source_target_pairs={{0,1},{1,0},{2,3},{3,2},{4,5},{5,4},{6,7},{7,6},{8,9},{9,8},{10,11... | collective-permute-start | bytes 196616 | tf_op jit(solution)/shard_map/ppermute | solution.py:277
  62.4 8.4 %collective-permute-done.3 = f32[2,64,128]{2,1,0:T(8,128)S(1)} collective-permute-done((f32[2,64,128]{2,1,0:T(8,128)S(1)}, f32[2,64,128]{2,1,0:T(8,128)S(1)}, u32[]{:S(2)}, u32[]{:S(2)}) %collective-permute-start.3) | collective-permute-done | bytes 65568 | tf_op jit(solution)/shard_map/ppermute | solution.py:277
  70.8 12.7 %collective-permute-done.4 = s32[16,64,128]{2,1,0:T(8,128)S(1)} collective-permute-done((s32[16,64,128]{2,1,0:T(8,128)}, s32[16,64,128]{2,1,0:T(8,128)S(1)}, u32[]{:S(2)}, u32[]{:S(2)}) %collective-permute-start.4) | collective-permute-done | bytes 524320 | tf_op jit(solution)/shard_map/ppermute | solution.py:277
  83.6 4.2 %collective-permute-done.5.far = f32[4,4,256,128]{3,2,1,0:T(8,128)} collective-permute-done((f32[4,4,256,128]{3,2,1,0:T(8,128)S(1)}, f32[4,4,256,128]{3,2,1,0:T(8,128)}, u32[]{:S(2)}, u32[]{:S(2)}) %collective-permute-start.5) | collective-permute-done | bytes 2097184 | tf_op jit(solution)/shard_map/ppermute | solution.py:277
  87.8 3.8 %first_scores.1 = (bf16[4,256,512]{2,1,0:T(8,128)(2,1)S(1)}, bf16[4,256,512]{2,1,0:T(8,128)(2,1)S(1)}, bf16[4,256,512]{2,1,0:T(8,128)(2,1)S(1)}, bf16[4,256,512]...) custom-call(f32[256,128]{1,0:T(8,128)S(1)} %bitcast.70, ...), custom_call_target="tpu_custom_call" | custom-call | flops 805306368 | bytes 10485760 | tf_op jit(solution)/shard_map/first_scores/pallas_call | solution.py:212
  91.6 3.8 %first_apply.1 = (bf16[4,128,512]{2,1,0:T(8,128)(2,1)S(1)}, bf16[4,128,512]{2,1,0:T(8,128)(2,1)S(1)}, f32[4,128,512]{2,1,0:T(8,128)S(1)}, f32[4,128,512]{2,1,0:T(8,128)S(1)}, f32[128,256]{1,0:T(8,128)S(1)}) custom-call(s32[66]{0:T(128)S(1)} %pad_add_fusion.1.scal, f32[4,128,512]{2,1,0:T(8,128)S(1)} %get-tuple-element.75.refs_0_, ...), custom_call_target="tpu_custom_call" | custom-call | flops 805306368 | bytes 12582912 | tf_op jit(solution)/shard_map/first_apply/pallas_call | solution.py:240
  97.3 2.4 %collective-permute-done.9.got = f32[4,128,512]{2,1,0:T(8,128)S(1)} collective-permute-done((f32[4,128,512]{2,1,0:T(8,128)S(1)}, f32[4,128,512]{2,1,0:T(8,128)S(1)}, u32[]{:S(2)}, u32[]{:S(2)}) %collective-permute-start.9) | collective-permute-done | bytes 1048608 | tf_op jit(solution)/shard_map/ppermute | solution.py:277
  100.8 1.8 collective-permute-start.11
  102.6 1.6 collective-permute-start.10
  104.3 3.9 %second_apply.1 = (f32[128,256]{1,0:T(8,128)S(1)}, f32[128,256]{1,0:T(8,128)S(1)}) custom-call(f32[128,256]{1,0:T(8,128)S(1)} %get-tuple-element.84.pa, f32[128,256]{1,0:T(8,128)S(1)} %collective-permute-done.6.pb, f32[128,256]{1,0:T(8,128)S(1)} %get-tuple-element.85.x0, bf16[4,256,512]{2,1,0:T(8,128)(2,1)S(1)} %copy-done.2, ...), custom_call_target="tpu_custom_call" | custom-call | flops 1610612736 | bytes 6291456 | tf_op jit(solution)/shard_map/second_apply/pallas_call | solution.py:259
  108.3 5.0 %collective-permute-done.7.pb = f32[128,256]{1,0:T(8,128)S(1)} collective-permute-done((f32[128,256]{1,0:T(8,128)S(1)}, f32[128,256]{1,0:T(8,128)S(1)}, u32[]{:S(2)}, u32[]{:S(2)}) %collective-permute-start.7) | collective-permute-done | bytes 131104 | tf_op jit(solution)/shard_map/ppermute | solution.py:277
  113.2 4.0 %third_apply.1 = (f32[128,256]{1,0:T(8,128)S(1)}, f32[128,256]{1,0:T(8,128)S(1)}, f32[128,256]{1,0:T(8,128)S(1)}, f32[128,256]{1,0:T(8,128)S(1)}) custom-call(f32[128,256]{1,0:T(8,128)S(1)} %get-tuple-element.88.pa, f32[128,256]{1,0:T(8,128)S(1)} %collective-permute-done.7.pb, f32[128,256]{1,0:T(8,128)S(1)} %get-tuple-element.89.resid, ...), custom_call_target="tpu_custom_call" | custom-call | flops 1610612736 | bytes 6291456 | tf_op jit(solution)/shard_map/third_apply/pallas_call | solution.py:259
  117.4 4.9 %collective-permute-done.8.pb = f32[128,256]{1,0:T(8,128)S(1)} collective-permute-done((f32[128,256]{1,0:T(8,128)S(1)}, f32[128,256]{1,0:T(8,128)S(1)}, u32[]{:S(2)}, u32[]{:S(2)}) %collective-permute-start.8) | collective-permute-done | bytes 131104 | tf_op jit(solution)/shard_map/ppermute | solution.py:277
  122.3 4.0 %collective-permute-done.12.t3 = f32[2,128,512]{2,1,0:T(8,128)S(1)} collective-permute-done((f32[2,128,512]{2,1,0:T(8,128)S(1)}, f32[2,128,512]{2,1,0:T(8,128)S(1)}, u32[]{:S(2)}, u32[]{:S(2)}) %collective-permute-start.12) | collective-permute-done | bytes 524320 | tf_op jit(solution)/shard_map/ppermute | solution.py:273
  130.6 6.0 %all-to-all-start.3 = ((f32[4,2,128,256]{3,2,1,0:T(8,128)}), f32[4,2,128,256]{3,2,1,0:T(8,128)S(1)}, u32[]{:S(2)}, u32[]{:S(2)}) async-start(f32[4,2,128,256]{3,2,1,0:T(8,128)} %broadcast_in_dim.14), calls=%async_computation.3 | async-start | bytes 2097152 | tf_op jit(solution)/shard_map/all_to_all | solution.py:289
  136.7 13.5 %all-to-all-done.3.vectors = f32[4,2,128,256]{3,2,1,0:T(8,128)S(1)} async-done(((f32[4,2,128,256]{3,2,1,0:T(8,128)}), f32[4,2,128,256]{3,2,1,0:T(8,128)S(1)}, u32[]{:S(2)}, u32[]{:S(2)}) %all-to-all-start.3) | async-done | bytes 1048608 | tf_op jit(solution)/shard_map/all_to_all | solution.py:289
  153.4 2.3 %rhs_terms.1 = f32[2,4,256,128]{3,2,1,0:T(8,128)} custom-call(s32[2]{0:T(128)S(1)} %pad_add_fusion.scal, f32[4,2,128,256]{3,2,1,0:T(8,128)S(1)} %all-to-all-done.3.vectors, f32[4,128,512]{2,1,0:T(8,128)S(1)} %get-tuple-element.91.own, f32[4,128,512]{2,1,0:T(8,128)S(1)} %collective-permute-done.9.got, f32[2,128,512]{2,1,0:T(8,128)S(1)} %copy-done.14, ...), custom_call_target="tpu_custom_call" | custom-call | flops 536870912 | bytes 4194304 | tf_op jit(solution)/shard_map/rhs_terms/pallas_call | solution.py:370
  155.7 4.4 %all-to-all-start.4 = ((f32[4,8,64,128]{3,2,1,0:T(8,128)}), f32[4,8,64,128]{3,2,1,0:T(8,128)S(1)}, u32[]{:S(2)}, u32[]{:S(2)}) async-start(f32[4,8,64,128]{3,2,1,0:T(8,128)} %bitcast.26), calls=%async_computation.4 | async-start | bytes 2097152 | tf_op jit(solution)/shard_map/all_to_all | solution.py:388
  160.3 4.8 %collective-permute-done.14 = f32[128,64]{0,1:T(8,128)S(1)} collective-permute-done((f32[128,64]{0,1:T(8,128)S(1)}, f32[128,64]{0,1:T(8,128)S(1)}, u32[]{:S(2)}, u32[]{:S(2)}) %collective-permute-start.14) | collective-permute-done | bytes 32800 | tf_op jit(solution)/shard_map/ppermute | solution.py:277
  166.3 8.4 %all-to-all-done.4 = f32[4,8,64,128]{3,2,1,0:T(8,128)S(1)} async-done(((f32[4,8,64,128]{3,2,1,0:T(8,128)}), f32[4,8,64,128]{3,2,1,0:T(8,128)S(1)}, u32[]{:S(2)}, u32[]{:S(2)}) %all-to-all-start.4) | async-done | bytes 1048608 | tf_op jit(solution)/shard_map/all_to_all | solution.py:388
  175.5 5.3 %all-to-all-start.5 = ((f32[8,64,128]{2,1,0:T(8,128)}), f32[8,64,128]{2,1,0:T(8,128)S(1)}, u32[]{:S(2)}, u32[]{:S(2)}) async-start(f32[8,64,128]{2,1,0:T(8,128)} %reduce_sum.18), calls=%async_computation.5 | async-start | bytes 524288 | tf_op jit(solution)/shard_map/all_to_all | solution.py:392
  180.8 10.5 %all-to-all-done.5 = f32[8,64,128]{2,1,0:T(8,128)S(1)} async-done(((f32[8,64,128]{2,1,0:T(8,128)}), f32[8,64,128]{2,1,0:T(8,128)S(1)}, u32[]{:S(2)}, u32[]{:S(2)}) %all-to-all-start.5) | async-done | bytes 262176 | tf_op jit(solution)/shard_map/all_to_all | solution.py:392
  (98 shorter events, 17.2 us)
Async XLA Ops:
  4.9 28.6 %all-to-all-start = ((f32[8,64,128]{2,1,0:T(8,128)}), f32[8,64,128]{2,1,0:T(8,128)S(1)}, u32[]{:S(2)}, u32[]{:S(2)}) async-start(f32[8,64,128]{2,1,0:T(8,128)} %broadcast_in_dim.10), calls=%async_computation | async-start | bytes 524288 | tf_op jit(solution)/shard_map/all_to_all | solution.py:289
  13.3 20.1 %collective-permute-start = (s32[8,64,128]{2,1,0:T(8,128)S(1)}, s32[8,64,128]{2,1,0:T(8,128)S(1)}, u32[]{:S(2)}, u32[]{:S(2)}) collective-permute-start(s32[8,64,128]{2,1,0:T(8,128)S(1)} %get-tuple-element.61), channel_id=1, source_target_pairs={{0,2},{1,3},{2,0},{3,1},{4,6},{5,7},{6,4},{7,5},{8,10},{9,11},{10,... | collective-permute-start | bytes 786440 | tf_op jit(solution)/shard_map/ppermute | solution.py:277
  34.5 18.4 %all-to-all-start.1 = ((f32[4,2,256,128]{3,2,1,0:T(8,128)}), f32[4,2,256,128]{3,2,1,0:T(8,128)S(1)}, u32[]{:S(2)}, u32[]{:S(2)}) async-start(f32[4,2,256,128]{3,2,1,0:T(8,128)} %broadcast_in_dim.11), calls=%async_computation.1 | async-start | bytes 2097152 | tf_op jit(solution)/shard_map/all_to_all | solution.py:289
  39.0 10.4 %collective-permute-start.1 = (f32[72,128]{1,0:T(8,128)S(1)}, f32[72,128]{1,0:T(8,128)S(1)}, u32[]{:S(2)}, u32[]{:S(2)}) collective-permute-start(f32[72,128]{1,0:T(8,128)S(1)} %select_maximum_fusion), channel_id=1, source_target_pairs={{0,2},{1,3},{2,0},{3,1},{4,6},{5,7},{6,4},{7,5},{8,10},{9,11},{10,... | collective-permute-start | bytes 110600 | tf_op jit(solution)/shard_map/ppermute | solution.py:277
  39.0 14.3 %collective-permute-start.2 = (s32[8,64,128]{2,1,0:T(8,128)S(1)}, s32[8,64,128]{2,1,0:T(8,128)S(1)}, u32[]{:S(2)}, u32[]{:S(2)}) collective-permute-start(s32[8,64,128]{2,1,0:T(8,128)S(1)} %get-tuple-element.67), channel_id=1, source_target_pairs={{0,2},{1,3},{2,0},{3,1},{4,6},{5,7},{6,4},{7,5},{8,10},{9,11},{10,... | collective-permute-start | bytes 786440 | tf_op jit(solution)/shard_map/ppermute | solution.py:277
  54.9 28.6 %all-to-all-start.2 = ((f32[4,1,4,256,128]{4,3,2,1,0:T(8,128)}), f32[4,1,4,256,128]{4,3,2,1,0:T(8,128)S(1)}, u32[]{:S(2)}, u32[]{:S(2)}) async-start(f32[4,1,4,256,128]{4,3,2,1,0:T(8,128)} %broadcast_in_dim.13), calls=%async_computation.2 | async-start | bytes 4194304 | tf_op jit(solution)/shard_map/all_to_all | solution.py:289
  59.6 23.8 %collective-permute-start.4 = (s32[16,64,128]{2,1,0:T(8,128)}, s32[16,64,128]{2,1,0:T(8,128)S(1)}, u32[]{:S(2)}, u32[]{:S(2)}) collective-permute-start(s32[16,64,128]{2,1,0:T(8,128)} %dynamic-slice_bitcast_fusion), channel_id=1, source_target_pairs={{0,2},{1,3},{2,0},{3,1},{4,6},{5,7},{6,4},{7,5},{8,10},{9,11},{10,... | collective-permute-start | bytes 1572872 | tf_op jit(solution)/shard_map/ppermute | solution.py:277
  59.6 11.2 %collective-permute-start.3 = (f32[2,64,128]{2,1,0:T(8,128)S(1)}, f32[2,64,128]{2,1,0:T(8,128)S(1)}, u32[]{:S(2)}, u32[]{:S(2)}) collective-permute-start(f32[2,64,128]{2,1,0:T(8,128)S(1)} %pad_maximum_fusion.6), channel_id=1, source_target_pairs={{0,1},{1,0},{2,3},{3,2},{4,5},{5,4},{6,7},{7,6},{8,9},{9,8},{10,11... | collective-permute-start | bytes 196616 | tf_op jit(solution)/shard_map/ppermute | solution.py:277
  83.5 4.3 %collective-permute-start.5 = (f32[4,4,256,128]{3,2,1,0:T(8,128)S(1)}, f32[4,4,256,128]{3,2,1,0:T(8,128)}, u32[]{:S(2)}, u32[]{:S(2)}) collective-permute-start(f32[4,4,256,128]{3,2,1,0:T(8,128)S(1)} %bitcast.61), channel_id=1, source_target_pairs={{0,4},{4,0},{1,5},{5,1},{2,6},{6,2},{3,7},{7,3},{8,12},{12,8},{9,1... | collective-permute-start | bytes 6291464 | tf_op jit(solution)/shard_map/ppermute | solution.py:277
  87.8 3.8 %copy-start = (s32[1,32,128,128]{3,2,1,0:T(8,128)S(1)}, s32[1,32,128,128]{3,2,1,0:T(8,128)}, u32[]{:S(2)}) copy-start(s32[1,32,128,128]{3,2,1,0:T(8,128)} %param.9) | copy-start | bytes 6291460
  91.5 3.9 %copy-start.1 = (bf16[4,256,512]{2,1,0:T(8,128)(2,1)}, bf16[4,256,512]{2,1,0:T(8,128)(2,1)S(1)}, u32[]{:S(2)}) copy-start(bf16[4,256,512]{2,1,0:T(8,128)(2,1)S(1)} %get-tuple-element.77.refs_2_.refs_0_) | copy-start | bytes 3145732
  91.6 3.9 %copy-start.3 = (bf16[4,256,512]{2,1,0:T(8,128)(2,1)}, bf16[4,256,512]{2,1,0:T(8,128)(2,1)S(1)}, u32[]{:S(2)}) copy-start(bf16[4,256,512]{2,1,0:T(8,128)(2,1)S(1)} %get-tuple-element.78.refs_3_.refs_1_) | copy-start | bytes 3145732
  91.6 3.9 %copy-start.5 = (bf16[4,256,512]{2,1,0:T(8,128)(2,1)}, bf16[4,256,512]{2,1,0:T(8,128)(2,1)S(1)}, u32[]{:S(2)}) copy-start(bf16[4,256,512]{2,1,0:T(8,128)(2,1)S(1)} %get-tuple-element.79.refs_4_.refs_2_) | copy-start | bytes 3145732
  91.6 3.9 %copy-start.7 = (bf16[4,256,512]{2,1,0:T(8,128)(2,1)}, bf16[4,256,512]{2,1,0:T(8,128)(2,1)S(1)}, u32[]{:S(2)}) copy-start(bf16[4,256,512]{2,1,0:T(8,128)(2,1)S(1)} %get-tuple-element.80.refs_5_.refs_3_) | copy-start | bytes 3145732
  97.0 2.7 %collective-permute-start.9 = (f32[4,128,512]{2,1,0:T(8,128)S(1)}, f32[4,128,512]{2,1,0:T(8,128)S(1)}, u32[]{:S(2)}, u32[]{:S(2)}) collective-permute-start(f32[4,128,512]{2,1,0:T(8,128)S(1)} %get-tuple-element.92), channel_id=1, source_target_pairs={{0,4},{4,0},{1,5},{5,1},{2,6},{6,2},{3,7},{7,3},{8,12},{12,8},{9,1... | collective-permute-start | bytes 3145736 | tf_op jit(solution)/shard_map/ppermute | solution.py:277
  97.2 7.0 %collective-permute-start.6 = (f32[128,256]{1,0:T(8,128)S(1)}, f32[128,256]{1,0:T(8,128)S(1)}, u32[]{:S(2)}, u32[]{:S(2)}) collective-permute-start(f32[128,256]{1,0:T(8,128)S(1)} %get-tuple-element.84.pa), channel_id=1, source_target_pairs={{0,1},{1,0},{2,3},{3,2},{4,5},{5,4},{6,7},{7,6},{8,9},{9,8},{10,11... | collective-permute-start | bytes 393224 | tf_op jit(solution)/shard_map/ppermute | solution.py:277
  97.2 7.0 %copy-start.18 = (bf16[4,128,512]{2,1,0:T(8,128)(2,1)S(1)}, bf16[4,128,512]{2,1,0:T(8,128)(2,1)}, u32[]{:S(2)}) copy-start(bf16[4,128,512]{2,1,0:T(8,128)(2,1)} %copy-done.17) | copy-start | bytes 1572868
  97.2 7.0 %copy-start.2 = (bf16[4,256,512]{2,1,0:T(8,128)(2,1)S(1)}, bf16[4,256,512]{2,1,0:T(8,128)(2,1)}, u32[]{:S(2)}) copy-start(bf16[4,256,512]{2,1,0:T(8,128)(2,1)} %copy-done.1) | copy-start | bytes 3145732
  97.3 7.0 %copy-start.4 = (bf16[4,256,512]{2,1,0:T(8,128)(2,1)S(1)}, bf16[4,256,512]{2,1,0:T(8,128)(2,1)}, u32[]{:S(2)}) copy-start(bf16[4,256,512]{2,1,0:T(8,128)(2,1)} %copy-done.3) | copy-start | bytes 3145732
  97.3 7.0 %copy-start.6 = (bf16[4,256,512]{2,1,0:T(8,128)(2,1)S(1)}, bf16[4,256,512]{2,1,0:T(8,128)(2,1)}, u32[]{:S(2)}) copy-start(bf16[4,256,512]{2,1,0:T(8,128)(2,1)} %copy-done.5) | copy-start | bytes 3145732
  97.3 7.0 %copy-start.8 = (bf16[4,256,512]{2,1,0:T(8,128)(2,1)S(1)}, bf16[4,256,512]{2,1,0:T(8,128)(2,1)}, u32[]{:S(2)}) copy-start(bf16[4,256,512]{2,1,0:T(8,128)(2,1)} %copy-done.7) | copy-start | bytes 3145732
  97.3 7.0 %copy-start.16 = (bf16[4,128,512]{2,1,0:T(8,128)(2,1)S(1)}, bf16[4,128,512]{2,1,0:T(8,128)(2,1)}, u32[]{:S(2)}) copy-start(bf16[4,128,512]{2,1,0:T(8,128)(2,1)} %copy-done.15) | copy-start | bytes 1572868
  99.8 26.5 %collective-permute-start.12 = (f32[2,128,512]{2,1,0:T(8,128)S(1)}, f32[2,128,512]{2,1,0:T(8,128)S(1)}, u32[]{:S(2)}, u32[]{:S(2)}) collective-permute-start(f32[2,128,512]{2,1,0:T(8,128)S(1)} %pad_maximum_fusion.2), channel_id=1, source_target_pairs={{0,24},{8,0},{16,8},{24,16},{1,25},{9,1},{17,9},{25,17},{2,26},{10... | collective-permute-start | bytes 1572872 | tf_op jit(solution)/shard_map/ppermute | solution.py:273
  100.8 25.5 %collective-permute-start.11 = (f32[2,128,512]{2,1,0:T(8,128)S(1)}, f32[2,128,512]{2,1,0:T(8,128)S(1)}, u32[]{:S(2)}, u32[]{:S(2)}) collective-permute-start(f32[2,128,512]{2,1,0:T(8,128)S(1)} %pad_maximum_fusion.1), channel_id=1, source_target_pairs={{0,16},{8,24},{16,0},{24,8},{1,17},{9,25},{17,1},{25,9},{2,18},{10... | collective-permute-start | bytes 1572872 | tf_op jit(solution)/shard_map/ppermute | solution.py:273
  102.6 24.5 %collective-permute-start.10 = (f32[2,128,512]{2,1,0:T(8,128)S(1)}, f32[2,128,512]{2,1,0:T(8,128)S(1)}, u32[]{:S(2)}, u32[]{:S(2)}) collective-permute-start(f32[2,128,512]{2,1,0:T(8,128)S(1)} %pad_maximum_fusion), channel_id=1, source_target_pairs={{0,8},{8,16},{16,24},{24,0},{1,9},{9,17},{17,25},{25,1},{2,10},{10... | collective-permute-start | bytes 1572872 | tf_op jit(solution)/shard_map/ppermute | solution.py:273
  108.2 5.1 %collective-permute-start.7 = (f32[128,256]{1,0:T(8,128)S(1)}, f32[128,256]{1,0:T(8,128)S(1)}, u32[]{:S(2)}, u32[]{:S(2)}) collective-permute-start(f32[128,256]{1,0:T(8,128)S(1)} %get-tuple-element.88.pa), channel_id=1, source_target_pairs={{0,1},{1,0},{2,3},{3,2},{4,5},{5,4},{6,7},{7,6},{8,9},{9,8},{10,11... | collective-permute-start | bytes 393224 | tf_op jit(solution)/shard_map/ppermute | solution.py:277
  117.3 5.1 %collective-permute-start.8 = (f32[128,256]{1,0:T(8,128)S(1)}, f32[128,256]{1,0:T(8,128)S(1)}, u32[]{:S(2)}, u32[]{:S(2)}) collective-permute-start(f32[128,256]{1,0:T(8,128)S(1)} %get-tuple-element.90.pa), channel_id=1, source_target_pairs={{0,1},{1,0},{2,3},{3,2},{4,5},{5,4},{6,7},{7,6},{8,9},{9,8},{10,11... | collective-permute-start | bytes 393224 | tf_op jit(solution)/shard_map/ppermute | solution.py:277
  128.1 1.4 collective-permute-start.13
  130.6 19.6 %all-to-all-start.3 = ((f32[4,2,128,256]{3,2,1,0:T(8,128)}), f32[4,2,128,256]{3,2,1,0:T(8,128)S(1)}, u32[]{:S(2)}, u32[]{:S(2)}) async-start(f32[4,2,128,256]{3,2,1,0:T(8,128)} %broadcast_in_dim.14), calls=%async_computation.3 | async-start | bytes 2097152 | tf_op jit(solution)/shard_map/all_to_all | solution.py:289
  155.7 19.0 %all-to-all-start.4 = ((f32[4,8,64,128]{3,2,1,0:T(8,128)}), f32[4,8,64,128]{3,2,1,0:T(8,128)S(1)}, u32[]{:S(2)}, u32[]{:S(2)}) async-start(f32[4,8,64,128]{3,2,1,0:T(8,128)} %bitcast.26), calls=%async_computation.4 | async-start | bytes 2097152 | tf_op jit(solution)/shard_map/all_to_all | solution.py:388
  160.2 4.9 %collective-permute-start.14 = (f32[128,64]{0,1:T(8,128)S(1)}, f32[128,64]{0,1:T(8,128)S(1)}, u32[]{:S(2)}, u32[]{:S(2)}) collective-permute-start(f32[128,64]{0,1:T(8,128)S(1)} %dynamic-slice_bitcast_fusion.3), channel_id=1, source_target_pairs={{0,2},{1,3},{2,0},{3,1},{4,6},{5,7},{6,4},{7,5},{8,10},{9,11},{10,... | collective-permute-start | bytes 98312 | tf_op jit(solution)/shard_map/ppermute | solution.py:277
  175.5 15.8 %all-to-all-start.5 = ((f32[8,64,128]{2,1,0:T(8,128)}), f32[8,64,128]{2,1,0:T(8,128)S(1)}, u32[]{:S(2)}, u32[]{:S(2)}) async-start(f32[8,64,128]{2,1,0:T(8,128)} %reduce_sum.18), calls=%async_computation.5 | async-start | bytes 524288 | tf_op jit(solution)/shard_map/all_to_all | solution.py:392
  (11 other events, 19.5 us)

commit v3 on v2

--- a/solution.py
+++ b/solution.py
@@ -74,31 +74,32 @@
 
 
 def first_kernel(scal, *refs):
-    (
-        own_scores, far_scores, own_hi, own_lo, far_hi, far_lo,
-        own_a, own_b, own_c, own_d, far_a, far_b, far_c, far_d,
-        own_weight, far_weight, own_target, far_target, part,
-    ) = refs
+    own_scores, far_scores, own_hi, own_lo, far_hi, far_lo, *refs = refs
+    *refs, own_weight, far_weight, own_target, far_target, part = refs
+    count = len(refs) // 2
+    own_a, own_moved = refs[0], refs[1:count]
+    far_a, far_moved = refs[count], refs[count + 1 :]
     i = pl.program_id(0)
-    core = scal[1]
+    x, core = scal[2], scal[1]
+    at = (lax.rem(x + 4 - i, 4) if REL else i) * 2
 
     @pl.when(i == 0)
     def _():
         part[...] = jnp.zeros_like(part)
 
     sides = (
-        (core, own_scores, own_hi, own_lo, own_a, (own_b, own_c, own_d), own_weight, own_target),
-        (1 - core, far_scores, far_hi, far_lo, far_a, (far_b, far_c, far_d), far_weight, far_target),
+        (core, own_scores, own_hi, own_lo, own_a, own_moved, own_weight, own_target),
+        (1 - core, far_scores, far_hi, far_lo, far_a, far_moved, far_weight, far_target),
     )
     for which, scores, hi, lo, lev_a, moved, weight, target in sides:
         for j in range(4):
             cols = slice(j * TILE, (j + 1) * TILE)
-            tile = j * GROUPS + i * 2 + which
-            a1 = scal[2 + tile].astype(f32)
-            b1 = scal[34 + tile].astype(f32)
+            tile = j * GROUPS + at + which
+            a1 = scal[3 + tile].astype(f32)
+            b1 = scal[35 + tile].astype(f32)
             a0, b0 = 1.0 - a1, 1.0 - b1
             la = lev_a[j, 0, 0].astype(f32)
-            lb = moved[min(j, 2)][max(j - 2, 0), 0].astype(f32)
+            lb = jnp.concatenate([rows[j, 0] for rows in moved], axis=0).astype(f32)
             ta = la + jnp.where(la > 0, 10.0, 0.0)
             tb = lb + jnp.where(lb > 0, 10.0, 0.0)
             weight[0, :HALF, cols] = (10.0 + a0 * la + b0 * lb).astype(bf16)
@@ -151,21 +152,24 @@
     apply_step(shared, part, stacked)
 
 
-def last_kernel(pa, pb, resid, direc, x1, out):
+def last_kernel(pa, pb, resid, direc, x1, out, copies):
     image = pa[...] + pb[...] + RIDGE * direc[...]
     rho = jnp.sum(resid[...] * resid[...], axis=1, keepdims=True)
     alpha = rho / jnp.sum(direc[...] * image, axis=1, keepdims=True)
-    out[...] = x1[...] + alpha * direc[...]
-
-
-def rhs_kernel(scal, vectors, own, got, t1, t2, t3, out, total):
+    solved = x1[...] + alpha * direc[...]
+    out[...] = solved
+    for k in range(4):
+        copies[k] = solved
+
+
+def rhs_kernel(scal, own_vectors, far_vectors, own, got, t1, t2, t3, out, total):
     x = scal[0]
     for k in range(4):
-        source = lax.rem(x + 4 - k, 4)
+        source = lax.rem(x + k, 4) if FG == "a2a" else k
         for slot in range(2):
-            chunk = vectors[source, slot]
+            chunk = (own_vectors, far_vectors)[slot][source]
             if k == 0:
-                tile = (own, got)[slot][x]
+                tile = (own, got)[slot][0 if REL else x]
             else:
                 tile = (t1, t2, t3)[k - 1][slot]
             tile = tile.astype(bf16)
@@ -226,15 +230,15 @@
     whole = (TILE, RANK)
 
     def side(i, s, far):
-        return i * 2 + (1 - s[1] if far else s[1])
+        return (lax.rem(s[2] + 4 - i, 4) if REL else i) * 2 + (1 - s[1] if far else s[1])
 
     levels_specs = []
     for far in (False, True):
         levels_specs += [
             spec((4, 1, 1, HALF, TILE), lambda i, s, far=far: (0, side(i, s, far), s[0], 0, 0)),
             *(
-                spec((n, 1, HALF, TILE), lambda i, s, far=far: (0, side(i, s, far), 0, 0))
-                for n in (1, 1, 2)
+                spec((4, 1, n, TILE), lambda i, s, far=far: (0, side(i, s, far), 0, 0))
+                for n in CHUNKS
             ),
         ]
     return pl.pallas_call(
@@ -282,11 +286,24 @@
 
 
 VMEM = 16777216
+FG = 'a2a'
+XS = 'perm'
+REL = 1
+YS = 'a2a'
+X0 = 'z'
+CHUNKS = (8,16,32,8)
 
 
 def everyone(value, axis, size):
     copies = jnp.broadcast_to(value[None], (size,) + value.shape)
     return lax.all_to_all(copies, axis, split_axis=0, concat_axis=0, tiled=True)
+
+
+def along_y(value, move):
+    pairs = [
+        (s * 4 + r, move(s) * 4 + r) for s in range(4) for r in range(4) if s // 2 == r % 2
+    ]
+    return lax.ppermute(value, ("y", "rep"), pairs)
 
 
 def per_device(factors_in, items, tile_user, levels):
@@ -298,34 +315,73 @@
 
     lev = levels[0].reshape(32, 2, HALF, TILE)
     other = pick(lev, 1 - half, 1)
-    chunks = (other[:8], other[8:16], other[16:])
+    parts, at = [], 0
+    for rows in CHUNKS:
+        parts.append(other[:, at : at + rows])
+        at += rows
     users = factors_in.T.reshape(strip, 2, TILE)
     kept = lax.dynamic_slice_in_dim(users, half * HALF, HALF, 2).reshape(strip, TILE)
     given = lax.dynamic_slice_in_dim(users, (1 - half) * HALF, HALF, 2).reshape(strip, TILE)
     blocks = jnp.zeros((8, TILE), f32).at[0, :32].set(tile_user[0].astype(f32))
     given = jnp.concatenate([given, blocks])
-    panel = items.T
-    panel, kept, given, chunks = tie((panel, kept, given, chunks))
-
-    lev_b = flip(chunks[0], "rep", 4, 2)
-    panel = everyone(panel, ("zh", "rep"), 8).reshape(2, RANK, TILE)
-    panel, given, lev_b, *chunks = tie((panel, given, lev_b, *chunks[1:]))
-    lev_c = flip(chunks[0], "rep", 4, 2)
-    got = flip(given, "rep", 4, 2)
-    user_b = got[strip, :32].astype(jnp.int32)
-    scal = jnp.concatenate([jnp.stack([half, core]).astype(jnp.int32), tile_user[0], user_b])
+
+    moved_levels = [flip(parts[0], "rep", 4, 2)]
+    if X0 == "z":
+        got = flip(given, "rep", 4, 2)
+    panel = everyone(items.T, ("zh", "rep"), 8).reshape(2, RANK, TILE)
+    if X0 == "y":
+        panel, given, moved_levels, *parts = tie((panel, given, moved_levels, *parts[1:]))
+        got = flip(given, "rep", 4, 2)
+    else:
+        panel, got, moved_levels, *parts = tie((panel, got, moved_levels, *parts[1:]))
+
+    moved_levels.append(flip(parts[0], "rep", 4, 2))
     low = jnp.where(half == 0, kept, got[:strip])
     high = jnp.where(half == 0, got[:strip], kept)
     pair = jnp.stack([low, high])
-
-    panel = everyone(panel, "y", 4).reshape(4, 2, RANK, TILE)
-    panel = lax.dynamic_slice_in_dim(panel, 2 * parity, 2, 0).reshape(1, 4, RANK, TILE)
-    panel, pair, scal, lev_c, last = tie((panel, pair, scal, lev_c, chunks[1]))
-    lev_d = flip(last, "rep", 4, 2)
-    next_pair = flip(pair, "rep", 4, 1)
-    own_panels = everyone(panel, "x", 4).reshape(4, 4, RANK, TILE)
-    own_panels, next_pair, lev_d = tie((own_panels, next_pair, lev_d))
+    if X0 == "z":
+        next_pair = flip(pair, "rep", 4, 1)
+    if YS == "perm":
+        inside = y // 2 == parity
+        beside = along_y(panel, lambda s: s ^ 1)
+        across = along_y(panel, lambda s: 3 - s)
+        beyond = along_y(panel, lambda s: (s + 2) % 4)
+        same = jnp.where(inside, panel, beyond)
+        odd = jnp.where(inside, beside, across)
+        even = y % 2 == 0
+        panel = jnp.stack([jnp.where(even, same, odd), jnp.where(even, odd, same)])
+    elif YS == "two":
+        inside = y // 2 == parity
+        across = along_y(panel, lambda s: 3 - s)
+        now = jnp.where(inside, panel, across)
+        beside = flip(now, "y", 4, 1)
+        even = (y % 2 == 0) == inside
+        panel = jnp.stack([jnp.where(even, now, beside), jnp.where(even, beside, now)])
+    else:
+        panel = everyone(panel, "y", 4).reshape(4, 2, RANK, TILE)
+        panel = lax.dynamic_slice_in_dim(panel, 2 * parity, 2, 0)
+    panel = panel.reshape(4, RANK, TILE)
+    if X0 == "y":
+        panel, pair, got, moved_levels, *parts = tie((panel, pair, got, moved_levels, *parts[1:]))
+        next_pair = flip(pair, "rep", 4, 1)
+    else:
+        panel, pair, next_pair, got, moved_levels, *parts = tie(
+            (panel, pair, next_pair, got, moved_levels, *parts[1:])
+        )
+
+    moved_levels.append(flip(parts[0], "rep", 4, 2))
+    if XS == "perm":
+        own_panels = jnp.stack([panel] + [shift(panel, "x", 4, k) for k in (1, 2, 3)])
+    else:
+        own_panels = everyone(panel, "x", 4).reshape(4, 4, RANK, TILE)
+    own_panels, pair, next_pair, got, moved_levels, *parts = tie(
+        (own_panels, pair, next_pair, got, moved_levels, *parts[1:])
+    )
+    moved_levels = moved_levels + [flip(rows, "rep", 4, 2) for rows in parts]
     far_panels = flip(own_panels, "core", 2, 1)
+    user_b = got[strip, :32].astype(jnp.int32)
+    place = jnp.stack([half, core, x]).astype(jnp.int32)
+    scal = jnp.concatenate([place, tile_user[0], user_b])
     first = jnp.where(parity == 0, pair, next_pair)
     second = jnp.where(parity == 0, next_pair, pair)
     x0_t = jnp.stack([first, second], axis=1).reshape(RANK, TILE)
@@ -336,7 +392,7 @@
         (own_scores, far_scores),
         panels,
         lev.reshape(4, GROUPS, 2, HALF, TILE),
-        [v.reshape(-1, GROUPS, HALF, TILE) for v in (lev_b, lev_c, lev_d)],
+        [rows.reshape(4, GROUPS, -1, TILE) for rows in moved_levels],
     )
     shared = (*panels, *weights)
     part_b = flip(part, "rep", 4, 1)
@@ -344,8 +400,8 @@
     got = flip(far_target, "core", 2, 1)
     moved = []
     for k in (1, 2, 3):
-        to = (x + k) % 4
-        moved.append(shift(jnp.stack([pick(target, to), pick(got, to)]), "x", 4, k))
+        to = k if REL else (x - k) % 4
+        moved.append(shift(jnp.stack([pick(target, to), pick(got, to)]), "x", 4, -k))
 
     resid, part = next_apply(second_kernel, (part, part_b, x0), shared, 2, "second_apply")
     part_b = flip(part, "rep", 4, 1)
@@ -354,28 +410,31 @@
     )
     part_b = flip(part, "rep", 4, 1)
     part_b, moved = tie((part_b, moved))
-    solved = pl.pallas_call(
+    solved, copies = pl.pallas_call(
         last_kernel,
-        out_shape=shaped(TILE, RANK),
+        out_shape=[shaped(TILE, RANK), shaped(4, TILE, RANK)],
         compiler_params=params(),
-        cost_estimate=cost(TILE * RANK * 10, 6 * TILE * RANK * 4),
+        cost_estimate=cost(TILE * RANK * 10, 10 * TILE * RANK * 4),
         name="last_update",
     )(part, part_b, resid1, direc1, x1)
 
-    pair = jnp.stack([solved, flip(solved, "core", 2, 1)])
-    vectors = everyone(pair, "x", 4)
+    if FG == "a2a":
+        vectors = lax.all_to_all(copies, "x", split_axis=0, concat_axis=0, tiled=True)
+    else:
+        vectors = jnp.stack([solved] + [shift(solved, "x", 4, -k) for k in (1, 2, 3)])
+    far_vectors = flip(vectors, "core", 2, 1)
 
     smem = pl.BlockSpec(memory_space=pltpu.SMEM)
     vmem = pl.BlockSpec(memory_space=pltpu.VMEM)
     terms = pl.pallas_call(
         rhs_kernel,
-        in_specs=[smem] + [vmem] * 6,
+        in_specs=[smem] + [vmem] * 7,
         out_shape=shaped(2, 4, RANK, TILE),
         scratch_shapes=[pltpu.VMEM((RANK, WIDE), f32)],
         compiler_params=params(),
         cost_estimate=cost(4 * 1024 * RANK * WIDE, 4 << 20),
         name="rhs_terms",
-    )(jnp.stack([x, core]).astype(jnp.int32), vectors, target, got, *moved)
+    )(jnp.stack([x, core]).astype(jnp.int32), vectors, far_vectors, target, got, *moved)
 
     terms, solved = tie((terms, solved))
     strips = solved.reshape(TILE, 4, strip)

time: 193 us -> 173 us (0.90)
  waiting for transfers between devices: 109 us -> 92.3 us
  blocking collectives: 0 us -> 12.9 us
  local copies, waits for them, and re-layouts: 15.6 us -> 6.46 us
  starting transfers between devices: 46.9 us -> 37.8 us
    ppermute x12 -> x13, waiting for transfers between devices: 68.8 us -> 34.6 us  [flip(): return lax.ppermute(value, axis, [(i, i ^ bit) for i in range(size)])]
    ppermute x3 -> x6, waiting for transfers between devices: 3.99 us -> 25 us  [shift(): lax.ppermute(value, axis, [(i, (i + by) % size) for i in range(size)])]
    all_to_all x0 -> x1, blocking collectives: none -> 12.9 us  [per_device(): lax.all_to_all(copies, 'x', split_axis=0, concat_axis=0, tiled=True)]
    all_to_all x4 -> x2, starting transfers between devices: 23.7 us -> 12.9 us  [everyone(): return lax.all_to_all(copies, axis, split_axis=0, concat_axis=0, tiled=True)]
    unnamed x44 -> x12, local copies, waits for them, and re-layouts: 6.4 us -> 0.03 us
    ppermute x3 -> x6, starting transfers between devices: 4.33 us -> 9.29 us  [shift(): lax.ppermute(value, axis, [(i, (i + by) % size) for i in range(size)])]
    all_to_all x4 -> x2, waiting for transfers between devices: 17 us -> 12.5 us  [everyone(): return lax.all_to_all(copies, axis, split_axis=0, concat_axis=0, tiled=True)]
    ppermute x12 -> x13, starting transfers between devices: 9.13 us -> 5.5 us  [flip(): return lax.ppermute(value, axis, [(i, i ^ bit) for i in range(size)])]
  transfers between devices with their start and end apart: 21 -> 23, of which waited for: 16 -> 16; matrix products, arithmetic and copies ran while one was open for 1% -> 3% of each run, Pallas kernels for 4% -> 7%
where the time goes in v3:
time: 173 us; the launch traced here: 172 us
  waiting for transfers between devices  92.3 us (53%)
  starting transfers between devices  37.8 us (22%)
  Pallas kernels  18.3 us (11%)
  blocking collectives  12.9 us (7%)
  local copies, waits for them, and re-layouts  6.46 us (4%)
  other arithmetic  3.43 us (2%)
    ppermute x13, waiting for transfers between devices, flip(): return lax.ppermute(value, axis, [(i, i ^ bit) for i in range(size)])  34.6 us
    ppermute x6, waiting for transfers between devices, shift(): lax.ppermute(value, axis, [(i, (i + by) % size) for i in range(size)])  25 us
    all_to_all x2, starting transfers between devices, everyone(): return lax.all_to_all(copies, axis, split_axis=0, concat_axis=0, tiled=True)  12.9 us
    all_to_all x1, blocking collectives, per_device(): lax.all_to_all(copies, 'x', split_axis=0, concat_axis=0, tiled=True)  12.9 us
    all_to_all x2, waiting for transfers between devices, everyone(): return lax.all_to_all(copies, axis, split_axis=0, concat_axis=0, tiled=True)  12.5 us
    all_to_all x1, waiting for transfers between devices, per_device(): lax.all_to_all(summed, ('zh', 'rep'), split_axis=0, concat_axis=0, tiled=...  11 us
    ppermute x6, starting transfers between devices, shift(): lax.ppermute(value, axis, [(i, (i + by) % size) for i in range(size)])  9.29 us
    all_to_all x1, waiting for transfers between devices, per_device(): lax.all_to_all(terms.reshape(4, 8, strip, TILE), 'y', split_axis=0, conca...  9.18 us
  transfers between devices with their start and end apart: 23, of which 16 were waited for; matrix products, arithmetic and copies ran while one was open for 3% of the time, Pallas kernels for 7%

profile of v3, /device:TPU:6, one launch (start us, length us, event | category | flops | bytes accessed | tf_op | source)
XLA Modules:
  0.0 172.1 jit_solution(12234350144155644066)
XLA Ops:
  0.6 1.5 broadcast_in_dim.4
  2.2 8.5 %all-to-all-start = ((f32[8,64,128]{2,1,0:T(8,128)}), f32[8,64,128]{2,1,0:T(8,128)S(1)}, u32[]{:S(2)}, u32[]{:S(2)}) async-start(f32[8,64,128]{2,1,0:T(8,128)} %broadcast_in_dim.4), calls=%async_computation | async-start | bytes 524288 | tf_op jit(solution)/shard_map/all_to_all | solution.py:299
  10.6 1.3 dynamic-slice_bitcast_fusion
  12.6 2.9 %collective-permute-start.1 = (s32[32,8,128]{2,1,0:T(8,128)S(1)}, s32[32,8,128]{2,1,0:T(8,128)S(1)}, u32[]{:S(2)}, u32[]{:S(2)}) collective-permute-start(s32[32,8,128]{2,1,0:T(8,128)S(1)} %get-tuple-element.121), channel_id=1, source_target_pairs={{0,2},{1,3},{2,0},{3,1},{4,6},{5,7},{6,4},{7,5},{8,10},{9,11},{10,... | collective-permute-start | bytes 393224 | tf_op jit(solution)/shard_map/ppermute | solution.py:281
  16.1 10.8 %collective-permute-done = f32[72,128]{1,0:T(8,128)S(1)} collective-permute-done((f32[72,128]{1,0:T(8,128)S(1)}, f32[72,128]{1,0:T(8,128)S(1)}, u32[]{:S(2)}, u32[]{:S(2)}) %collective-permute-start) | collective-permute-done | bytes 36896 | tf_op jit(solution)/shard_map/ppermute | solution.py:281
  26.9 1.0 broadcast_in_dim.5
  27.9 4.5 %all-to-all-start.1 = ((f32[4,2,256,128]{3,2,1,0:T(8,128)}), f32[4,2,256,128]{3,2,1,0:T(8,128)S(1)}, u32[]{:S(2)}, u32[]{:S(2)}) async-start(f32[4,2,256,128]{3,2,1,0:T(8,128)} %broadcast_in_dim.5), calls=%async_computation.1 | async-start | bytes 2097152 | tf_op jit(solution)/shard_map/all_to_all | solution.py:299
  32.6 1.6 collective-permute-start.2
  34.2 12.5 %all-to-all-done.1 = f32[4,2,256,128]{3,2,1,0:T(8,128)S(1)} async-done(((f32[4,2,256,128]{3,2,1,0:T(8,128)}), f32[4,2,256,128]{3,2,1,0:T(8,128)S(1)}, u32[]{:S(2)}, u32[]{:S(2)}) %all-to-all-start.1) | async-done | bytes 1048608 | tf_op jit(solution)/shard_map/all_to_all | solution.py:299
  47.7 1.1 collective-permute-start.5
  48.9 2.1 %collective-permute-start.4 = (f32[4,256,128]{2,1,0:T(8,128)S(1)}, f32[4,256,128]{2,1,0:T(8,128)S(1)}, u32[]{:S(2)}, u32[]{:S(2)}) collective-permute-start(f32[4,256,128]{2,1,0:T(8,128)S(1)} %bitcast.61), channel_id=1, source_target_pairs={{0,8},{8,16},{16,24},{24,0},{1,9},{9,17},{17,25},{25,1},{2,10},{10... | collective-permute-start | bytes 1572872 | tf_op jit(solution)/shard_map/ppermute | solution.py:277
  51.0 20.4 %collective-permute-done.6 = f32[4,256,128]{2,1,0:T(8,128)S(1)} collective-permute-done((f32[4,256,128]{2,1,0:T(8,128)S(1)}, f32[4,256,128]{2,1,0:T(8,128)S(1)}, u32[]{:S(2)}, u32[]{:S(2)}) %collective-permute-start.6) | collective-permute-done | bytes 524320 | tf_op jit(solution)/shard_map/ppermute | solution.py:277
  72.2 1.7 collective-permute-done.7
  75.5 2.6 %collective-permute-done.8.far = f32[4,4,256,128]{3,2,1,0:T(8,128)} collective-permute-done((f32[4,4,256,128]{3,2,1,0:T(8,128)S(1)}, f32[4,4,256,128]{3,2,1,0:T(8,128)}, u32[]{:S(2)}, u32[]{:S(2)}) %collective-permute-start.8) | collective-permute-done | bytes 2097184 | tf_op jit(solution)/shard_map/ppermute | solution.py:281
  78.1 3.7 %first_scores.1 = (bf16[4,256,512]{2,1,0:T(8,128)(2,1)S(1)}, bf16[4,256,512]{2,1,0:T(8,128)(2,1)S(1)}, bf16[4,256,512]{2,1,0:T(8,128)(2,1)S(1)}, bf16[4,256,512]...) custom-call(f32[256,128]{1,0:T(8,128)S(1)} %bitcast.58, ...), custom_call_target="tpu_custom_call" | custom-call | flops 805306368 | bytes 10485760 | tf_op jit(solution)/shard_map/first_scores/pallas_call | solution.py:216
  82.6 4.3 %first_apply.1 = (bf16[4,128,512]{2,1,0:T(8,128)(2,1)S(1)}, bf16[4,128,512]{2,1,0:T(8,128)(2,1)S(1)}, f32[4,128,512]{2,1,0:T(8,128)S(1)}, f32[4,128,512]{2,1,0:T(8,128)S(1)}, f32[128,256]{1,0:T(8,128)S(1)}) custom-call(s32[67]{0:T(128)S(1)} %concatenate.9.scal, f32[4,128,512]{2,1,0:T(8,128)S(1)} %get-tuple-element.82.refs_0_, ...), custom_call_target="tpu_custom_call" | custom-call | flops 805306368 | bytes 12582912 | tf_op jit(solution)/shard_map/first_apply/pallas_call | solution.py:244
  87.1 2.5 %collective-permute-done.13.got = f32[4,128,512]{2,1,0:T(8,128)S(1)} collective-permute-done((f32[4,128,512]{2,1,0:T(8,128)S(1)}, f32[4,128,512]{2,1,0:T(8,128)S(1)}, u32[]{:S(2)}, u32[]{:S(2)}) %collective-permute-start.13) | collective-permute-done | bytes 1048608 | tf_op jit(solution)/shard_map/ppermute | solution.py:281
  90.3 2.8 %collective-permute-start.15 = (f32[2,128,512]{2,1,0:T(8,128)S(1)}, f32[2,128,512]{2,1,0:T(8,128)S(1)}, u32[]{:S(2)}, u32[]{:S(2)}) collective-permute-start(f32[2,128,512]{2,1,0:T(8,128)S(1)} %pad_maximum_fusion.2), channel_id=1, source_target_pairs={{0,16},{8,24},{16,0},{24,8},{1,17},{9,25},{17,1},{25,9},{2,18},{10... | collective-permute-start | bytes 1572872 | tf_op jit(solution)/shard_map/ppermute | solution.py:277
  93.1 1.9 %collective-permute-start.16 = (f32[2,128,512]{2,1,0:T(8,128)S(1)}, f32[2,128,512]{2,1,0:T(8,128)S(1)}, u32[]{:S(2)}, u32[]{:S(2)}) collective-permute-start(f32[2,128,512]{2,1,0:T(8,128)S(1)} %pad_maximum_fusion.3), channel_id=1, source_target_pairs={{0,8},{8,16},{16,24},{24,0},{1,9},{9,17},{17,25},{25,1},{2,10},{10... | collective-permute-start | bytes 1572872 | tf_op jit(solution)/shard_map/ppermute | solution.py:277
  95.0 3.8 %second_apply.1 = (f32[128,256]{1,0:T(8,128)S(1)}, f32[128,256]{1,0:T(8,128)S(1)}) custom-call(f32[128,256]{1,0:T(8,128)S(1)} %get-tuple-element.92.pa, f32[128,256]{1,0:T(8,128)S(1)} %collective-permute-done.10.pb, f32[128,256]{1,0:T(8,128)S(1)} %get-tuple-element.93.x0, bf16[4,256,512]{2,1,0:T(8,128)(2,1)S(1)} %get-tuple-element.84.refs_2_.refs_0_, ...), custom_call_target="tpu_custom_call" | custom-call | flops 1610612736 | bytes 6291456 | tf_op jit(solution)/shard_map/second_apply/pallas_call | solution.py:263
  98.9 5.0 %collective-permute-done.11.pb = f32[128,256]{1,0:T(8,128)S(1)} collective-permute-done((f32[128,256]{1,0:T(8,128)S(1)}, f32[128,256]{1,0:T(8,128)S(1)}, u32[]{:S(2)}, u32[]{:S(2)}) %collective-permute-start.11) | collective-permute-done | bytes 131104 | tf_op jit(solution)/shard_map/ppermute | solution.py:281
  103.9 4.0 %third_apply.1 = (f32[128,256]{1,0:T(8,128)S(1)}, f32[128,256]{1,0:T(8,128)S(1)}, f32[128,256]{1,0:T(8,128)S(1)}, f32[128,256]{1,0:T(8,128)S(1)}) custom-call(f32[128,256]{1,0:T(8,128)S(1)} %get-tuple-element.96.pa, f32[128,256]{1,0:T(8,128)S(1)} %collective-permute-done.11.pb, f32[128,256]{1,0:T(8,128)S(1)} %get-tuple-element.97.resid, ...), custom_call_target="tpu_custom_call" | custom-call | flops 1610612736 | bytes 6291456 | tf_op jit(solution)/shard_map/third_apply/pallas_call | solution.py:263
  108.1 4.9 %collective-permute-done.12.pb = f32[128,256]{1,0:T(8,128)S(1)} collective-permute-done((f32[128,256]{1,0:T(8,128)S(1)}, f32[128,256]{1,0:T(8,128)S(1)}, u32[]{:S(2)}, u32[]{:S(2)}) %collective-permute-start.12) | collective-permute-done | bytes 131104 | tf_op jit(solution)/shard_map/ppermute | solution.py:281
  113.0 3.2 %collective-permute-done.15.t2 = f32[2,128,512]{2,1,0:T(8,128)S(1)} collective-permute-done((f32[2,128,512]{2,1,0:T(8,128)S(1)}, f32[2,128,512]{2,1,0:T(8,128)S(1)}, u32[]{:S(2)}, u32[]{:S(2)}) %collective-permute-start.15) | collective-permute-done | bytes 524320 | tf_op jit(solution)/shard_map/ppermute | solution.py:277
  117.1 12.9 %all_to_all.25.own_vectors = f32[4,128,256]{2,1,0:T(8,128)S(1)} all-to-all(f32[4,128,256]{2,1,0:T(8,128)S(1)} %get-tuple-element.105), channel_id=1, replica_groups=mesh['y'=4,'zh'=2,'x'=4,'core'=2,'rep'=4] {'x'}, dimensions={0} | all-to-all | bytes 1048576 | tf_op jit(solution)/shard_map/all_to_all | solution.py:422
  130.1 1.8 %collective-permute-done.17.far_vectors = f32[4,128,256]{2,1,0:T(8,128)S(1)} collective-permute-done((f32[4,128,256]{2,1,0:T(8,128)S(1)}, f32[4,128,256]{2,1,0:T(8,128)S(1)}, u32[]{:S(2)}, u32[]{:S(2)}) %collective-permute-start.17) | collective-permute-done | bytes 524320 | tf_op jit(solution)/shard_map/ppermute | solution.py:281
  131.9 2.3 %rhs_terms.1 = f32[2,4,256,128]{3,2,1,0:T(8,128)} custom-call(s32[2]{0:T(128)S(1)} %pad_add_fusion.scal, f32[4,128,256]{2,1,0:T(8,128)S(1)} %all_to_all.25.own_vectors, f32[4,128,256]{2,1,0:T(8,128)S(1)} %collective-permute-done.17.far_vectors, f32[4,128,512]{2,1,0:T(8,128)S(1)} %get-tuple-element.99.own, f32[4,128,512]{2,1,0:T(8,128)S(1)} %collective-permute-done.13.got, ...), custom_call_target="tpu_custom_call" | custom-call | flops 536870912 | bytes 4194304 | tf_op jit(solution)/shard_map/rhs_terms/pallas_call | solution.py:429
  134.2 4.5 %all-to-all-start.3 = ((f32[4,8,64,128]{3,2,1,0:T(8,128)}), f32[4,8,64,128]{3,2,1,0:T(8,128)S(1)}, u32[]{:S(2)}, u32[]{:S(2)}) async-start(f32[4,8,64,128]{3,2,1,0:T(8,128)} %bitcast.25), calls=%async_computation.3 | async-start | bytes 2097152 | tf_op jit(solution)/shard_map/all_to_all | solution.py:447
  139.2 4.5 %collective-permute-done.18 = f32[128,64]{0,1:T(8,128)S(1)} collective-permute-done((f32[128,64]{0,1:T(8,128)S(1)}, f32[128,64]{0,1:T(8,128)S(1)}, u32[]{:S(2)}, u32[]{:S(2)}) %collective-permute-start.18) | collective-permute-done | bytes 32800 | tf_op jit(solution)/shard_map/ppermute | solution.py:281
  145.0 9.2 %all-to-all-done.3 = f32[4,8,64,128]{3,2,1,0:T(8,128)S(1)} async-done(((f32[4,8,64,128]{3,2,1,0:T(8,128)}), f32[4,8,64,128]{3,2,1,0:T(8,128)S(1)}, u32[]{:S(2)}, u32[]{:S(2)}) %all-to-all-start.3) | async-done | bytes 1048608 | tf_op jit(solution)/shard_map/all_to_all | solution.py:447
  154.9 5.6 %all-to-all-start.4 = ((f32[8,64,128]{2,1,0:T(8,128)}), f32[8,64,128]{2,1,0:T(8,128)S(1)}, u32[]{:S(2)}, u32[]{:S(2)}) async-start(f32[8,64,128]{2,1,0:T(8,128)} %reduce_sum.18), calls=%async_computation.4 | async-start | bytes 524288 | tf_op jit(solution)/shard_map/all_to_all | solution.py:451
  160.5 11.0 %all-to-all-done.4 = f32[8,64,128]{2,1,0:T(8,128)S(1)} async-done(((f32[8,64,128]{2,1,0:T(8,128)}), f32[8,64,128]{2,1,0:T(8,128)S(1)}, u32[]{:S(2)}, u32[]{:S(2)}) %all-to-all-start.4) | async-done | bytes 262176 | tf_op jit(solution)/shard_map/all_to_all | solution.py:451
  (71 shorter events, 10.7 us)
Async XLA Ops:
  0.6 14.9 %copy-start.5 = (s32[1,32]{1,0:T(1,128)S(1)}, s32[1,32]{1,0:T(1,128)}, u32[]{:S(2)}) copy-start(s32[1,32]{1,0:T(1,128)} %param.8) | copy-start | bytes 388
  0.6 14.9 %copy-start.2 = (f32[256,64]{0,1:T(8,128)S(1)}, f32[256,64]{0,1:T(8,128)}, u32[]{:S(2)}) copy-start(f32[256,64]{0,1:T(8,128)} %param.6) | copy-start | bytes 196612
  2.2 24.7 %all-to-all-start = ((f32[8,64,128]{2,1,0:T(8,128)}), f32[8,64,128]{2,1,0:T(8,128)S(1)}, u32[]{:S(2)}, u32[]{:S(2)}) async-start(f32[8,64,128]{2,1,0:T(8,128)} %broadcast_in_dim.4), calls=%async_computation | async-start | bytes 524288 | tf_op jit(solution)/shard_map/all_to_all | solution.py:299
  12.6 14.3 %collective-permute-start.1 = (s32[32,8,128]{2,1,0:T(8,128)S(1)}, s32[32,8,128]{2,1,0:T(8,128)S(1)}, u32[]{:S(2)}, u32[]{:S(2)}) collective-permute-start(s32[32,8,128]{2,1,0:T(8,128)S(1)} %get-tuple-element.121), channel_id=1, source_target_pairs={{0,2},{1,3},{2,0},{3,1},{4,6},{5,7},{6,4},{7,5},{8,10},{9,11},{10,... | collective-permute-start | bytes 393224 | tf_op jit(solution)/shard_map/ppermute | solution.py:281
  15.9 11.0 %collective-permute-start = (f32[72,128]{1,0:T(8,128)S(1)}, f32[72,128]{1,0:T(8,128)S(1)}, u32[]{:S(2)}, u32[]{:S(2)}) collective-permute-start(f32[72,128]{1,0:T(8,128)S(1)} %select_maximum_fusion), channel_id=1, source_target_pairs={{0,2},{1,3},{2,0},{3,1},{4,6},{5,7},{6,4},{7,5},{8,10},{9,11},{10,... | collective-permute-start | bytes 110600 | tf_op jit(solution)/shard_map/ppermute | solution.py:281
  26.9 19.9 %copy-start.4 = (f32[72,128]{1,0:T(8,128)}, f32[72,128]{1,0:T(8,128)S(1)}, u32[]{:S(2)}) copy-start(f32[72,128]{1,0:T(8,128)S(1)} %collective-permute-done) | copy-start | bytes 110596
  27.9 18.8 %all-to-all-start.1 = ((f32[4,2,256,128]{3,2,1,0:T(8,128)}), f32[4,2,256,128]{3,2,1,0:T(8,128)S(1)}, u32[]{:S(2)}, u32[]{:S(2)}) async-start(f32[4,2,256,128]{3,2,1,0:T(8,128)} %broadcast_in_dim.5), calls=%async_computation.1 | async-start | bytes 2097152 | tf_op jit(solution)/shard_map/all_to_all | solution.py:299
  32.5 14.3 %collective-permute-start.3 = (s32[32,16,128]{2,1,0:T(8,128)S(1)}, s32[32,16,128]{2,1,0:T(8,128)S(1)}, u32[]{:S(2)}, u32[]{:S(2)}) collective-permute-start(s32[32,16,128]{2,1,0:T(8,128)S(1)} %slice.48), channel_id=1, source_target_pairs={{0,2},{1,3},{2,0},{3,1},{4,6},{5,7},{6,4},{7,5},{8,10},{9,11},{10,... | collective-permute-start | bytes 786440 | tf_op jit(solution)/shard_map/ppermute | solution.py:281
  32.6 16.2 %copy-start.1 = (f32[2,64,128]{2,1,0:T(8,128)}, f32[2,64,128]{2,1,0:T(8,128)S(1)}, u32[]{:S(2)}) copy-start(f32[2,64,128]{2,1,0:T(8,128)S(1)} %pad_maximum_fusion.6) | copy-start | bytes 196612
  32.6 14.2 %collective-permute-start.2 = (f32[2,64,128]{2,1,0:T(8,128)S(1)}, f32[2,64,128]{2,1,0:T(8,128)S(1)}, u32[]{:S(2)}, u32[]{:S(2)}) collective-permute-start(f32[2,64,128]{2,1,0:T(8,128)S(1)} %pad_maximum_fusion.6), channel_id=1, source_target_pairs={{0,1},{1,0},{2,3},{3,2},{4,5},{5,4},{6,7},{7,6},{8,9},{9,8},{10,11... | collective-permute-start | bytes 196616 | tf_op jit(solution)/shard_map/ppermute | solution.py:281
  46.8 2.0 %copy-start.3 = (f32[2,64,128]{2,1,0:T(8,128)}, f32[2,64,128]{2,1,0:T(8,128)S(1)}, u32[]{:S(2)}) copy-start(f32[2,64,128]{2,1,0:T(8,128)S(1)} %collective-permute-done.2) | copy-start | bytes 196612
  46.8 24.5 %collective-permute-start.6 = (f32[4,256,128]{2,1,0:T(8,128)S(1)}, f32[4,256,128]{2,1,0:T(8,128)S(1)}, u32[]{:S(2)}, u32[]{:S(2)}) collective-permute-start(f32[4,256,128]{2,1,0:T(8,128)S(1)} %bitcast.59), channel_id=1, source_target_pairs={{0,24},{8,0},{16,8},{24,16},{1,25},{9,1},{17,9},{25,17},{2,26},{10... | collective-permute-start | bytes 1572872 | tf_op jit(solution)/shard_map/ppermute | solution.py:277
  47.7 23.6 %collective-permute-start.5 = (f32[4,256,128]{2,1,0:T(8,128)S(1)}, f32[4,256,128]{2,1,0:T(8,128)S(1)}, u32[]{:S(2)}, u32[]{:S(2)}) collective-permute-start(f32[4,256,128]{2,1,0:T(8,128)S(1)} %bitcast.60), channel_id=1, source_target_pairs={{0,16},{8,24},{16,0},{24,8},{1,17},{9,25},{17,1},{25,9},{2,18},{10... | collective-permute-start | bytes 1572872 | tf_op jit(solution)/shard_map/ppermute | solution.py:277
  48.9 23.1 %collective-permute-start.4 = (f32[4,256,128]{2,1,0:T(8,128)S(1)}, f32[4,256,128]{2,1,0:T(8,128)S(1)}, u32[]{:S(2)}, u32[]{:S(2)}) collective-permute-start(f32[4,256,128]{2,1,0:T(8,128)S(1)} %bitcast.61), channel_id=1, source_target_pairs={{0,8},{8,16},{16,24},{24,0},{1,9},{9,17},{17,25},{25,1},{2,10},{10... | collective-permute-start | bytes 1572872 | tf_op jit(solution)/shard_map/ppermute | solution.py:277
  51.0 22.9 %collective-permute-start.7 = (s32[32,32,128]{2,1,0:T(8,128)S(1)}, s32[32,32,128]{2,1,0:T(8,128)S(1)}, u32[]{:S(2)}, u32[]{:S(2)}) collective-permute-start(s32[32,32,128]{2,1,0:T(8,128)S(1)} %slice.49), channel_id=1, source_target_pairs={{0,2},{1,3},{2,0},{3,1},{4,6},{5,7},{6,4},{7,5},{8,10},{9,11},{10,... | collective-permute-start | bytes 1572872 | tf_op jit(solution)/shard_map/ppermute | solution.py:281
  73.8 4.3 %collective-permute-start.8 = (f32[4,4,256,128]{3,2,1,0:T(8,128)S(1)}, f32[4,4,256,128]{3,2,1,0:T(8,128)}, u32[]{:S(2)}, u32[]{:S(2)}) collective-permute-start(f32[4,4,256,128]{3,2,1,0:T(8,128)S(1)} %pad_maximum_fusion.own), channel_id=1, source_target_pairs={{0,4},{4,0},{1,5},{5,1},{2,6},{6,2},{3,7},{7,3},{8,12},{12,8},{9,1... | collective-permute-start | bytes 6291464 | tf_op jit(solution)/shard_map/ppermute | solution.py:281
  73.8 8.8 %collective-permute-start.9 = (s32[32,8,128]{2,1,0:T(8,128)}, s32[32,8,128]{2,1,0:T(8,128)S(1)}, u32[]{:S(2)}, u32[]{:S(2)}) collective-permute-start(s32[32,8,128]{2,1,0:T(8,128)} %get-tuple-element.91), channel_id=1, source_target_pairs={{0,2},{1,3},{2,0},{3,1},{4,6},{5,7},{6,4},{7,5},{8,10},{9,11},{10,... | collective-permute-start | bytes 393224 | tf_op jit(solution)/shard_map/ppermute | solution.py:281
  78.1 4.5 %copy-start = (s32[1,32,128,128]{3,2,1,0:T(8,128)S(1)}, s32[1,32,128,128]{3,2,1,0:T(8,128)}, u32[]{:S(2)}) copy-start(s32[1,32,128,128]{3,2,1,0:T(8,128)} %param.9) | copy-start | bytes 6291460
  86.9 2.7 %collective-permute-start.13 = (f32[4,128,512]{2,1,0:T(8,128)S(1)}, f32[4,128,512]{2,1,0:T(8,128)S(1)}, u32[]{:S(2)}, u32[]{:S(2)}) collective-permute-start(f32[4,128,512]{2,1,0:T(8,128)S(1)} %get-tuple-element.100), channel_id=1, source_target_pairs={{0,4},{4,0},{1,5},{5,1},{2,6},{6,2},{3,7},{7,3},{8,12},{12,8},{9,1... | collective-permute-start | bytes 3145736 | tf_op jit(solution)/shard_map/ppermute | solution.py:281
  87.0 7.9 %collective-permute-start.10 = (f32[128,256]{1,0:T(8,128)S(1)}, f32[128,256]{1,0:T(8,128)S(1)}, u32[]{:S(2)}, u32[]{:S(2)}) collective-permute-start(f32[128,256]{1,0:T(8,128)S(1)} %get-tuple-element.92.pa), channel_id=1, source_target_pairs={{0,1},{1,0},{2,3},{3,2},{4,5},{5,4},{6,7},{7,6},{8,9},{9,8},{10,11... | collective-permute-start | bytes 393224 | tf_op jit(solution)/shard_map/ppermute | solution.py:281
  89.7 23.3 %collective-permute-start.14 = (f32[2,128,512]{2,1,0:T(8,128)S(1)}, f32[2,128,512]{2,1,0:T(8,128)S(1)}, u32[]{:S(2)}, u32[]{:S(2)}) collective-permute-start(f32[2,128,512]{2,1,0:T(8,128)S(1)} %pad_maximum_fusion.1), channel_id=1, source_target_pairs={{0,24},{8,0},{16,8},{24,16},{1,25},{9,1},{17,9},{25,17},{2,26},{10... | collective-permute-start | bytes 1572872 | tf_op jit(solution)/shard_map/ppermute | solution.py:277
  90.3 25.9 %collective-permute-start.15 = (f32[2,128,512]{2,1,0:T(8,128)S(1)}, f32[2,128,512]{2,1,0:T(8,128)S(1)}, u32[]{:S(2)}, u32[]{:S(2)}) collective-permute-start(f32[2,128,512]{2,1,0:T(8,128)S(1)} %pad_maximum_fusion.2), channel_id=1, source_target_pairs={{0,16},{8,24},{16,0},{24,8},{1,17},{9,25},{17,1},{25,9},{2,18},{10... | collective-permute-start | bytes 1572872 | tf_op jit(solution)/shard_map/ppermute | solution.py:277
  93.1 23.8 %collective-permute-start.16 = (f32[2,128,512]{2,1,0:T(8,128)S(1)}, f32[2,128,512]{2,1,0:T(8,128)S(1)}, u32[]{:S(2)}, u32[]{:S(2)}) collective-permute-start(f32[2,128,512]{2,1,0:T(8,128)S(1)} %pad_maximum_fusion.3), channel_id=1, source_target_pairs={{0,8},{8,16},{16,24},{24,0},{1,9},{9,17},{17,25},{25,1},{2,10},{10... | collective-permute-start | bytes 1572872 | tf_op jit(solution)/shard_map/ppermute | solution.py:277
  98.8 5.1 %collective-permute-start.11 = (f32[128,256]{1,0:T(8,128)S(1)}, f32[128,256]{1,0:T(8,128)S(1)}, u32[]{:S(2)}, u32[]{:S(2)}) collective-permute-start(f32[128,256]{1,0:T(8,128)S(1)} %get-tuple-element.96.pa), channel_id=1, source_target_pairs={{0,1},{1,0},{2,3},{3,2},{4,5},{5,4},{6,7},{7,6},{8,9},{9,8},{10,11... | collective-permute-start | bytes 393224 | tf_op jit(solution)/shard_map/ppermute | solution.py:281
  107.9 5.1 %collective-permute-start.12 = (f32[128,256]{1,0:T(8,128)S(1)}, f32[128,256]{1,0:T(8,128)S(1)}, u32[]{:S(2)}, u32[]{:S(2)}) collective-permute-start(f32[128,256]{1,0:T(8,128)S(1)} %get-tuple-element.98.pa), channel_id=1, source_target_pairs={{0,1},{1,0},{2,3},{3,2},{4,5},{5,4},{6,7},{7,6},{8,9},{9,8},{10,11... | collective-permute-start | bytes 393224 | tf_op jit(solution)/shard_map/ppermute | solution.py:281
  130.0 1.9 %collective-permute-start.17 = (f32[4,128,256]{2,1,0:T(8,128)S(1)}, f32[4,128,256]{2,1,0:T(8,128)S(1)}, u32[]{:S(2)}, u32[]{:S(2)}) collective-permute-start(f32[4,128,256]{2,1,0:T(8,128)S(1)} %all_to_all.25.own_vectors), channel_id=1, source_target_pairs={{0,4},{4,0},{1,5},{5,1},{2,6},{6,2},{3,7},{7,3},{8,12},{12,8},{9,1... | collective-permute-start | bytes 1572872 | tf_op jit(solution)/shard_map/ppermute | solution.py:281
  134.2 19.9 %all-to-all-start.3 = ((f32[4,8,64,128]{3,2,1,0:T(8,128)}), f32[4,8,64,128]{3,2,1,0:T(8,128)S(1)}, u32[]{:S(2)}, u32[]{:S(2)}) async-start(f32[4,8,64,128]{3,2,1,0:T(8,128)} %bitcast.25), calls=%async_computation.3 | async-start | bytes 2097152 | tf_op jit(solution)/shard_map/all_to_all | solution.py:447
  138.9 4.9 %collective-permute-start.18 = (f32[128,64]{0,1:T(8,128)S(1)}, f32[128,64]{0,1:T(8,128)S(1)}, u32[]{:S(2)}, u32[]{:S(2)}) collective-permute-start(f32[128,64]{0,1:T(8,128)S(1)} %dynamic-slice_bitcast_fusion.1), channel_id=1, source_target_pairs={{0,2},{1,3},{2,0},{3,1},{4,6},{5,7},{6,4},{7,5},{8,10},{9,11},{10,... | collective-permute-start | bytes 98312 | tf_op jit(solution)/shard_map/ppermute | solution.py:281
  154.9 16.6 %all-to-all-start.4 = ((f32[8,64,128]{2,1,0:T(8,128)}), f32[8,64,128]{2,1,0:T(8,128)S(1)}, u32[]{:S(2)}, u32[]{:S(2)}) async-start(f32[8,64,128]{2,1,0:T(8,128)} %reduce_sum.18), calls=%async_computation.4 | async-start | bytes 524288 | tf_op jit(solution)/shard_map/all_to_all | solution.py:451

commit v4 on v3

--- a/solution.py
+++ b/solution.py
@@ -288,10 +288,13 @@
 VMEM = 16777216
 FG = 'a2a'
 XS = 'perm'
+YS = 'a2a'
 REL = 1
-YS = 'a2a'
-X0 = 'z'
-CHUNKS = (8,16,32,8)
+FP = 'early'
+TAIL = 'a2a'
+XC = 0
+NP = 'y'
+CHUNKS = (56,8)
 
 
 def everyone(value, axis, size):
@@ -325,22 +328,20 @@
     blocks = jnp.zeros((8, TILE), f32).at[0, :32].set(tile_user[0].astype(f32))
     given = jnp.concatenate([given, blocks])
 
-    moved_levels = [flip(parts[0], "rep", 4, 2)]
-    if X0 == "z":
-        got = flip(given, "rep", 4, 2)
-    panel = everyone(items.T, ("zh", "rep"), 8).reshape(2, RANK, TILE)
-    if X0 == "y":
-        panel, given, moved_levels, *parts = tie((panel, given, moved_levels, *parts[1:]))
-        got = flip(given, "rep", 4, 2)
-    else:
-        panel, got, moved_levels, *parts = tie((panel, got, moved_levels, *parts[1:]))
-
-    moved_levels.append(flip(parts[0], "rep", 4, 2))
+    moved_levels = []
+    got = flip(given, "rep", 4, 2)
     low = jnp.where(half == 0, kept, got[:strip])
     high = jnp.where(half == 0, got[:strip], kept)
     pair = jnp.stack([low, high])
-    if X0 == "z":
+    next_pair = flip(pair, "rep", 4, 1)
+    panel = everyone(items.T, ("zh", "rep"), 8).reshape(2, RANK, TILE)
+    if NP == "z":
+        panel, pair, next_pair, got, *parts = tie((panel, pair, next_pair, got, *parts))
+    else:
+        panel, pair, got, *parts = tie((panel, pair, got, *parts))
         next_pair = flip(pair, "rep", 4, 1)
+
+    moved_levels.append(flip(parts[0], "rep", 4, 2))
     if YS == "perm":
         inside = y // 2 == parity
         beside = along_y(panel, lambda s: s ^ 1)
@@ -361,21 +362,21 @@
         panel = everyone(panel, "y", 4).reshape(4, 2, RANK, TILE)
         panel = lax.dynamic_slice_in_dim(panel, 2 * parity, 2, 0)
     panel = panel.reshape(4, RANK, TILE)
-    if X0 == "y":
-        panel, pair, got, moved_levels, *parts = tie((panel, pair, got, moved_levels, *parts[1:]))
-        next_pair = flip(pair, "rep", 4, 1)
-    else:
-        panel, pair, next_pair, got, moved_levels, *parts = tie(
-            (panel, pair, next_pair, got, moved_levels, *parts[1:])
-        )
-
-    moved_levels.append(flip(parts[0], "rep", 4, 2))
-    if XS == "perm":
+    panel, pair, got, *parts = tie((panel, pair, got, *parts[1:]))
+
+    if XC:
+        moved_levels.append(flip(parts[0], "rep", 4, 2))
+        parts = parts[1:]
+    if XS == "ring":
+        left, right = shift(panel, "x", 4, 1), shift(panel, "x", 4, -1)
+        over = jnp.concatenate([shift(left[:2], "x", 4, 1), shift(right[2:], "x", 4, -1)])
+        own_panels = jnp.stack([panel, left, over, right])
+    elif XS == "perm":
         own_panels = jnp.stack([panel] + [shift(panel, "x", 4, k) for k in (1, 2, 3)])
     else:
         own_panels = everyone(panel, "x", 4).reshape(4, 4, RANK, TILE)
     own_panels, pair, next_pair, got, moved_levels, *parts = tie(
-        (own_panels, pair, next_pair, got, moved_levels, *parts[1:])
+        (own_panels, pair, next_pair, got, moved_levels, *parts)
     )
     moved_levels = moved_levels + [flip(rows, "rep", 4, 2) for rows in parts]
     far_panels = flip(own_panels, "core", 2, 1)
@@ -420,6 +421,10 @@
 
     if FG == "a2a":
         vectors = lax.all_to_all(copies, "x", split_axis=0, concat_axis=0, tiled=True)
+    elif FG == "ring":
+        left, right = shift(solved, "x", 4, -1), shift(solved, "x", 4, 1)
+        over = jnp.concatenate([shift(left[:HALF], "x", 4, -1), shift(right[HALF:], "x", 4, 1)])
+        vectors = jnp.stack([solved, left, over, right])
     else:
         vectors = jnp.stack([solved] + [shift(solved, "x", 4, -k) for k in (1, 2, 3)])
     far_vectors = flip(vectors, "core", 2, 1)
@@ -436,7 +441,8 @@
         name="rhs_terms",
     )(jnp.stack([x, core]).astype(jnp.int32), vectors, far_vectors, target, got, *moved)
 
-    terms, solved = tie((terms, solved))
+    if FP == 'late':
+        terms, solved = tie((terms, solved))
     strips = solved.reshape(TILE, 4, strip)
     sent = flip(pick(strips, rep ^ 2, 1), "rep", 4, 2)
     kept = pick(strips, rep, 1)
@@ -444,13 +450,37 @@
     high = jnp.where(half == 0, sent, kept).reshape(2, HALF, strip)
     factors = jnp.stack([low, high], axis=1).reshape(2 * TILE, strip)
 
-    summed = lax.all_to_all(
-        terms.reshape(4, 8, strip, TILE), "y", split_axis=0, concat_axis=0, tiled=True
-    ).sum(axis=0)
-    summed, factors = tie((summed, factors))
-    pieces = lax.all_to_all(
-        summed, ("zh", "rep"), split_axis=0, concat_axis=0, tiled=True
-    )
+    if TAIL == "one":
+        pieces = lax.all_to_all(
+            terms.reshape(32, strip, TILE),
+            ("y", "zh", "rep"),
+            split_axis=0,
+            concat_axis=0,
+            tiled=True,
+        )
+        pieces = pieces.reshape(4, 8, strip, TILE).sum(axis=0)
+    else:
+        if TAIL == "two":
+            pair = terms.reshape(4, 8, strip, TILE)
+            inside = y // 2 == parity
+            mine = jnp.where(inside, 1 - y % 2, y % 2)
+            kept_terms = pick(pair, 1 - mine)
+            kept_terms = kept_terms + flip(pick(pair, mine), "y", 4, 1)
+            pairs = [
+                (s * 4 + r, (3 - s) * 4 + r)
+                for s in range(4)
+                for r in range(4)
+                if s // 2 != r % 2
+            ]
+            summed = kept_terms + lax.ppermute(kept_terms, ("y", "rep"), pairs)
+        else:
+            summed = lax.all_to_all(
+                terms.reshape(4, 8, strip, TILE), "y", split_axis=0, concat_axis=0, tiled=True
+            ).sum(axis=0)
+        summed, factors = tie((summed, factors))
+        pieces = lax.all_to_all(
+            summed, ("zh", "rep"), split_axis=0, concat_axis=0, tiled=True
+        )
     chosen = pick(pieces.reshape(2, 2, 2, strip, TILE), y // 2, 2)
     scale = (2 * 64 * TILE) ** -0.5
     item_rhs = jnp.sum(chosen, axis=(0, 1)).T * (scale * STEP)

time: 173 us -> 168 us (0.971)
  starting transfers between devices: 37.8 us -> 31.9 us
    all_to_all x2, waiting for transfers between devices: 12.5 us -> 22 us  [everyone(): return lax.all_to_all(copies, axis, split_axis=0, concat_axis=0, tiled=True)]
    ppermute x13 -> x11, waiting for transfers between devices: 34.6 us -> 27.2 us  [flip(): return lax.ppermute(value, axis, [(i, i ^ bit) for i in range(size)])]
    all_to_all x1, starting transfers between devices: 5.57 us -> 3.61 us  [per_device(): lax.all_to_all(summed, ('zh', 'rep'), split_axis=0, concat_axis=0, tiled=...]
    all_to_all x2, starting transfers between devices: 12.9 us -> 11.1 us  [everyone(): return lax.all_to_all(copies, axis, split_axis=0, concat_axis=0, tiled=True)]
    ppermute x13 -> x11, starting transfers between devices: 5.5 us -> 4.62 us  [flip(): return lax.ppermute(value, axis, [(i, i ^ bit) for i in range(size)])]
  transfers between devices with their start and end apart: 23 -> 21, of which waited for: 16 -> 16; matrix products, arithmetic and copies ran while one was open for 3% -> 3% of each run, Pallas kernels for 7% -> 7%
where the time goes in v4:
time: 168 us; the launch traced here: 167 us
  waiting for transfers between devices  93 us (55%)
  starting transfers between devices  31.9 us (19%)
  Pallas kernels  18 us (11%)
  blocking collectives  12.9 us (8%)
  local copies, waits for them, and re-layouts  7.53 us (4%)
  other arithmetic  2.54 us (2%)
    ppermute x11, waiting for transfers between devices, flip(): return lax.ppermute(value, axis, [(i, i ^ bit) for i in range(size)])  27.2 us
    ppermute x6, waiting for transfers between devices, shift(): lax.ppermute(value, axis, [(i, (i + by) % size) for i in range(size)])  23.5 us
    all_to_all x2, waiting for transfers between devices, everyone(): return lax.all_to_all(copies, axis, split_axis=0, concat_axis=0, tiled=True)  22 us
    all_to_all x1, blocking collectives, per_device(): lax.all_to_all(copies, 'x', split_axis=0, concat_axis=0, tiled=True)  12.9 us
    all_to_all x2, starting transfers between devices, everyone(): return lax.all_to_all(copies, axis, split_axis=0, concat_axis=0, tiled=True)  11.1 us
    all_to_all x1, waiting for transfers between devices, per_device(): lax.all_to_all(summed, ('zh', 'rep'), split_axis=0, concat_axis=0, tiled=...  11 us
    all_to_all x1, waiting for transfers between devices, per_device(): lax.all_to_all(terms.reshape(4, 8, strip, TILE), 'y', split_axis=0, conca...  9.19 us
    ppermute x6, starting transfers between devices, shift(): lax.ppermute(value, axis, [(i, (i + by) % size) for i in range(size)])  8.65 us
  transfers between devices with their start and end apart: 21, of which 16 were waited for; matrix products, arithmetic and copies ran while one was open for 3% of the time, Pallas kernels for 7%

profile of v4, /device:TPU:6, one launch (start us, length us, event | category | flops | bytes accessed | tf_op | source)
XLA Modules:
  0.0 166.8 jit_solution(11153308406022951921)
XLA Ops:
  2.5 3.4 %collective-permute-start = (f32[72,128]{1,0:T(8,128)S(1)}, f32[72,128]{1,0:T(8,128)S(1)}, u32[]{:S(2)}, u32[]{:S(2)}) collective-permute-start(f32[72,128]{1,0:T(8,128)S(1)} %select_maximum_fusion), channel_id=1, source_target_pairs={{0,2},{1,3},{2,0},{3,1},{4,6},{5,7},{6,4},{7,5},{8,10},{9,11},{10,... | collective-permute-start | bytes 110600 | tf_op jit(solution)/shard_map/ppermute | solution.py:281
  5.9 1.5 broadcast_in_dim.4
  7.3 6.7 %all-to-all-start = ((f32[8,64,128]{2,1,0:T(8,128)}), f32[8,64,128]{2,1,0:T(8,128)S(1)}, u32[]{:S(2)}, u32[]{:S(2)}) async-start(f32[8,64,128]{2,1,0:T(8,128)} %broadcast_in_dim.4), calls=%async_computation | async-start | bytes 524288 | tf_op jit(solution)/shard_map/all_to_all | solution.py:302
  14.0 1.3 dynamic-slice_bitcast_fusion
  15.3 1.0 slice.40
  16.5 9.1 %all-to-all-done = f32[8,64,128]{2,1,0:T(8,128)S(1)} async-done(((f32[8,64,128]{2,1,0:T(8,128)}), f32[8,64,128]{2,1,0:T(8,128)S(1)}, u32[]{:S(2)}, u32[]{:S(2)}) %all-to-all-start) | async-done | bytes 262176 | tf_op jit(solution)/shard_map/all_to_all | solution.py:302
  25.6 1.0 broadcast_in_dim.5
  26.7 4.5 %all-to-all-start.1 = ((f32[4,2,256,128]{3,2,1,0:T(8,128)}), f32[4,2,256,128]{3,2,1,0:T(8,128)S(1)}, u32[]{:S(2)}, u32[]{:S(2)}) async-start(f32[4,2,256,128]{3,2,1,0:T(8,128)} %broadcast_in_dim.5), calls=%async_computation.1 | async-start | bytes 2097152 | tf_op jit(solution)/shard_map/all_to_all | solution.py:302
  31.3 12.9 %all-to-all-done.1 = f32[4,2,256,128]{3,2,1,0:T(8,128)S(1)} async-done(((f32[4,2,256,128]{3,2,1,0:T(8,128)}), f32[4,2,256,128]{3,2,1,0:T(8,128)S(1)}, u32[]{:S(2)}, u32[]{:S(2)}) %all-to-all-start.1) | async-done | bytes 1048608 | tf_op jit(solution)/shard_map/all_to_all | solution.py:302
  45.1 1.1 collective-permute-start.2
  46.2 2.1 %collective-permute-start.1 = (f32[4,256,128]{2,1,0:T(8,128)S(1)}, f32[4,256,128]{2,1,0:T(8,128)S(1)}, u32[]{:S(2)}, u32[]{:S(2)}) collective-permute-start(f32[4,256,128]{2,1,0:T(8,128)S(1)} %bitcast.55), channel_id=1, source_target_pairs={{0,8},{8,16},{16,24},{24,0},{1,9},{9,17},{17,25},{25,1},{2,10},{10... | collective-permute-start | bytes 1572872 | tf_op jit(solution)/shard_map/ppermute | solution.py:277
  48.3 18.5 %collective-permute-done.3 = f32[4,256,128]{2,1,0:T(8,128)S(1)} collective-permute-done((f32[4,256,128]{2,1,0:T(8,128)S(1)}, f32[4,256,128]{2,1,0:T(8,128)S(1)}, u32[]{:S(2)}, u32[]{:S(2)}) %collective-permute-start.3) | collective-permute-done | bytes 524320 | tf_op jit(solution)/shard_map/ppermute | solution.py:277
  67.6 3.9 %collective-permute-done.4 = f32[2,64,128]{2,1,0:T(8,128)S(1)} collective-permute-done((f32[2,64,128]{2,1,0:T(8,128)S(1)}, f32[2,64,128]{2,1,0:T(8,128)S(1)}, u32[]{:S(2)}, u32[]{:S(2)}) %collective-permute-start.4) | collective-permute-done | bytes 65568 | tf_op jit(solution)/shard_map/ppermute | solution.py:281
  71.7 4.1 %collective-permute-done.6.far = f32[4,4,256,128]{3,2,1,0:T(8,128)} collective-permute-done((f32[4,4,256,128]{3,2,1,0:T(8,128)S(1)}, f32[4,4,256,128]{3,2,1,0:T(8,128)}, u32[]{:S(2)}, u32[]{:S(2)}) %collective-permute-start.6) | collective-permute-done | bytes 2097184 | tf_op jit(solution)/shard_map/ppermute | solution.py:281
  75.8 3.7 %first_scores.1 = (bf16[4,256,512]{2,1,0:T(8,128)(2,1)S(1)}, bf16[4,256,512]{2,1,0:T(8,128)(2,1)S(1)}, bf16[4,256,512]{2,1,0:T(8,128)(2,1)S(1)}, bf16[4,256,512]...) custom-call(f32[256,128]{1,0:T(8,128)S(1)} %bitcast.52, ...), custom_call_target="tpu_custom_call" | custom-call | flops 805306368 | bytes 10485760 | tf_op jit(solution)/shard_map/first_scores/pallas_call | solution.py:216
  80.1 4.0 %first_apply.1 = (bf16[4,128,512]{2,1,0:T(8,128)(2,1)S(1)}, bf16[4,128,512]{2,1,0:T(8,128)(2,1)S(1)}, f32[4,128,512]{2,1,0:T(8,128)S(1)}, f32[4,128,512]{2,1,0:T(8,128)S(1)}, f32[128,256]{1,0:T(8,128)S(1)}) custom-call(s32[67]{0:T(128)S(1)} %concatenate.9.scal, f32[4,128,512]{2,1,0:T(8,128)S(1)} %get-tuple-element.68.refs_0_, ...), custom_call_target="tpu_custom_call" | custom-call | flops 805306368 | bytes 12582912 | tf_op jit(solution)/shard_map/first_apply/pallas_call | solution.py:244
  84.4 2.5 %collective-permute-done.11.got = f32[4,128,512]{2,1,0:T(8,128)S(1)} collective-permute-done((f32[4,128,512]{2,1,0:T(8,128)S(1)}, f32[4,128,512]{2,1,0:T(8,128)S(1)}, u32[]{:S(2)}, u32[]{:S(2)}) %collective-permute-start.11) | collective-permute-done | bytes 1048608 | tf_op jit(solution)/shard_map/ppermute | solution.py:281
  87.2 2.1 %collective-permute-start.13 = (f32[2,128,512]{2,1,0:T(8,128)S(1)}, f32[2,128,512]{2,1,0:T(8,128)S(1)}, u32[]{:S(2)}, u32[]{:S(2)}) collective-permute-start(f32[2,128,512]{2,1,0:T(8,128)S(1)} %pad_maximum_fusion.2), channel_id=1, source_target_pairs={{0,16},{8,24},{16,0},{24,8},{1,17},{9,25},{17,1},{25,9},{2,18},{10... | collective-permute-start | bytes 1572872 | tf_op jit(solution)/shard_map/ppermute | solution.py:277
  89.4 2.2 %collective-permute-start.14 = (f32[2,128,512]{2,1,0:T(8,128)S(1)}, f32[2,128,512]{2,1,0:T(8,128)S(1)}, u32[]{:S(2)}, u32[]{:S(2)}) collective-permute-start(f32[2,128,512]{2,1,0:T(8,128)S(1)} %pad_maximum_fusion.3), channel_id=1, source_target_pairs={{0,8},{8,16},{16,24},{24,0},{1,9},{9,17},{17,25},{25,1},{2,10},{10... | collective-permute-start | bytes 1572872 | tf_op jit(solution)/shard_map/ppermute | solution.py:277
  91.6 3.8 %second_apply.1 = (f32[128,256]{1,0:T(8,128)S(1)}, f32[128,256]{1,0:T(8,128)S(1)}) custom-call(f32[128,256]{1,0:T(8,128)S(1)} %get-tuple-element.76.pa, f32[128,256]{1,0:T(8,128)S(1)} %collective-permute-done.8.pb, f32[128,256]{1,0:T(8,128)S(1)} %get-tuple-element.77.x0, bf16[4,256,512]{2,1,0:T(8,128)(2,1)S(1)} %get-tuple-element.70.refs_2_.refs_0_, ...), custom_call_target="tpu_custom_call" | custom-call | flops 1610612736 | bytes 6291456 | tf_op jit(solution)/shard_map/second_apply/pallas_call | solution.py:263
  95.7 5.0 %collective-permute-done.9.pb = f32[128,256]{1,0:T(8,128)S(1)} collective-permute-done((f32[128,256]{1,0:T(8,128)S(1)}, f32[128,256]{1,0:T(8,128)S(1)}, u32[]{:S(2)}, u32[]{:S(2)}) %collective-permute-start.9) | collective-permute-done | bytes 131104 | tf_op jit(solution)/shard_map/ppermute | solution.py:281
  100.6 4.0 %third_apply.1 = (f32[128,256]{1,0:T(8,128)S(1)}, f32[128,256]{1,0:T(8,128)S(1)}, f32[128,256]{1,0:T(8,128)S(1)}, f32[128,256]{1,0:T(8,128)S(1)}) custom-call(f32[128,256]{1,0:T(8,128)S(1)} %get-tuple-element.80.pa, f32[128,256]{1,0:T(8,128)S(1)} %collective-permute-done.9.pb, f32[128,256]{1,0:T(8,128)S(1)} %get-tuple-element.81.resid, ...), custom_call_target="tpu_custom_call" | custom-call | flops 1610612736 | bytes 6291456 | tf_op jit(solution)/shard_map/third_apply/pallas_call | solution.py:263
  104.8 4.9 %collective-permute-done.10.pb = f32[128,256]{1,0:T(8,128)S(1)} collective-permute-done((f32[128,256]{1,0:T(8,128)S(1)}, f32[128,256]{1,0:T(8,128)S(1)}, u32[]{:S(2)}, u32[]{:S(2)}) %collective-permute-start.10) | collective-permute-done | bytes 131104 | tf_op jit(solution)/shard_map/ppermute | solution.py:281
  109.7 3.7 %collective-permute-done.12.t1 = f32[2,128,512]{2,1,0:T(8,128)S(1)} collective-permute-done((f32[2,128,512]{2,1,0:T(8,128)S(1)}, f32[2,128,512]{2,1,0:T(8,128)S(1)}, u32[]{:S(2)}, u32[]{:S(2)}) %collective-permute-start.12) | collective-permute-done | bytes 524320 | tf_op jit(solution)/shard_map/ppermute | solution.py:277
  114.3 12.9 %all_to_all.25.own_vectors = f32[4,128,256]{2,1,0:T(8,128)S(1)} all-to-all(f32[4,128,256]{2,1,0:T(8,128)S(1)} %get-tuple-element.89), channel_id=1, replica_groups=mesh['y'=4,'zh'=2,'x'=4,'core'=2,'rep'=4] {'x'}, dimensions={0} | all-to-all | bytes 1048576 | tf_op jit(solution)/shard_map/all_to_all | solution.py:423
  127.3 1.8 %collective-permute-done.15.far_vectors = f32[4,128,256]{2,1,0:T(8,128)S(1)} collective-permute-done((f32[4,128,256]{2,1,0:T(8,128)S(1)}, f32[4,128,256]{2,1,0:T(8,128)S(1)}, u32[]{:S(2)}, u32[]{:S(2)}) %collective-permute-start.15) | collective-permute-done | bytes 524320 | tf_op jit(solution)/shard_map/ppermute | solution.py:281
  129.1 2.3 %rhs_terms.1 = f32[2,4,256,128]{3,2,1,0:T(8,128)} custom-call(s32[2]{0:T(128)S(1)} %pad_add_fusion.scal, f32[4,128,256]{2,1,0:T(8,128)S(1)} %all_to_all.25.own_vectors, f32[4,128,256]{2,1,0:T(8,128)S(1)} %collective-permute-done.15.far_vectors, f32[4,128,512]{2,1,0:T(8,128)S(1)} %get-tuple-element.83.own, f32[4,128,512]{2,1,0:T(8,128)S(1)} %collective-permute-done.11.got, ...), custom_call_target="tpu_custom_call" | custom-call | flops 536870912 | bytes 4194304 | tf_op jit(solution)/shard_map/rhs_terms/pallas_call | solution.py:434
  131.4 3.9 %all-to-all-start.3 = ((f32[4,8,64,128]{3,2,1,0:T(8,128)}), f32[4,8,64,128]{3,2,1,0:T(8,128)S(1)}, u32[]{:S(2)}, u32[]{:S(2)}) async-start(f32[4,8,64,128]{3,2,1,0:T(8,128)} %bitcast.23), calls=%async_computation.3 | async-start | bytes 2097152 | tf_op jit(solution)/shard_map/all_to_all | solution.py:477
  135.9 4.4 %collective-permute-done.16 = f32[128,64]{0,1:T(8,128)S(1)} collective-permute-done((f32[128,64]{0,1:T(8,128)S(1)}, f32[128,64]{0,1:T(8,128)S(1)}, u32[]{:S(2)}, u32[]{:S(2)}) %collective-permute-start.16) | collective-permute-done | bytes 32800 | tf_op jit(solution)/shard_map/ppermute | solution.py:281
  141.5 9.2 %all-to-all-done.3 = f32[4,8,64,128]{3,2,1,0:T(8,128)S(1)} async-done(((f32[4,8,64,128]{3,2,1,0:T(8,128)}), f32[4,8,64,128]{3,2,1,0:T(8,128)S(1)}, u32[]{:S(2)}, u32[]{:S(2)}) %all-to-all-start.3) | async-done | bytes 1048608 | tf_op jit(solution)/shard_map/all_to_all | solution.py:477
  151.5 3.6 %all-to-all-start.4 = ((f32[8,64,128]{2,1,0:T(8,128)}), f32[8,64,128]{2,1,0:T(8,128)S(1)}, u32[]{:S(2)}, u32[]{:S(2)}) async-start(f32[8,64,128]{2,1,0:T(8,128)} %reduce_sum.18), calls=%async_computation.4 | async-start | bytes 524288 | tf_op jit(solution)/shard_map/all_to_all | solution.py:481
  155.1 11.0 %all-to-all-done.4 = f32[8,64,128]{2,1,0:T(8,128)S(1)} async-done(((f32[8,64,128]{2,1,0:T(8,128)}), f32[8,64,128]{2,1,0:T(8,128)S(1)}, u32[]{:S(2)}, u32[]{:S(2)}) %all-to-all-start.4) | async-done | bytes 262176 | tf_op jit(solution)/shard_map/all_to_all | solution.py:481
  (58 shorter events, 9.8 us)
Async XLA Ops:
  2.5 13.9 %collective-permute-start = (f32[72,128]{1,0:T(8,128)S(1)}, f32[72,128]{1,0:T(8,128)S(1)}, u32[]{:S(2)}, u32[]{:S(2)}) collective-permute-start(f32[72,128]{1,0:T(8,128)S(1)} %select_maximum_fusion), channel_id=1, source_target_pairs={{0,2},{1,3},{2,0},{3,1},{4,6},{5,7},{6,4},{7,5},{8,10},{9,11},{10,... | collective-permute-start | bytes 110600 | tf_op jit(solution)/shard_map/ppermute | solution.py:281
  7.3 18.3 %all-to-all-start = ((f32[8,64,128]{2,1,0:T(8,128)}), f32[8,64,128]{2,1,0:T(8,128)S(1)}, u32[]{:S(2)}, u32[]{:S(2)}) async-start(f32[8,64,128]{2,1,0:T(8,128)} %broadcast_in_dim.4), calls=%async_computation | async-start | bytes 524288 | tf_op jit(solution)/shard_map/all_to_all | solution.py:302
  26.7 17.5 %all-to-all-start.1 = ((f32[4,2,256,128]{3,2,1,0:T(8,128)}), f32[4,2,256,128]{3,2,1,0:T(8,128)S(1)}, u32[]{:S(2)}, u32[]{:S(2)}) async-start(f32[4,2,256,128]{3,2,1,0:T(8,128)} %broadcast_in_dim.5), calls=%async_computation.1 | async-start | bytes 2097152 | tf_op jit(solution)/shard_map/all_to_all | solution.py:302
  31.1 40.4 %collective-permute-start.5 = (s32[32,56,128]{2,1,0:T(8,128)}, s32[32,56,128]{2,1,0:T(8,128)S(1)}, u32[]{:S(2)}, u32[]{:S(2)}) collective-permute-start(s32[32,56,128]{2,1,0:T(8,128)} %slice.40), channel_id=1, source_target_pairs={{0,2},{1,3},{2,0},{3,1},{4,6},{5,7},{6,4},{7,5},{8,10},{9,11},{10,... | collective-permute-start | bytes 2752520 | tf_op jit(solution)/shard_map/ppermute | solution.py:281
  44.2 22.6 %collective-permute-start.3 = (f32[4,256,128]{2,1,0:T(8,128)S(1)}, f32[4,256,128]{2,1,0:T(8,128)S(1)}, u32[]{:S(2)}, u32[]{:S(2)}) collective-permute-start(f32[4,256,128]{2,1,0:T(8,128)S(1)} %bitcast.53), channel_id=1, source_target_pairs={{0,24},{8,0},{16,8},{24,16},{1,25},{9,1},{17,9},{25,17},{2,26},{10... | collective-permute-start | bytes 1572872 | tf_op jit(solution)/shard_map/ppermute | solution.py:277
  45.1 21.7 %collective-permute-start.2 = (f32[4,256,128]{2,1,0:T(8,128)S(1)}, f32[4,256,128]{2,1,0:T(8,128)S(1)}, u32[]{:S(2)}, u32[]{:S(2)}) collective-permute-start(f32[4,256,128]{2,1,0:T(8,128)S(1)} %bitcast.54), channel_id=1, source_target_pairs={{0,16},{8,24},{16,0},{24,8},{1,17},{9,25},{17,1},{25,9},{2,18},{10... | collective-permute-start | bytes 1572872 | tf_op jit(solution)/shard_map/ppermute | solution.py:277
  46.2 21.2 %collective-permute-start.1 = (f32[4,256,128]{2,1,0:T(8,128)S(1)}, f32[4,256,128]{2,1,0:T(8,128)S(1)}, u32[]{:S(2)}, u32[]{:S(2)}) collective-permute-start(f32[4,256,128]{2,1,0:T(8,128)S(1)} %bitcast.55), channel_id=1, source_target_pairs={{0,8},{8,16},{16,24},{24,0},{1,9},{9,17},{17,25},{25,1},{2,10},{10... | collective-permute-start | bytes 1572872 | tf_op jit(solution)/shard_map/ppermute | solution.py:277
  48.3 23.2 %collective-permute-start.4 = (f32[2,64,128]{2,1,0:T(8,128)S(1)}, f32[2,64,128]{2,1,0:T(8,128)S(1)}, u32[]{:S(2)}, u32[]{:S(2)}) collective-permute-start(f32[2,64,128]{2,1,0:T(8,128)S(1)} %pad_maximum_fusion.6), channel_id=1, source_target_pairs={{0,1},{1,0},{2,3},{3,2},{4,5},{5,4},{6,7},{7,6},{8,9},{9,8},{10,11... | collective-permute-start | bytes 196616 | tf_op jit(solution)/shard_map/ppermute | solution.py:281
  67.4 4.1 %copy-start.1 = (s32[1,32]{1,0:T(1,128)S(1)}, s32[1,32]{1,0:T(1,128)}, u32[]{:S(2)}) copy-start(s32[1,32]{1,0:T(1,128)} %param.8) | copy-start | bytes 388
  71.5 4.3 %collective-permute-start.6 = (f32[4,4,256,128]{3,2,1,0:T(8,128)S(1)}, f32[4,4,256,128]{3,2,1,0:T(8,128)}, u32[]{:S(2)}, u32[]{:S(2)}) collective-permute-start(f32[4,4,256,128]{3,2,1,0:T(8,128)S(1)} %pad_maximum_fusion.own), channel_id=1, source_target_pairs={{0,4},{4,0},{1,5},{5,1},{2,6},{6,2},{3,7},{7,3},{8,12},{12,8},{9,1... | collective-permute-start | bytes 6291464 | tf_op jit(solution)/shard_map/ppermute | solution.py:281
  71.5 8.6 %collective-permute-start.7 = (s32[32,8,128]{2,1,0:T(8,128)S(1)}, s32[32,8,128]{2,1,0:T(8,128)S(1)}, u32[]{:S(2)}, u32[]{:S(2)}) collective-permute-start(s32[32,8,128]{2,1,0:T(8,128)S(1)} %slice.41), channel_id=1, source_target_pairs={{0,2},{1,3},{2,0},{3,1},{4,6},{5,7},{6,4},{7,5},{8,10},{9,11},{10,... | collective-permute-start | bytes 393224 | tf_op jit(solution)/shard_map/ppermute | solution.py:281
  75.8 4.3 %copy-start = (s32[1,32,128,128]{3,2,1,0:T(8,128)S(1)}, s32[1,32,128,128]{3,2,1,0:T(8,128)}, u32[]{:S(2)}) copy-start(s32[1,32,128,128]{3,2,1,0:T(8,128)} %param.9) | copy-start | bytes 6291460
  84.1 2.7 %collective-permute-start.11 = (f32[4,128,512]{2,1,0:T(8,128)S(1)}, f32[4,128,512]{2,1,0:T(8,128)S(1)}, u32[]{:S(2)}, u32[]{:S(2)}) collective-permute-start(f32[4,128,512]{2,1,0:T(8,128)S(1)} %get-tuple-element.84), channel_id=1, source_target_pairs={{0,4},{4,0},{1,5},{5,1},{2,6},{6,2},{3,7},{7,3},{8,12},{12,8},{9,1... | collective-permute-start | bytes 3145736 | tf_op jit(solution)/shard_map/ppermute | solution.py:281
  84.3 7.3 %collective-permute-start.8 = (f32[128,256]{1,0:T(8,128)S(1)}, f32[128,256]{1,0:T(8,128)S(1)}, u32[]{:S(2)}, u32[]{:S(2)}) collective-permute-start(f32[128,256]{1,0:T(8,128)S(1)} %get-tuple-element.76.pa), channel_id=1, source_target_pairs={{0,1},{1,0},{2,3},{3,2},{4,5},{5,4},{6,7},{7,6},{8,9},{9,8},{10,11... | collective-permute-start | bytes 393224 | tf_op jit(solution)/shard_map/ppermute | solution.py:281
  86.9 26.5 %collective-permute-start.12 = (f32[2,128,512]{2,1,0:T(8,128)S(1)}, f32[2,128,512]{2,1,0:T(8,128)S(1)}, u32[]{:S(2)}, u32[]{:S(2)}) collective-permute-start(f32[2,128,512]{2,1,0:T(8,128)S(1)} %pad_maximum_fusion.1), channel_id=1, source_target_pairs={{0,24},{8,0},{16,8},{24,16},{1,25},{9,1},{17,9},{25,17},{2,26},{10... | collective-permute-start | bytes 1572872 | tf_op jit(solution)/shard_map/ppermute | solution.py:277
  87.2 26.2 %collective-permute-start.13 = (f32[2,128,512]{2,1,0:T(8,128)S(1)}, f32[2,128,512]{2,1,0:T(8,128)S(1)}, u32[]{:S(2)}, u32[]{:S(2)}) collective-permute-start(f32[2,128,512]{2,1,0:T(8,128)S(1)} %pad_maximum_fusion.2), channel_id=1, source_target_pairs={{0,16},{8,24},{16,0},{24,8},{1,17},{9,25},{17,1},{25,9},{2,18},{10... | collective-permute-start | bytes 1572872 | tf_op jit(solution)/shard_map/ppermute | solution.py:277
  89.4 24.8 %collective-permute-start.14 = (f32[2,128,512]{2,1,0:T(8,128)S(1)}, f32[2,128,512]{2,1,0:T(8,128)S(1)}, u32[]{:S(2)}, u32[]{:S(2)}) collective-permute-start(f32[2,128,512]{2,1,0:T(8,128)S(1)} %pad_maximum_fusion.3), channel_id=1, source_target_pairs={{0,8},{8,16},{16,24},{24,0},{1,9},{9,17},{17,25},{25,1},{2,10},{10... | collective-permute-start | bytes 1572872 | tf_op jit(solution)/shard_map/ppermute | solution.py:277
  95.4 5.2 %collective-permute-start.9 = (f32[128,256]{1,0:T(8,128)S(1)}, f32[128,256]{1,0:T(8,128)S(1)}, u32[]{:S(2)}, u32[]{:S(2)}) collective-permute-start(f32[128,256]{1,0:T(8,128)S(1)} %get-tuple-element.80.pa), channel_id=1, source_target_pairs={{0,1},{1,0},{2,3},{3,2},{4,5},{5,4},{6,7},{7,6},{8,9},{9,8},{10,11... | collective-permute-start | bytes 393224 | tf_op jit(solution)/shard_map/ppermute | solution.py:281
  104.7 5.1 %collective-permute-start.10 = (f32[128,256]{1,0:T(8,128)S(1)}, f32[128,256]{1,0:T(8,128)S(1)}, u32[]{:S(2)}, u32[]{:S(2)}) collective-permute-start(f32[128,256]{1,0:T(8,128)S(1)} %get-tuple-element.82.pa), channel_id=1, source_target_pairs={{0,1},{1,0},{2,3},{3,2},{4,5},{5,4},{6,7},{7,6},{8,9},{9,8},{10,11... | collective-permute-start | bytes 393224 | tf_op jit(solution)/shard_map/ppermute | solution.py:281
  127.2 1.9 %collective-permute-start.15 = (f32[4,128,256]{2,1,0:T(8,128)S(1)}, f32[4,128,256]{2,1,0:T(8,128)S(1)}, u32[]{:S(2)}, u32[]{:S(2)}) collective-permute-start(f32[4,128,256]{2,1,0:T(8,128)S(1)} %all_to_all.25.own_vectors), channel_id=1, source_target_pairs={{0,4},{4,0},{1,5},{5,1},{2,6},{6,2},{3,7},{7,3},{8,12},{12,8},{9,1... | collective-permute-start | bytes 1572872 | tf_op jit(solution)/shard_map/ppermute | solution.py:281
  131.4 19.3 %all-to-all-start.3 = ((f32[4,8,64,128]{3,2,1,0:T(8,128)}), f32[4,8,64,128]{3,2,1,0:T(8,128)S(1)}, u32[]{:S(2)}, u32[]{:S(2)}) async-start(f32[4,8,64,128]{3,2,1,0:T(8,128)} %bitcast.23), calls=%async_computation.3 | async-start | bytes 2097152 | tf_op jit(solution)/shard_map/all_to_all | solution.py:477
  135.4 4.9 %collective-permute-start.16 = (f32[128,64]{0,1:T(8,128)S(1)}, f32[128,64]{0,1:T(8,128)S(1)}, u32[]{:S(2)}, u32[]{:S(2)}) collective-permute-start(f32[128,64]{0,1:T(8,128)S(1)} %dynamic-slice_bitcast_fusion.1), channel_id=1, source_target_pairs={{0,2},{1,3},{2,0},{3,1},{4,6},{5,7},{6,4},{7,5},{8,10},{9,11},{10,... | collective-permute-start | bytes 98312 | tf_op jit(solution)/shard_map/ppermute | solution.py:281
  151.5 14.6 %all-to-all-start.4 = ((f32[8,64,128]{2,1,0:T(8,128)}), f32[8,64,128]{2,1,0:T(8,128)S(1)}, u32[]{:S(2)}, u32[]{:S(2)}) async-start(f32[8,64,128]{2,1,0:T(8,128)} %reduce_sum.18), calls=%async_computation.4 | async-start | bytes 524288 | tf_op jit(solution)/shard_map/all_to_all | solution.py:481

commit v5 on v4

--- a/solution.py
+++ b/solution.py
@@ -152,26 +152,23 @@
     apply_step(shared, part, stacked)
 
 
-def last_kernel(pa, pb, resid, direc, x1, out, copies):
+def last_kernel(pa, pb, resid, direc, x1, out):
     image = pa[...] + pb[...] + RIDGE * direc[...]
     rho = jnp.sum(resid[...] * resid[...], axis=1, keepdims=True)
     alpha = rho / jnp.sum(direc[...] * image, axis=1, keepdims=True)
-    solved = x1[...] + alpha * direc[...]
-    out[...] = solved
+    out[...] = x1[...] + alpha * direc[...]
+
+
+def rhs_kernel(own_vectors, far_vectors, own, got, t1, t2, t3, out, total):
     for k in range(4):
-        copies[k] = solved
-
-
-def rhs_kernel(scal, own_vectors, far_vectors, own, got, t1, t2, t3, out, total):
-    x = scal[0]
-    for k in range(4):
-        source = lax.rem(x + k, 4) if FG == "a2a" else k
         for slot in range(2):
-            chunk = (own_vectors, far_vectors)[slot][source]
-            if k == 0:
-                tile = (own, got)[slot][0 if REL else x]
+            chunk = (own_vectors, far_vectors)[slot][k]
+            if slot == 1:
+                tile = got[k]
+            elif k == 0:
+                tile = own[0]
             else:
-                tile = (t1, t2, t3)[k - 1][slot]
+                tile = (t1, t2, t3)[k - 1][0]
             tile = tile.astype(bf16)
             high, low = split(chunk.T)
             both = jnp.concatenate([high, low], axis=1)
@@ -286,15 +283,14 @@
 
 
 VMEM = 16777216
-FG = 'a2a'
-XS = 'perm'
-YS = 'a2a'
 REL = 1
 FP = 'early'
 TAIL = 'a2a'
 XC = 0
 NP = 'y'
+XS = 'perm'
 CHUNKS = (56,8)
+YS = 'a2a'
 
 
 def everyone(value, axis, size):
@@ -398,11 +394,7 @@
     shared = (*panels, *weights)
     part_b = flip(part, "rep", 4, 1)
 
-    got = flip(far_target, "core", 2, 1)
-    moved = []
-    for k in (1, 2, 3):
-        to = k if REL else (x - k) % 4
-        moved.append(shift(jnp.stack([pick(target, to), pick(got, to)]), "x", 4, -k))
+    moved = [shift(jnp.stack([target[k], far_target[k]]), "x", 4, -k) for k in (1, 2, 3)]
 
     resid, part = next_apply(second_kernel, (part, part_b, x0), shared, 2, "second_apply")
     part_b = flip(part, "rep", 4, 1)
@@ -411,35 +403,28 @@
     )
     part_b = flip(part, "rep", 4, 1)
     part_b, moved = tie((part_b, moved))
-    solved, copies = pl.pallas_call(
+    got = flip(jnp.stack([far_target[0]] + [v[1] for v in moved]), "core", 2, 1)
+    solved = pl.pallas_call(
         last_kernel,
-        out_shape=[shaped(TILE, RANK), shaped(4, TILE, RANK)],
+        out_shape=shaped(TILE, RANK),
         compiler_params=params(),
-        cost_estimate=cost(TILE * RANK * 10, 10 * TILE * RANK * 4),
+        cost_estimate=cost(TILE * RANK * 10, 6 * TILE * RANK * 4),
         name="last_update",
     )(part, part_b, resid1, direc1, x1)
 
-    if FG == "a2a":
-        vectors = lax.all_to_all(copies, "x", split_axis=0, concat_axis=0, tiled=True)
-    elif FG == "ring":
-        left, right = shift(solved, "x", 4, -1), shift(solved, "x", 4, 1)
-        over = jnp.concatenate([shift(left[:HALF], "x", 4, -1), shift(right[HALF:], "x", 4, 1)])
-        vectors = jnp.stack([solved, left, over, right])
-    else:
-        vectors = jnp.stack([solved] + [shift(solved, "x", 4, -k) for k in (1, 2, 3)])
+    vectors = jnp.stack([solved] + [shift(solved, "x", 4, -k) for k in (1, 2, 3)])
     far_vectors = flip(vectors, "core", 2, 1)
 
-    smem = pl.BlockSpec(memory_space=pltpu.SMEM)
     vmem = pl.BlockSpec(memory_space=pltpu.VMEM)
     terms = pl.pallas_call(
         rhs_kernel,
-        in_specs=[smem] + [vmem] * 7,
+        in_specs=[vmem] * 7,
         out_shape=shaped(2, 4, RANK, TILE),
         scratch_shapes=[pltpu.VMEM((RANK, WIDE), f32)],
         compiler_params=params(),
         cost_estimate=cost(4 * 1024 * RANK * WIDE, 4 << 20),
         name="rhs_terms",
-    )(jnp.stack([x, core]).astype(jnp.int32), vectors, far_vectors, target, got, *moved)
+    )(vectors, far_vectors, target, got, *moved)
 
     if FP == 'late':
         terms, solved = tie((terms, solved))

time: 168 us -> 164 us (0.976)
  blocking collectives: 12.9 us -> 0 us
  starting transfers between devices: 31.9 us -> 40.6 us
    all_to_all x1 -> x0, blocking collectives: 12.9 us -> none  [per_device(): lax.all_to_all(copies, 'x', split_axis=0, concat_axis=0, tiled=True)]
    ppermute x6 -> x9, waiting for transfers between devices: 23.5 us -> 31.7 us  [shift(): lax.ppermute(value, axis, [(i, (i + by) % size) for i in range(size)])]
    ppermute x11, waiting for transfers between devices: 27.2 us -> 20.8 us  [flip(): return lax.ppermute(value, axis, [(i, i ^ bit) for i in range(size)])]
    ppermute x11, starting transfers between devices: 4.62 us -> 9.65 us  [flip(): return lax.ppermute(value, axis, [(i, i ^ bit) for i in range(size)])]
    ppermute x6 -> x9, starting transfers between devices: 8.65 us -> 12.3 us  [shift(): lax.ppermute(value, axis, [(i, (i + by) % size) for i in range(size)])]
  transfers between devices with their start and end apart: 21 -> 24, of which waited for: 16 -> 19; matrix products, arithmetic and copies ran while one was open for 3% -> 4% of each run, Pallas kernels for 7% -> 7%
where the time goes in v5:
time: 164 us
  waiting for transfers between devices  94.4 us (58%)
  starting transfers between devices  40.6 us (25%)
  Pallas kernels  17.6 us (11%)
  local copies, waits for them, and re-layouts  7.64 us (5%)
  other arithmetic  2.57 us (2%)
    ppermute x9, waiting for transfers between devices, shift(): lax.ppermute(value, axis, [(i, (i + by) % size) for i in range(size)])  31.7 us
    all_to_all x2, waiting for transfers between devices, everyone(): return lax.all_to_all(copies, axis, split_axis=0, concat_axis=0, tiled=True)  22 us
    ppermute x11, waiting for transfers between devices, flip(): return lax.ppermute(value, axis, [(i, i ^ bit) for i in range(size)])  20.8 us
    ppermute x9, starting transfers between devices, shift(): lax.ppermute(value, axis, [(i, (i + by) % size) for i in range(size)])  12.3 us
    all_to_all x2, starting transfers between devices, everyone(): return lax.all_to_all(copies, axis, split_axis=0, concat_axis=0, tiled=True)  11.1 us
    all_to_all x1, waiting for transfers between devices, per_device(): lax.all_to_all(summed, ('zh', 'rep'), split_axis=0, concat_axis=0, tiled=...  11 us
    ppermute x11, starting transfers between devices, flip(): return lax.ppermute(value, axis, [(i, i ^ bit) for i in range(size)])  9.65 us
    all_to_all x1, waiting for transfers between devices, per_device(): lax.all_to_all(terms.reshape(4, 8, strip, TILE), 'y', split_axis=0, conca...  8.88 us
  transfers between devices with their start and end apart: 24, of which 19 were waited for; matrix products, arithmetic and copies ran while one was open for 4% of the time, Pallas kernels for 7%

profile of v5, /device:TPU:6, one launch (start us, length us, event | category | flops | bytes accessed | tf_op | source)
XLA Modules:
  0.0 163.8 jit_solution(3453253990160304181)
XLA Ops:
  2.5 3.4 %collective-permute-start = (f32[72,128]{1,0:T(8,128)S(1)}, f32[72,128]{1,0:T(8,128)S(1)}, u32[]{:S(2)}, u32[]{:S(2)}) collective-permute-start(f32[72,128]{1,0:T(8,128)S(1)} %select_maximum_fusion), channel_id=1, source_target_pairs={{0,2},{1,3},{2,0},{3,1},{4,6},{5,7},{6,4},{7,5},{8,10},{9,11},{10,... | collective-permute-start | bytes 110600 | tf_op jit(solution)/shard_map/ppermute | solution.py:278
  7.3 6.7 %all-to-all-start = ((f32[8,64,128]{2,1,0:T(8,128)}), f32[8,64,128]{2,1,0:T(8,128)S(1)}, u32[]{:S(2)}, u32[]{:S(2)}) async-start(f32[8,64,128]{2,1,0:T(8,128)} %broadcast_in_dim.4), calls=%async_computation | async-start | bytes 524288 | tf_op jit(solution)/shard_map/all_to_all | solution.py:298
  16.5 9.1 %all-to-all-done = f32[8,64,128]{2,1,0:T(8,128)S(1)} async-done(((f32[8,64,128]{2,1,0:T(8,128)}), f32[8,64,128]{2,1,0:T(8,128)S(1)}, u32[]{:S(2)}, u32[]{:S(2)}) %all-to-all-start) | async-done | bytes 262176 | tf_op jit(solution)/shard_map/all_to_all | solution.py:298
  26.6 4.5 %all-to-all-start.1 = ((f32[4,2,256,128]{3,2,1,0:T(8,128)}), f32[4,2,256,128]{3,2,1,0:T(8,128)S(1)}, u32[]{:S(2)}, u32[]{:S(2)}) async-start(f32[4,2,256,128]{3,2,1,0:T(8,128)} %broadcast_in_dim.5), calls=%async_computation.1 | async-start | bytes 2097152 | tf_op jit(solution)/shard_map/all_to_all | solution.py:298
  31.3 12.9 %all-to-all-done.1 = f32[4,2,256,128]{3,2,1,0:T(8,128)S(1)} async-done(((f32[4,2,256,128]{3,2,1,0:T(8,128)}), f32[4,2,256,128]{3,2,1,0:T(8,128)S(1)}, u32[]{:S(2)}, u32[]{:S(2)}) %all-to-all-start.1) | async-done | bytes 1048608 | tf_op jit(solution)/shard_map/all_to_all | solution.py:298
  46.2 2.1 %collective-permute-start.1 = (f32[4,256,128]{2,1,0:T(8,128)S(1)}, f32[4,256,128]{2,1,0:T(8,128)S(1)}, u32[]{:S(2)}, u32[]{:S(2)}) collective-permute-start(f32[4,256,128]{2,1,0:T(8,128)S(1)} %bitcast.60), channel_id=1, source_target_pairs={{0,8},{8,16},{16,24},{24,0},{1,9},{9,17},{17,25},{25,1},{2,10},{10... | collective-permute-start | bytes 1572872 | tf_op jit(solution)/shard_map/ppermute | solution.py:274
  48.3 18.5 %collective-permute-done.3 = f32[4,256,128]{2,1,0:T(8,128)S(1)} collective-permute-done((f32[4,256,128]{2,1,0:T(8,128)S(1)}, f32[4,256,128]{2,1,0:T(8,128)S(1)}, u32[]{:S(2)}, u32[]{:S(2)}) %collective-permute-start.3) | collective-permute-done | bytes 524320 | tf_op jit(solution)/shard_map/ppermute | solution.py:274
  67.6 3.9 %collective-permute-done.4 = f32[2,64,128]{2,1,0:T(8,128)S(1)} collective-permute-done((f32[2,64,128]{2,1,0:T(8,128)S(1)}, f32[2,64,128]{2,1,0:T(8,128)S(1)}, u32[]{:S(2)}, u32[]{:S(2)}) %collective-permute-start.4) | collective-permute-done | bytes 65568 | tf_op jit(solution)/shard_map/ppermute | solution.py:278
  71.6 4.1 %collective-permute-done.6.far = f32[4,4,256,128]{3,2,1,0:T(8,128)} collective-permute-done((f32[4,4,256,128]{3,2,1,0:T(8,128)S(1)}, f32[4,4,256,128]{3,2,1,0:T(8,128)}, u32[]{:S(2)}, u32[]{:S(2)}) %collective-permute-start.6) | collective-permute-done | bytes 2097184 | tf_op jit(solution)/shard_map/ppermute | solution.py:278
  75.8 3.8 %first_scores.1 = (bf16[4,256,512]{2,1,0:T(8,128)(2,1)S(1)}, bf16[4,256,512]{2,1,0:T(8,128)(2,1)S(1)}, bf16[4,256,512]{2,1,0:T(8,128)(2,1)S(1)}, bf16[4,256,512]...) custom-call(f32[256,128]{1,0:T(8,128)S(1)} %bitcast.57, ...), custom_call_target="tpu_custom_call" | custom-call | flops 805306368 | bytes 10485760 | tf_op jit(solution)/shard_map/first_scores/pallas_call | solution.py:213
  80.1 4.1 %first_apply.1 = (bf16[4,128,512]{2,1,0:T(8,128)(2,1)S(1)}, bf16[4,128,512]{2,1,0:T(8,128)(2,1)S(1)}, f32[4,128,512]{2,1,0:T(8,128)S(1)}, f32[4,128,512]{2,1,0:T(8,128)S(1)}, f32[128,256]{1,0:T(8,128)S(1)}) custom-call(s32[67]{0:T(128)S(1)} %concatenate.9.scal, f32[4,128,512]{2,1,0:T(8,128)S(1)} %get-tuple-element.66.refs_0_, ...), custom_call_target="tpu_custom_call" | custom-call | flops 805306368 | bytes 12582912 | tf_op jit(solution)/shard_map/first_apply/pallas_call | solution.py:241
  84.8 2.1 %collective-permute-start.12 = (f32[2,128,512]{2,1,0:T(8,128)S(1)}, f32[2,128,512]{2,1,0:T(8,128)S(1)}, u32[]{:S(2)}, u32[]{:S(2)}) collective-permute-start(f32[2,128,512]{2,1,0:T(8,128)S(1)} %pad_maximum_fusion.3), channel_id=1, source_target_pairs={{0,16},{8,24},{16,0},{24,8},{1,17},{9,25},{17,1},{25,9},{2,18},{10... | collective-permute-start | bytes 1572872 | tf_op jit(solution)/shard_map/ppermute | solution.py:274
  86.9 2.2 %collective-permute-start.13 = (f32[2,128,512]{2,1,0:T(8,128)S(1)}, f32[2,128,512]{2,1,0:T(8,128)S(1)}, u32[]{:S(2)}, u32[]{:S(2)}) collective-permute-start(f32[2,128,512]{2,1,0:T(8,128)S(1)} %pad_maximum_fusion.4), channel_id=1, source_target_pairs={{0,8},{8,16},{16,24},{24,0},{1,9},{9,17},{17,25},{25,1},{2,10},{10... | collective-permute-start | bytes 1572872 | tf_op jit(solution)/shard_map/ppermute | solution.py:274
  89.7 3.8 %second_apply.1 = (f32[128,256]{1,0:T(8,128)S(1)}, f32[128,256]{1,0:T(8,128)S(1)}) custom-call(f32[128,256]{1,0:T(8,128)S(1)} %get-tuple-element.74.pa, f32[128,256]{1,0:T(8,128)S(1)} %collective-permute-done.8.pb, f32[128,256]{1,0:T(8,128)S(1)} %get-tuple-element.75.x0, bf16[4,256,512]{2,1,0:T(8,128)(2,1)S(1)} %get-tuple-element.68.refs_2_.refs_0_, ...), custom_call_target="tpu_custom_call" | custom-call | flops 1610612736 | bytes 6291456 | tf_op jit(solution)/shard_map/second_apply/pallas_call | solution.py:260
  93.6 1.5 collective-permute-start.9
  95.1 3.6 %collective-permute-done.9.pb = f32[128,256]{1,0:T(8,128)S(1)} collective-permute-done((f32[128,256]{1,0:T(8,128)S(1)}, f32[128,256]{1,0:T(8,128)S(1)}, u32[]{:S(2)}, u32[]{:S(2)}) %collective-permute-start.9) | collective-permute-done | bytes 131104 | tf_op jit(solution)/shard_map/ppermute | solution.py:278
  98.6 4.0 %third_apply.1 = (f32[128,256]{1,0:T(8,128)S(1)}, f32[128,256]{1,0:T(8,128)S(1)}, f32[128,256]{1,0:T(8,128)S(1)}, f32[128,256]{1,0:T(8,128)S(1)}) custom-call(f32[128,256]{1,0:T(8,128)S(1)} %get-tuple-element.78.pa, f32[128,256]{1,0:T(8,128)S(1)} %collective-permute-done.9.pb, f32[128,256]{1,0:T(8,128)S(1)} %get-tuple-element.79.resid, ...), custom_call_target="tpu_custom_call" | custom-call | flops 1610612736 | bytes 6291456 | tf_op jit(solution)/shard_map/third_apply/pallas_call | solution.py:260
  102.7 1.7 %collective-permute-start.10 = (f32[128,256]{1,0:T(8,128)S(1)}, f32[128,256]{1,0:T(8,128)S(1)}, u32[]{:S(2)}, u32[]{:S(2)}) collective-permute-start(f32[128,256]{1,0:T(8,128)S(1)} %get-tuple-element.80.pa), channel_id=1, source_target_pairs={{0,1},{1,0},{2,3},{3,2},{4,5},{5,4},{6,7},{7,6},{8,9},{9,8},{10,11... | collective-permute-start | bytes 393224 | tf_op jit(solution)/shard_map/ppermute | solution.py:278
  104.4 3.6 %collective-permute-done.10.pb = f32[128,256]{1,0:T(8,128)S(1)} collective-permute-done((f32[128,256]{1,0:T(8,128)S(1)}, f32[128,256]{1,0:T(8,128)S(1)}, u32[]{:S(2)}, u32[]{:S(2)}) %collective-permute-start.10) | collective-permute-done | bytes 131104 | tf_op jit(solution)/shard_map/ppermute | solution.py:278
  107.9 3.0 %collective-permute-done.11.t1 = f32[2,128,512]{2,1,0:T(8,128)S(1)} collective-permute-done((f32[2,128,512]{2,1,0:T(8,128)S(1)}, f32[2,128,512]{2,1,0:T(8,128)S(1)}, u32[]{:S(2)}, u32[]{:S(2)}) %collective-permute-start.11) | collective-permute-done | bytes 524320 | tf_op jit(solution)/shard_map/ppermute | solution.py:274
  112.1 2.7 %collective-permute-start.16 = (f32[128,256]{1,0:T(8,128)S(1)}, f32[128,256]{1,0:T(8,128)S(1)}, u32[]{:S(2)}, u32[]{:S(2)}) collective-permute-start(f32[128,256]{1,0:T(8,128)S(1)} %last_update.1), channel_id=1, source_target_pairs={{0,8},{8,16},{16,24},{24,0},{1,9},{9,17},{17,25},{25,1},{2,10},{10... | collective-permute-start | bytes 393224 | tf_op jit(solution)/shard_map/ppermute | solution.py:274
  115.7 5.3 %collective-permute-done.16 = f32[128,256]{1,0:T(8,128)S(1)} collective-permute-done((f32[128,256]{1,0:T(8,128)S(1)}, f32[128,256]{1,0:T(8,128)S(1)}, u32[]{:S(2)}, u32[]{:S(2)}) %collective-permute-start.16) | collective-permute-done | bytes 131104 | tf_op jit(solution)/shard_map/ppermute | solution.py:274
  121.0 1.6 collective-permute-done.15
  122.6 1.9 %collective-permute-done.14 = f32[128,256]{1,0:T(8,128)S(1)} collective-permute-done((f32[128,256]{1,0:T(8,128)S(1)}, f32[128,256]{1,0:T(8,128)S(1)}, u32[]{:S(2)}, u32[]{:S(2)}) %collective-permute-start.14) | collective-permute-done | bytes 131104 | tf_op jit(solution)/shard_map/ppermute | solution.py:274
  124.7 1.9 %collective-permute-done.17.far_vectors = f32[4,128,256]{2,1,0:T(8,128)S(1)} collective-permute-done((f32[4,128,256]{2,1,0:T(8,128)S(1)}, f32[4,128,256]{2,1,0:T(8,128)S(1)}, u32[]{:S(2)}, u32[]{:S(2)}) %collective-permute-start.17) | collective-permute-done | bytes 524320 | tf_op jit(solution)/shard_map/ppermute | solution.py:278
  126.6 1.7 %rhs_terms.1 = f32[2,4,256,128]{3,2,1,0:T(8,128)} custom-call(f32[4,128,256]{2,1,0:T(8,128)S(1)} %pad_maximum_fusion.5.own_vectors, f32[4,128,256]{2,1,0:T(8,128)S(1)} %collective-permute-done.17.far_vectors, f32[4,128,512]{2,1,0:T(8,128)S(1)} %get-tuple-element.81.own, f32[4,128,512]{2,1,0:T(8,128)S(1)} %collective-permute-done.18.got, ...), custom_call_target="tpu_custom_call" | custom-call | flops 536870912 | bytes 4194304 | tf_op jit(solution)/shard_map/rhs_terms/pallas_call | solution.py:419
  128.3 3.7 %all-to-all-start.2 = ((f32[4,8,64,128]{3,2,1,0:T(8,128)}), f32[4,8,64,128]{3,2,1,0:T(8,128)S(1)}, u32[]{:S(2)}, u32[]{:S(2)}) async-start(f32[4,8,64,128]{3,2,1,0:T(8,128)} %bitcast.27), calls=%async_computation.2 | async-start | bytes 2097152 | tf_op jit(solution)/shard_map/all_to_all | solution.py:462
  132.2 2.7 %collective-permute-start.19 = (f32[128,64]{0,1:T(8,128)S(1)}, f32[128,64]{0,1:T(8,128)S(1)}, u32[]{:S(2)}, u32[]{:S(2)}) collective-permute-start(f32[128,64]{0,1:T(8,128)S(1)} %dynamic-slice_bitcast_fusion.1), channel_id=1, source_target_pairs={{0,2},{1,3},{2,0},{3,1},{4,6},{5,7},{6,4},{7,5},{8,10},{9,11},{10,... | collective-permute-start | bytes 98312 | tf_op jit(solution)/shard_map/ppermute | solution.py:278
  134.9 2.5 %collective-permute-done.19 = f32[128,64]{0,1:T(8,128)S(1)} collective-permute-done((f32[128,64]{0,1:T(8,128)S(1)}, f32[128,64]{0,1:T(8,128)S(1)}, u32[]{:S(2)}, u32[]{:S(2)}) %collective-permute-start.19) | collective-permute-done | bytes 32800 | tf_op jit(solution)/shard_map/ppermute | solution.py:278
  138.6 8.9 %all-to-all-done.2 = f32[4,8,64,128]{3,2,1,0:T(8,128)S(1)} async-done(((f32[4,8,64,128]{3,2,1,0:T(8,128)}), f32[4,8,64,128]{3,2,1,0:T(8,128)S(1)}, u32[]{:S(2)}, u32[]{:S(2)}) %all-to-all-start.2) | async-done | bytes 1048608 | tf_op jit(solution)/shard_map/all_to_all | solution.py:462
  148.3 3.8 %all-to-all-start.3 = ((f32[8,64,128]{2,1,0:T(8,128)}), f32[8,64,128]{2,1,0:T(8,128)S(1)}, u32[]{:S(2)}, u32[]{:S(2)}) async-start(f32[8,64,128]{2,1,0:T(8,128)} %reduce_sum.18), calls=%async_computation.3 | async-start | bytes 524288 | tf_op jit(solution)/shard_map/all_to_all | solution.py:466
  152.1 11.0 %all-to-all-done.3 = f32[8,64,128]{2,1,0:T(8,128)S(1)} async-done(((f32[8,64,128]{2,1,0:T(8,128)}), f32[8,64,128]{2,1,0:T(8,128)S(1)}, u32[]{:S(2)}, u32[]{:S(2)}) %all-to-all-start.3) | async-done | bytes 262176 | tf_op jit(solution)/shard_map/all_to_all | solution.py:466
  (66 shorter events, 16.6 us)
Async XLA Ops:
  2.5 13.9 %collective-permute-start = (f32[72,128]{1,0:T(8,128)S(1)}, f32[72,128]{1,0:T(8,128)S(1)}, u32[]{:S(2)}, u32[]{:S(2)}) collective-permute-start(f32[72,128]{1,0:T(8,128)S(1)} %select_maximum_fusion), channel_id=1, source_target_pairs={{0,2},{1,3},{2,0},{3,1},{4,6},{5,7},{6,4},{7,5},{8,10},{9,11},{10,... | collective-permute-start | bytes 110600 | tf_op jit(solution)/shard_map/ppermute | solution.py:278
  7.3 18.3 %all-to-all-start = ((f32[8,64,128]{2,1,0:T(8,128)}), f32[8,64,128]{2,1,0:T(8,128)S(1)}, u32[]{:S(2)}, u32[]{:S(2)}) async-start(f32[8,64,128]{2,1,0:T(8,128)} %broadcast_in_dim.4), calls=%async_computation | async-start | bytes 524288 | tf_op jit(solution)/shard_map/all_to_all | solution.py:298
  26.6 17.5 %all-to-all-start.1 = ((f32[4,2,256,128]{3,2,1,0:T(8,128)}), f32[4,2,256,128]{3,2,1,0:T(8,128)S(1)}, u32[]{:S(2)}, u32[]{:S(2)}) async-start(f32[4,2,256,128]{3,2,1,0:T(8,128)} %broadcast_in_dim.5), calls=%async_computation.1 | async-start | bytes 2097152 | tf_op jit(solution)/shard_map/all_to_all | solution.py:298
  31.1 40.4 %collective-permute-start.5 = (s32[32,56,128]{2,1,0:T(8,128)}, s32[32,56,128]{2,1,0:T(8,128)S(1)}, u32[]{:S(2)}, u32[]{:S(2)}) collective-permute-start(s32[32,56,128]{2,1,0:T(8,128)} %slice.74), channel_id=1, source_target_pairs={{0,2},{1,3},{2,0},{3,1},{4,6},{5,7},{6,4},{7,5},{8,10},{9,11},{10,... | collective-permute-start | bytes 2752520 | tf_op jit(solution)/shard_map/ppermute | solution.py:278
  44.2 22.6 %collective-permute-start.3 = (f32[4,256,128]{2,1,0:T(8,128)S(1)}, f32[4,256,128]{2,1,0:T(8,128)S(1)}, u32[]{:S(2)}, u32[]{:S(2)}) collective-permute-start(f32[4,256,128]{2,1,0:T(8,128)S(1)} %bitcast.58), channel_id=1, source_target_pairs={{0,24},{8,0},{16,8},{24,16},{1,25},{9,1},{17,9},{25,17},{2,26},{10... | collective-permute-start | bytes 1572872 | tf_op jit(solution)/shard_map/ppermute | solution.py:274
  45.1 21.7 %collective-permute-start.2 = (f32[4,256,128]{2,1,0:T(8,128)S(1)}, f32[4,256,128]{2,1,0:T(8,128)S(1)}, u32[]{:S(2)}, u32[]{:S(2)}) collective-permute-start(f32[4,256,128]{2,1,0:T(8,128)S(1)} %bitcast.59), channel_id=1, source_target_pairs={{0,16},{8,24},{16,0},{24,8},{1,17},{9,25},{17,1},{25,9},{2,18},{10... | collective-permute-start | bytes 1572872 | tf_op jit(solution)/shard_map/ppermute | solution.py:274
  46.2 21.2 %collective-permute-start.1 = (f32[4,256,128]{2,1,0:T(8,128)S(1)}, f32[4,256,128]{2,1,0:T(8,128)S(1)}, u32[]{:S(2)}, u32[]{:S(2)}) collective-permute-start(f32[4,256,128]{2,1,0:T(8,128)S(1)} %bitcast.60), channel_id=1, source_target_pairs={{0,8},{8,16},{16,24},{24,0},{1,9},{9,17},{17,25},{25,1},{2,10},{10... | collective-permute-start | bytes 1572872 | tf_op jit(solution)/shard_map/ppermute | solution.py:274
  48.3 23.2 %collective-permute-start.4 = (f32[2,64,128]{2,1,0:T(8,128)S(1)}, f32[2,64,128]{2,1,0:T(8,128)S(1)}, u32[]{:S(2)}, u32[]{:S(2)}) collective-permute-start(f32[2,64,128]{2,1,0:T(8,128)S(1)} %pad_maximum_fusion.8), channel_id=1, source_target_pairs={{0,1},{1,0},{2,3},{3,2},{4,5},{5,4},{6,7},{7,6},{8,9},{9,8},{10,11... | collective-permute-start | bytes 196616 | tf_op jit(solution)/shard_map/ppermute | solution.py:278
  67.4 4.1 %copy-start.1 = (s32[1,32]{1,0:T(1,128)S(1)}, s32[1,32]{1,0:T(1,128)}, u32[]{:S(2)}) copy-start(s32[1,32]{1,0:T(1,128)} %param.8) | copy-start | bytes 388
  71.5 4.3 %collective-permute-start.6 = (f32[4,4,256,128]{3,2,1,0:T(8,128)S(1)}, f32[4,4,256,128]{3,2,1,0:T(8,128)}, u32[]{:S(2)}, u32[]{:S(2)}) collective-permute-start(f32[4,4,256,128]{3,2,1,0:T(8,128)S(1)} %pad_maximum_fusion.own), channel_id=1, source_target_pairs={{0,4},{4,0},{1,5},{5,1},{2,6},{6,2},{3,7},{7,3},{8,12},{12,8},{9,1... | collective-permute-start | bytes 6291464 | tf_op jit(solution)/shard_map/ppermute | solution.py:278
  71.5 8.6 %collective-permute-start.7 = (s32[32,8,128]{2,1,0:T(8,128)S(1)}, s32[32,8,128]{2,1,0:T(8,128)S(1)}, u32[]{:S(2)}, u32[]{:S(2)}) collective-permute-start(s32[32,8,128]{2,1,0:T(8,128)S(1)} %slice.75), channel_id=1, source_target_pairs={{0,2},{1,3},{2,0},{3,1},{4,6},{5,7},{6,4},{7,5},{8,10},{9,11},{10,... | collective-permute-start | bytes 393224 | tf_op jit(solution)/shard_map/ppermute | solution.py:278
  75.8 4.3 %copy-start = (s32[1,32,128,128]{3,2,1,0:T(8,128)S(1)}, s32[1,32,128,128]{3,2,1,0:T(8,128)}, u32[]{:S(2)}) copy-start(s32[1,32,128,128]{3,2,1,0:T(8,128)} %param.9) | copy-start | bytes 6291460
  84.2 5.6 %collective-permute-start.8 = (f32[128,256]{1,0:T(8,128)S(1)}, f32[128,256]{1,0:T(8,128)S(1)}, u32[]{:S(2)}, u32[]{:S(2)}) collective-permute-start(f32[128,256]{1,0:T(8,128)S(1)} %get-tuple-element.74.pa), channel_id=1, source_target_pairs={{0,1},{1,0},{2,3},{3,2},{4,5},{5,4},{6,7},{7,6},{8,9},{9,8},{10,11... | collective-permute-start | bytes 393224 | tf_op jit(solution)/shard_map/ppermute | solution.py:278
  84.5 26.4 %collective-permute-start.11 = (f32[2,128,512]{2,1,0:T(8,128)S(1)}, f32[2,128,512]{2,1,0:T(8,128)S(1)}, u32[]{:S(2)}, u32[]{:S(2)}) collective-permute-start(f32[2,128,512]{2,1,0:T(8,128)S(1)} %pad_maximum_fusion.2), channel_id=1, source_target_pairs={{0,24},{8,0},{16,8},{24,16},{1,25},{9,1},{17,9},{25,17},{2,26},{10... | collective-permute-start | bytes 1572872 | tf_op jit(solution)/shard_map/ppermute | solution.py:274
  84.8 26.1 %collective-permute-start.12 = (f32[2,128,512]{2,1,0:T(8,128)S(1)}, f32[2,128,512]{2,1,0:T(8,128)S(1)}, u32[]{:S(2)}, u32[]{:S(2)}) collective-permute-start(f32[2,128,512]{2,1,0:T(8,128)S(1)} %pad_maximum_fusion.3), channel_id=1, source_target_pairs={{0,16},{8,24},{16,0},{24,8},{1,17},{9,25},{17,1},{25,9},{2,18},{10... | collective-permute-start | bytes 1572872 | tf_op jit(solution)/shard_map/ppermute | solution.py:274
  86.9 24.7 %collective-permute-start.13 = (f32[2,128,512]{2,1,0:T(8,128)S(1)}, f32[2,128,512]{2,1,0:T(8,128)S(1)}, u32[]{:S(2)}, u32[]{:S(2)}) collective-permute-start(f32[2,128,512]{2,1,0:T(8,128)S(1)} %pad_maximum_fusion.4), channel_id=1, source_target_pairs={{0,8},{8,16},{16,24},{24,0},{1,9},{9,17},{17,25},{25,1},{2,10},{10... | collective-permute-start | bytes 1572872 | tf_op jit(solution)/shard_map/ppermute | solution.py:274
  93.6 5.1 %collective-permute-start.9 = (f32[128,256]{1,0:T(8,128)S(1)}, f32[128,256]{1,0:T(8,128)S(1)}, u32[]{:S(2)}, u32[]{:S(2)}) collective-permute-start(f32[128,256]{1,0:T(8,128)S(1)} %get-tuple-element.78.pa), channel_id=1, source_target_pairs={{0,1},{1,0},{2,3},{3,2},{4,5},{5,4},{6,7},{7,6},{8,9},{9,8},{10,11... | collective-permute-start | bytes 393224 | tf_op jit(solution)/shard_map/ppermute | solution.py:278
  102.7 5.2 %collective-permute-start.10 = (f32[128,256]{1,0:T(8,128)S(1)}, f32[128,256]{1,0:T(8,128)S(1)}, u32[]{:S(2)}, u32[]{:S(2)}) collective-permute-start(f32[128,256]{1,0:T(8,128)S(1)} %get-tuple-element.80.pa), channel_id=1, source_target_pairs={{0,1},{1,0},{2,3},{3,2},{4,5},{5,4},{6,7},{7,6},{8,9},{9,8},{10,11... | collective-permute-start | bytes 393224 | tf_op jit(solution)/shard_map/ppermute | solution.py:278
  111.8 14.8 %collective-permute-start.18 = (f32[4,128,512]{2,1,0:T(8,128)S(1)}, f32[4,128,512]{2,1,0:T(8,128)S(1)}, u32[]{:S(2)}, u32[]{:S(2)}) collective-permute-start(f32[4,128,512]{2,1,0:T(8,128)S(1)} %pad_maximum_fusion.1), channel_id=1, source_target_pairs={{0,4},{4,0},{1,5},{5,1},{2,6},{6,2},{3,7},{7,3},{8,12},{12,8},{9,1... | collective-permute-start | bytes 3145736 | tf_op jit(solution)/shard_map/ppermute | solution.py:278
  112.1 9.0 %collective-permute-start.16 = (f32[128,256]{1,0:T(8,128)S(1)}, f32[128,256]{1,0:T(8,128)S(1)}, u32[]{:S(2)}, u32[]{:S(2)}) collective-permute-start(f32[128,256]{1,0:T(8,128)S(1)} %last_update.1), channel_id=1, source_target_pairs={{0,8},{8,16},{16,24},{24,0},{1,9},{9,17},{17,25},{25,1},{2,10},{10... | collective-permute-start | bytes 393224 | tf_op jit(solution)/shard_map/ppermute | solution.py:274
  114.8 7.9 %collective-permute-start.15 = (f32[128,256]{1,0:T(8,128)S(1)}, f32[128,256]{1,0:T(8,128)S(1)}, u32[]{:S(2)}, u32[]{:S(2)}) collective-permute-start(f32[128,256]{1,0:T(8,128)S(1)} %last_update.1), channel_id=1, source_target_pairs={{0,16},{8,24},{16,0},{24,8},{1,17},{9,25},{17,1},{25,9},{2,18},{10... | collective-permute-start | bytes 393224 | tf_op jit(solution)/shard_map/ppermute | solution.py:274
  115.2 9.4 %collective-permute-start.14 = (f32[128,256]{1,0:T(8,128)S(1)}, f32[128,256]{1,0:T(8,128)S(1)}, u32[]{:S(2)}, u32[]{:S(2)}) collective-permute-start(f32[128,256]{1,0:T(8,128)S(1)} %last_update.1), channel_id=1, source_target_pairs={{0,24},{8,0},{16,8},{24,16},{1,25},{9,1},{17,9},{25,17},{2,26},{10... | collective-permute-start | bytes 393224 | tf_op jit(solution)/shard_map/ppermute | solution.py:274
  124.6 2.0 %collective-permute-start.17 = (f32[4,128,256]{2,1,0:T(8,128)S(1)}, f32[4,128,256]{2,1,0:T(8,128)S(1)}, u32[]{:S(2)}, u32[]{:S(2)}) collective-permute-start(f32[4,128,256]{2,1,0:T(8,128)S(1)} %pad_maximum_fusion.5.own_vectors), channel_id=1, source_target_pairs={{0,4},{4,0},{1,5},{5,1},{2,6},{6,2},{3,7},{7,3},{8,12},{12,8},{9,1... | collective-permute-start | bytes 1572872 | tf_op jit(solution)/shard_map/ppermute | solution.py:278
  128.3 19.2 %all-to-all-start.2 = ((f32[4,8,64,128]{3,2,1,0:T(8,128)}), f32[4,8,64,128]{3,2,1,0:T(8,128)S(1)}, u32[]{:S(2)}, u32[]{:S(2)}) async-start(f32[4,8,64,128]{3,2,1,0:T(8,128)} %bitcast.27), calls=%async_computation.2 | async-start | bytes 2097152 | tf_op jit(solution)/shard_map/all_to_all | solution.py:462
  132.2 5.3 %collective-permute-start.19 = (f32[128,64]{0,1:T(8,128)S(1)}, f32[128,64]{0,1:T(8,128)S(1)}, u32[]{:S(2)}, u32[]{:S(2)}) collective-permute-start(f32[128,64]{0,1:T(8,128)S(1)} %dynamic-slice_bitcast_fusion.1), channel_id=1, source_target_pairs={{0,2},{1,3},{2,0},{3,1},{4,6},{5,7},{6,4},{7,5},{8,10},{9,11},{10,... | collective-permute-start | bytes 98312 | tf_op jit(solution)/shard_map/ppermute | solution.py:278
  148.3 14.9 %all-to-all-start.3 = ((f32[8,64,128]{2,1,0:T(8,128)}), f32[8,64,128]{2,1,0:T(8,128)S(1)}, u32[]{:S(2)}, u32[]{:S(2)}) async-start(f32[8,64,128]{2,1,0:T(8,128)} %reduce_sum.18), calls=%async_computation.3 | async-start | bytes 524288 | tf_op jit(solution)/shard_map/all_to_all | solution.py:466

commit v6 on v5

--- a/solution.py
+++ b/solution.py
@@ -290,7 +290,8 @@
 NP = 'y'
 XS = 'perm'
 CHUNKS = (56,8)
-YS = 'a2a'
+YS = 'perm'
+DT = 'after'
 
 
 def everyone(value, axis, size):
@@ -402,8 +403,6 @@
         third_kernel, (part, part_b, resid, x0), shared, 4, "third_apply"
     )
     part_b = flip(part, "rep", 4, 1)
-    part_b, moved = tie((part_b, moved))
-    got = flip(jnp.stack([far_target[0]] + [v[1] for v in moved]), "core", 2, 1)
     solved = pl.pallas_call(
         last_kernel,
         out_shape=shaped(TILE, RANK),
@@ -412,7 +411,13 @@
         name="last_update",
     )(part, part_b, resid1, direc1, x1)
 
-    vectors = jnp.stack([solved] + [shift(solved, "x", 4, -k) for k in (1, 2, 3)])
+    vectors = [shift(solved, "x", 4, -k) for k in (1, 2, 3)]
+    if DT == "after":
+        vectors, moved = tie((vectors, moved))
+    else:
+        solved, moved = tie((solved, moved))
+    got = flip(jnp.stack([far_target[0]] + [v[1] for v in moved]), "core", 2, 1)
+    vectors = jnp.stack([solved] + vectors)
     far_vectors = flip(vectors, "core", 2, 1)
 
     vmem = pl.BlockSpec(memory_space=pltpu.VMEM)

time: 164 us -> 162 us (0.988)
  waiting for transfers between devices: 94.4 us -> 83.3 us
  starting transfers between devices: 40.6 us -> 50.1 us
    all_to_all x2 -> x1, waiting for transfers between devices: 22 us -> 9.12 us  [everyone(): return lax.all_to_all(copies, axis, split_axis=0, concat_axis=0, tiled=True)]
    ppermute x0 -> x3, starting transfers between devices: none -> 8.28 us  [along_y(): return lax.ppermute(value, ('y', 'rep'), pairs)]
    ppermute x0 -> x3, waiting for transfers between devices: none -> 7.37 us  [along_y(): return lax.ppermute(value, ('y', 'rep'), pairs)]
    ppermute x9, waiting for transfers between devices: 31.7 us -> 25.6 us  [shift(): lax.ppermute(value, axis, [(i, (i + by) % size) for i in range(size)])]
    all_to_all x2 -> x1, starting transfers between devices: 11.1 us -> 6.67 us  [everyone(): return lax.all_to_all(copies, axis, split_axis=0, concat_axis=0, tiled=True)]
    all_to_all x1, starting transfers between devices: 3.85 us -> 7.22 us  [per_device(): lax.all_to_all(summed, ('zh', 'rep'), split_axis=0, concat_axis=0, tiled=...]
    ppermute x11, waiting for transfers between devices: 20.8 us -> 23.9 us  [flip(): return lax.ppermute(value, axis, [(i, i ^ bit) for i in range(size)])]
    ppermute x11, starting transfers between devices: 9.65 us -> 12.7 us  [flip(): return lax.ppermute(value, axis, [(i, i ^ bit) for i in range(size)])]
  transfers between devices with their start and end apart: 24 -> 26, of which waited for: 19 -> 20; matrix products, arithmetic and copies ran while one was open for 4% -> 4% of each run, Pallas kernels for 7% -> 7%
where the time goes in v6:
time: 162 us; the launch traced here: 161 us
  waiting for transfers between devices  83.3 us (51%)
  starting transfers between devices  50.1 us (31%)
  Pallas kernels  17.6 us (11%)
  local copies, waits for them, and re-layouts  6.59 us (4%)
  other arithmetic  2.68 us (2%)
    ppermute x9, waiting for transfers between devices, shift(): lax.ppermute(value, axis, [(i, (i + by) % size) for i in range(size)])  25.6 us
    ppermute x11, waiting for transfers between devices, flip(): return lax.ppermute(value, axis, [(i, i ^ bit) for i in range(size)])  23.9 us
    ppermute x11, starting transfers between devices, flip(): return lax.ppermute(value, axis, [(i, i ^ bit) for i in range(size)])  12.7 us
    all_to_all x1, waiting for transfers between devices, per_device(): lax.all_to_all(summed, ('zh', 'rep'), split_axis=0, concat_axis=0, tiled=...  11 us
    ppermute x9, starting transfers between devices, shift(): lax.ppermute(value, axis, [(i, (i + by) % size) for i in range(size)])  10.9 us
    all_to_all x1, waiting for transfers between devices, everyone(): return lax.all_to_all(copies, axis, split_axis=0, concat_axis=0, tiled=True)  9.12 us
    ppermute x3, starting transfers between devices, along_y(): return lax.ppermute(value, ('y', 'rep'), pairs)  8.28 us
    pallas_call x2, Pallas kernels, next_apply(): pl.pallas_call(kernel, grid=(4,), in_specs=[spec(whole)] * len(vectors) +...  7.92 us
  transfers between devices with their start and end apart: 26, of which 20 were waited for; matrix products, arithmetic and copies ran while one was open for 4% of the time, Pallas kernels for 7%

profile of v6, /device:TPU:6, one launch (start us, length us, event | category | flops | bytes accessed | tf_op | source)
XLA Modules:
  0.0 161.3 jit_solution(15910932862614826693)
XLA Ops:
  2.5 3.4 %collective-permute-start = (f32[72,128]{1,0:T(8,128)S(1)}, f32[72,128]{1,0:T(8,128)S(1)}, u32[]{:S(2)}, u32[]{:S(2)}) collective-permute-start(f32[72,128]{1,0:T(8,128)S(1)} %select_maximum_fusion), channel_id=1, source_target_pairs={{0,2},{1,3},{2,0},{3,1},{4,6},{5,7},{6,4},{7,5},{8,10},{9,11},{10,... | collective-permute-start | bytes 110600 | tf_op jit(solution)/shard_map/ppermute | solution.py:278
  5.9 1.5 broadcast_in_dim.2
  7.3 6.7 %all-to-all-start = ((f32[8,64,128]{2,1,0:T(8,128)}), f32[8,64,128]{2,1,0:T(8,128)S(1)}, u32[]{:S(2)}, u32[]{:S(2)}) async-start(f32[8,64,128]{2,1,0:T(8,128)} %broadcast_in_dim.2), calls=%async_computation | async-start | bytes 524288 | tf_op jit(solution)/shard_map/all_to_all | solution.py:299
  16.5 9.1 %all-to-all-done = f32[8,64,128]{2,1,0:T(8,128)S(1)} async-done(((f32[8,64,128]{2,1,0:T(8,128)}), f32[8,64,128]{2,1,0:T(8,128)S(1)}, u32[]{:S(2)}, u32[]{:S(2)}) %all-to-all-start) | async-done | bytes 262176 | tf_op jit(solution)/shard_map/all_to_all | solution.py:299
  25.6 4.9 %collective-permute-start.3 = (f32[2,256,128]{2,1,0:T(8,128)S(1)}, f32[2,256,128]{2,1,0:T(8,128)S(1)}, u32[]{:S(2)}, u32[]{:S(2)}) collective-permute-start(f32[2,256,128]{2,1,0:T(8,128)S(1)} %bitcast.66), channel_id=1, source_target_pairs={{0,192},{2,194},{64,128},{66,130},{129,65},{131,67},{193,1},{195,3... | collective-permute-start | bytes 786440 | tf_op jit(solution)/shard_map/ppermute | solution.py:306
  30.5 2.0 %collective-permute-start.2 = (f32[2,256,128]{2,1,0:T(8,128)S(1)}, f32[2,256,128]{2,1,0:T(8,128)S(1)}, u32[]{:S(2)}, u32[]{:S(2)}) collective-permute-start(f32[2,256,128]{2,1,0:T(8,128)S(1)} %bitcast.67), channel_id=1, source_target_pairs={{0,64},{2,66},{64,0},{66,2},{129,193},{131,195},{193,129},{195,131... | collective-permute-start | bytes 786440 | tf_op jit(solution)/shard_map/ppermute | solution.py:306
  34.5 6.4 %collective-permute-done.2 = f32[2,256,128]{2,1,0:T(8,128)S(1)} collective-permute-done((f32[2,256,128]{2,1,0:T(8,128)S(1)}, f32[2,256,128]{2,1,0:T(8,128)S(1)}, u32[]{:S(2)}, u32[]{:S(2)}) %collective-permute-start.2) | collective-permute-done | bytes 262176 | tf_op jit(solution)/shard_map/ppermute | solution.py:306
  43.7 2.1 %collective-permute-start.4 = (f32[4,256,128]{2,1,0:T(8,128)S(1)}, f32[4,256,128]{2,1,0:T(8,128)S(1)}, u32[]{:S(2)}, u32[]{:S(2)}) collective-permute-start(f32[4,256,128]{2,1,0:T(8,128)S(1)} %bitcast.64), channel_id=1, source_target_pairs={{0,8},{8,16},{16,24},{24,0},{1,9},{9,17},{17,25},{25,1},{2,10},{10... | collective-permute-start | bytes 1572872 | tf_op jit(solution)/shard_map/ppermute | solution.py:274
  45.8 1.9 %collective-permute-start.7 = (f32[2,64,128]{2,1,0:T(8,128)S(1)}, f32[2,64,128]{2,1,0:T(8,128)S(1)}, u32[]{:S(2)}, u32[]{:S(2)}) collective-permute-start(f32[2,64,128]{2,1,0:T(8,128)S(1)} %pad_maximum_fusion.9), channel_id=1, source_target_pairs={{0,1},{1,0},{2,3},{3,2},{4,5},{5,4},{6,7},{7,6},{8,9},{9,8},{10,11... | collective-permute-start | bytes 196616 | tf_op jit(solution)/shard_map/ppermute | solution.py:278
  47.6 17.1 %collective-permute-done.6 = f32[4,256,128]{2,1,0:T(8,128)S(1)} collective-permute-done((f32[4,256,128]{2,1,0:T(8,128)S(1)}, f32[4,256,128]{2,1,0:T(8,128)S(1)}, u32[]{:S(2)}, u32[]{:S(2)}) %collective-permute-start.6) | collective-permute-done | bytes 524320 | tf_op jit(solution)/shard_map/ppermute | solution.py:274
  65.5 3.6 %collective-permute-done.8 = s32[32,56,128]{2,1,0:T(8,128)S(1)} collective-permute-done((s32[32,56,128]{2,1,0:T(8,128)}, s32[32,56,128]{2,1,0:T(8,128)S(1)}, u32[]{:S(2)}, u32[]{:S(2)}) %collective-permute-start.8) | collective-permute-done | bytes 917536 | tf_op jit(solution)/shard_map/ppermute | solution.py:278
  69.3 4.1 %collective-permute-done.9.far = f32[4,4,256,128]{3,2,1,0:T(8,128)} collective-permute-done((f32[4,4,256,128]{3,2,1,0:T(8,128)S(1)}, f32[4,4,256,128]{3,2,1,0:T(8,128)}, u32[]{:S(2)}, u32[]{:S(2)}) %collective-permute-start.9) | collective-permute-done | bytes 2097184 | tf_op jit(solution)/shard_map/ppermute | solution.py:278
  73.5 3.8 %first_scores.1 = (bf16[4,256,512]{2,1,0:T(8,128)(2,1)S(1)}, bf16[4,256,512]{2,1,0:T(8,128)(2,1)S(1)}, bf16[4,256,512]{2,1,0:T(8,128)(2,1)S(1)}, bf16[4,256,512]...) custom-call(f32[256,128]{1,0:T(8,128)S(1)} %bitcast.61, ...), custom_call_target="tpu_custom_call" | custom-call | flops 805306368 | bytes 10485760 | tf_op jit(solution)/shard_map/first_scores/pallas_call | solution.py:213
  77.6 4.1 %first_apply.1 = (bf16[4,128,512]{2,1,0:T(8,128)(2,1)S(1)}, bf16[4,128,512]{2,1,0:T(8,128)(2,1)S(1)}, f32[4,128,512]{2,1,0:T(8,128)S(1)}, f32[4,128,512]{2,1,0:T(8,128)S(1)}, f32[128,256]{1,0:T(8,128)S(1)}) custom-call(s32[67]{0:T(128)S(1)} %concatenate.9.scal, f32[4,128,512]{2,1,0:T(8,128)S(1)} %get-tuple-element.68.refs_0_, ...), custom_call_target="tpu_custom_call" | custom-call | flops 805306368 | bytes 12582912 | tf_op jit(solution)/shard_map/first_apply/pallas_call | solution.py:241
  84.3 2.9 %collective-permute-done.11.pb = f32[128,256]{1,0:T(8,128)S(1)} collective-permute-done((f32[128,256]{1,0:T(8,128)S(1)}, f32[128,256]{1,0:T(8,128)S(1)}, u32[]{:S(2)}, u32[]{:S(2)}) %collective-permute-start.11) | collective-permute-done | bytes 131104 | tf_op jit(solution)/shard_map/ppermute | solution.py:278
  87.3 3.9 %second_apply.1 = (f32[128,256]{1,0:T(8,128)S(1)}, f32[128,256]{1,0:T(8,128)S(1)}) custom-call(f32[128,256]{1,0:T(8,128)S(1)} %get-tuple-element.76.pa, f32[128,256]{1,0:T(8,128)S(1)} %collective-permute-done.11.pb, f32[128,256]{1,0:T(8,128)S(1)} %get-tuple-element.77.x0, bf16[4,256,512]{2,1,0:T(8,128)(2,1)S(1)} %get-tuple-element.70.refs_2_.refs_0_, ...), custom_call_target="tpu_custom_call" | custom-call | flops 1610612736 | bytes 6291456 | tf_op jit(solution)/shard_map/second_apply/pallas_call | solution.py:260
  91.5 1.5 collective-permute-start.19
  93.0 3.1 %collective-permute-done.12.pb = f32[128,256]{1,0:T(8,128)S(1)} collective-permute-done((f32[128,256]{1,0:T(8,128)S(1)}, f32[128,256]{1,0:T(8,128)S(1)}, u32[]{:S(2)}, u32[]{:S(2)}) %collective-permute-start.12) | collective-permute-done | bytes 131104 | tf_op jit(solution)/shard_map/ppermute | solution.py:278
  96.2 4.1 %third_apply.1 = (f32[128,256]{1,0:T(8,128)S(1)}, f32[128,256]{1,0:T(8,128)S(1)}, f32[128,256]{1,0:T(8,128)S(1)}, f32[128,256]{1,0:T(8,128)S(1)}) custom-call(f32[128,256]{1,0:T(8,128)S(1)} %get-tuple-element.80.pa, f32[128,256]{1,0:T(8,128)S(1)} %collective-permute-done.12.pb, f32[128,256]{1,0:T(8,128)S(1)} %get-tuple-element.81.resid, ...), custom_call_target="tpu_custom_call" | custom-call | flops 1610612736 | bytes 6291456 | tf_op jit(solution)/shard_map/third_apply/pallas_call | solution.py:260
  100.8 4.7 %collective-permute-done.13.pb = f32[128,256]{1,0:T(8,128)S(1)} collective-permute-done((f32[128,256]{1,0:T(8,128)S(1)}, f32[128,256]{1,0:T(8,128)S(1)}, u32[]{:S(2)}, u32[]{:S(2)}) %collective-permute-start.13) | collective-permute-done | bytes 131104 | tf_op jit(solution)/shard_map/ppermute | solution.py:278
  106.3 2.3 %collective-permute-start.15 = (f32[128,256]{1,0:T(8,128)S(1)}, f32[128,256]{1,0:T(8,128)S(1)}, u32[]{:S(2)}, u32[]{:S(2)}) collective-permute-start(f32[128,256]{1,0:T(8,128)S(1)} %last_update.1), channel_id=1, source_target_pairs={{0,16},{8,24},{16,0},{24,8},{1,17},{9,25},{17,1},{25,9},{2,18},{10... | collective-permute-start | bytes 393224 | tf_op jit(solution)/shard_map/ppermute | solution.py:274
  108.6 1.7 %collective-permute-done.17.t1 = f32[2,128,512]{2,1,0:T(8,128)S(1)} collective-permute-done((f32[2,128,512]{2,1,0:T(8,128)S(1)}, f32[2,128,512]{2,1,0:T(8,128)S(1)}, u32[]{:S(2)}, u32[]{:S(2)}) %collective-permute-start.17) | collective-permute-done | bytes 524320 | tf_op jit(solution)/shard_map/ppermute | solution.py:274
  110.4 2.8 %collective-permute-done.16 = f32[128,256]{1,0:T(8,128)S(1)} collective-permute-done((f32[128,256]{1,0:T(8,128)S(1)}, f32[128,256]{1,0:T(8,128)S(1)}, u32[]{:S(2)}, u32[]{:S(2)}) %collective-permute-start.16) | collective-permute-done | bytes 131104 | tf_op jit(solution)/shard_map/ppermute | solution.py:274
  113.2 3.3 %collective-permute-done.14 = f32[128,256]{1,0:T(8,128)S(1)} collective-permute-done((f32[128,256]{1,0:T(8,128)S(1)}, f32[128,256]{1,0:T(8,128)S(1)}, u32[]{:S(2)}, u32[]{:S(2)}) %collective-permute-start.14) | collective-permute-done | bytes 131104 | tf_op jit(solution)/shard_map/ppermute | solution.py:274
  117.4 2.8 %collective-permute-done.20.far_vectors = f32[4,128,256]{2,1,0:T(8,128)S(1)} collective-permute-done((f32[4,128,256]{2,1,0:T(8,128)S(1)}, f32[4,128,256]{2,1,0:T(8,128)S(1)}, u32[]{:S(2)}, u32[]{:S(2)}) %collective-permute-start.20) | collective-permute-done | bytes 524320 | tf_op jit(solution)/shard_map/ppermute | solution.py:278
  120.1 1.7 %rhs_terms.1 = f32[2,4,256,128]{3,2,1,0:T(8,128)} custom-call(f32[4,128,256]{2,1,0:T(8,128)S(1)} %pad_maximum_fusion.6.own_vectors, f32[4,128,256]{2,1,0:T(8,128)S(1)} %collective-permute-done.20.far_vectors, f32[4,128,512]{2,1,0:T(8,128)S(1)} %get-tuple-element.86.own, f32[4,128,512]{2,1,0:T(8,128)S(1)} %collective-permute-done.21.got, ...), custom_call_target="tpu_custom_call" | custom-call | flops 536870912 | bytes 4194304 | tf_op jit(solution)/shard_map/rhs_terms/pallas_call | solution.py:424
  121.9 4.3 %all-to-all-start.1 = ((f32[4,8,64,128]{3,2,1,0:T(8,128)}), f32[4,8,64,128]{3,2,1,0:T(8,128)S(1)}, u32[]{:S(2)}, u32[]{:S(2)}) async-start(f32[4,8,64,128]{3,2,1,0:T(8,128)} %bitcast.29), calls=%async_computation.1 | async-start | bytes 2097152 | tf_op jit(solution)/shard_map/all_to_all | solution.py:467
  126.4 5.5 %collective-permute-start.22 = (f32[128,64]{0,1:T(8,128)S(1)}, f32[128,64]{0,1:T(8,128)S(1)}, u32[]{:S(2)}, u32[]{:S(2)}) collective-permute-start(f32[128,64]{0,1:T(8,128)S(1)} %dynamic-slice_bitcast_fusion.1), channel_id=1, source_target_pairs={{0,2},{1,3},{2,0},{3,1},{4,6},{5,7},{6,4},{7,5},{8,10},{9,11},{10,... | collective-permute-start | bytes 98312 | tf_op jit(solution)/shard_map/ppermute | solution.py:278
  131.9 2.2 %collective-permute-done.22 = f32[128,64]{0,1:T(8,128)S(1)} collective-permute-done((f32[128,64]{0,1:T(8,128)S(1)}, f32[128,64]{0,1:T(8,128)S(1)}, u32[]{:S(2)}, u32[]{:S(2)}) %collective-permute-start.22) | collective-permute-done | bytes 32800 | tf_op jit(solution)/shard_map/ppermute | solution.py:278
  135.3 6.3 %all-to-all-done.1 = f32[4,8,64,128]{3,2,1,0:T(8,128)S(1)} async-done(((f32[4,8,64,128]{3,2,1,0:T(8,128)}), f32[4,8,64,128]{3,2,1,0:T(8,128)S(1)}, u32[]{:S(2)}, u32[]{:S(2)}) %all-to-all-start.1) | async-done | bytes 1048608 | tf_op jit(solution)/shard_map/all_to_all | solution.py:467
  142.4 7.2 %all-to-all-start.2 = ((f32[8,64,128]{2,1,0:T(8,128)}), f32[8,64,128]{2,1,0:T(8,128)S(1)}, u32[]{:S(2)}, u32[]{:S(2)}) async-start(f32[8,64,128]{2,1,0:T(8,128)} %reduce_sum.18), calls=%async_computation.2 | async-start | bytes 524288 | tf_op jit(solution)/shard_map/all_to_all | solution.py:471
  149.6 11.0 %all-to-all-done.2 = f32[8,64,128]{2,1,0:T(8,128)S(1)} async-done(((f32[8,64,128]{2,1,0:T(8,128)}), f32[8,64,128]{2,1,0:T(8,128)S(1)}, u32[]{:S(2)}, u32[]{:S(2)}) %all-to-all-start.2) | async-done | bytes 262176 | tf_op jit(solution)/shard_map/all_to_all | solution.py:471
  (70 shorter events, 18.2 us)
Async XLA Ops:
  2.5 13.9 %collective-permute-start = (f32[72,128]{1,0:T(8,128)S(1)}, f32[72,128]{1,0:T(8,128)S(1)}, u32[]{:S(2)}, u32[]{:S(2)}) collective-permute-start(f32[72,128]{1,0:T(8,128)S(1)} %select_maximum_fusion), channel_id=1, source_target_pairs={{0,2},{1,3},{2,0},{3,1},{4,6},{5,7},{6,4},{7,5},{8,10},{9,11},{10,... | collective-permute-start | bytes 110600 | tf_op jit(solution)/shard_map/ppermute | solution.py:278
  7.3 18.3 %all-to-all-start = ((f32[8,64,128]{2,1,0:T(8,128)}), f32[8,64,128]{2,1,0:T(8,128)S(1)}, u32[]{:S(2)}, u32[]{:S(2)}) async-start(f32[8,64,128]{2,1,0:T(8,128)} %broadcast_in_dim.2), calls=%async_computation | async-start | bytes 524288 | tf_op jit(solution)/shard_map/all_to_all | solution.py:299
  25.6 8.9 %collective-permute-start.3 = (f32[2,256,128]{2,1,0:T(8,128)S(1)}, f32[2,256,128]{2,1,0:T(8,128)S(1)}, u32[]{:S(2)}, u32[]{:S(2)}) collective-permute-start(f32[2,256,128]{2,1,0:T(8,128)S(1)} %bitcast.66), channel_id=1, source_target_pairs={{0,192},{2,194},{64,128},{66,130},{129,65},{131,67},{193,1},{195,3... | collective-permute-start | bytes 786440 | tf_op jit(solution)/shard_map/ppermute | solution.py:306
  30.5 10.4 %collective-permute-start.2 = (f32[2,256,128]{2,1,0:T(8,128)S(1)}, f32[2,256,128]{2,1,0:T(8,128)S(1)}, u32[]{:S(2)}, u32[]{:S(2)}) collective-permute-start(f32[2,256,128]{2,1,0:T(8,128)S(1)} %bitcast.67), channel_id=1, source_target_pairs={{0,64},{2,66},{64,0},{66,2},{129,193},{131,195},{193,129},{195,131... | collective-permute-start | bytes 786440 | tf_op jit(solution)/shard_map/ppermute | solution.py:306
  32.6 9.0 %collective-permute-start.1 = (f32[2,256,128]{2,1,0:T(8,128)S(1)}, f32[2,256,128]{2,1,0:T(8,128)S(1)}, u32[]{:S(2)}, u32[]{:S(2)}) collective-permute-start(f32[2,256,128]{2,1,0:T(8,128)S(1)} %bitcast.68), channel_id=1, source_target_pairs={{0,128},{2,130},{64,192},{66,194},{129,1},{131,3},{193,65},{195,67... | collective-permute-start | bytes 786440 | tf_op jit(solution)/shard_map/ppermute | solution.py:306
  33.9 35.2 %collective-permute-start.8 = (s32[32,56,128]{2,1,0:T(8,128)}, s32[32,56,128]{2,1,0:T(8,128)S(1)}, u32[]{:S(2)}, u32[]{:S(2)}) collective-permute-start(s32[32,56,128]{2,1,0:T(8,128)} %slice.74), channel_id=1, source_target_pairs={{0,2},{1,3},{2,0},{3,1},{4,6},{5,7},{6,4},{7,5},{8,10},{9,11},{10,... | collective-permute-start | bytes 2752520 | tf_op jit(solution)/shard_map/ppermute | solution.py:278
  41.7 23.1 %collective-permute-start.6 = (f32[4,256,128]{2,1,0:T(8,128)S(1)}, f32[4,256,128]{2,1,0:T(8,128)S(1)}, u32[]{:S(2)}, u32[]{:S(2)}) collective-permute-start(f32[4,256,128]{2,1,0:T(8,128)S(1)} %bitcast.62), channel_id=1, source_target_pairs={{0,24},{8,0},{16,8},{24,16},{1,25},{9,1},{17,9},{25,17},{2,26},{10... | collective-permute-start | bytes 1572872 | tf_op jit(solution)/shard_map/ppermute | solution.py:274
  42.6 22.2 %collective-permute-start.5 = (f32[4,256,128]{2,1,0:T(8,128)S(1)}, f32[4,256,128]{2,1,0:T(8,128)S(1)}, u32[]{:S(2)}, u32[]{:S(2)}) collective-permute-start(f32[4,256,128]{2,1,0:T(8,128)S(1)} %bitcast.63), channel_id=1, source_target_pairs={{0,16},{8,24},{16,0},{24,8},{1,17},{9,25},{17,1},{25,9},{2,18},{10... | collective-permute-start | bytes 1572872 | tf_op jit(solution)/shard_map/ppermute | solution.py:274
  43.7 21.7 %collective-permute-start.4 = (f32[4,256,128]{2,1,0:T(8,128)S(1)}, f32[4,256,128]{2,1,0:T(8,128)S(1)}, u32[]{:S(2)}, u32[]{:S(2)}) collective-permute-start(f32[4,256,128]{2,1,0:T(8,128)S(1)} %bitcast.64), channel_id=1, source_target_pairs={{0,8},{8,16},{16,24},{24,0},{1,9},{9,17},{17,25},{25,1},{2,10},{10... | collective-permute-start | bytes 1572872 | tf_op jit(solution)/shard_map/ppermute | solution.py:274
  45.8 19.8 %collective-permute-start.7 = (f32[2,64,128]{2,1,0:T(8,128)S(1)}, f32[2,64,128]{2,1,0:T(8,128)S(1)}, u32[]{:S(2)}, u32[]{:S(2)}) collective-permute-start(f32[2,64,128]{2,1,0:T(8,128)S(1)} %pad_maximum_fusion.9), channel_id=1, source_target_pairs={{0,1},{1,0},{2,3},{3,2},{4,5},{5,4},{6,7},{7,6},{8,9},{9,8},{10,11... | collective-permute-start | bytes 196616 | tf_op jit(solution)/shard_map/ppermute | solution.py:278
  65.3 3.9 %copy-start.1 = (s32[1,32]{1,0:T(1,128)S(1)}, s32[1,32]{1,0:T(1,128)}, u32[]{:S(2)}) copy-start(s32[1,32]{1,0:T(1,128)} %param.8) | copy-start | bytes 388
  69.2 4.3 %collective-permute-start.9 = (f32[4,4,256,128]{3,2,1,0:T(8,128)S(1)}, f32[4,4,256,128]{3,2,1,0:T(8,128)}, u32[]{:S(2)}, u32[]{:S(2)}) collective-permute-start(f32[4,4,256,128]{3,2,1,0:T(8,128)S(1)} %pad_maximum_fusion.own), channel_id=1, source_target_pairs={{0,4},{4,0},{1,5},{5,1},{2,6},{6,2},{3,7},{7,3},{8,12},{12,8},{9,1... | collective-permute-start | bytes 6291464 | tf_op jit(solution)/shard_map/ppermute | solution.py:278
  69.2 8.4 %collective-permute-start.10 = (s32[32,8,128]{2,1,0:T(8,128)S(1)}, s32[32,8,128]{2,1,0:T(8,128)S(1)}, u32[]{:S(2)}, u32[]{:S(2)}) collective-permute-start(s32[32,8,128]{2,1,0:T(8,128)S(1)} %slice.75), channel_id=1, source_target_pairs={{0,2},{1,3},{2,0},{3,1},{4,6},{5,7},{6,4},{7,5},{8,10},{9,11},{10,... | collective-permute-start | bytes 393224 | tf_op jit(solution)/shard_map/ppermute | solution.py:278
  73.5 4.2 %copy-start = (s32[1,32,128,128]{3,2,1,0:T(8,128)S(1)}, s32[1,32,128,128]{3,2,1,0:T(8,128)}, u32[]{:S(2)}) copy-start(s32[1,32,128,128]{3,2,1,0:T(8,128)} %param.9) | copy-start | bytes 6291460
  81.7 5.6 %collective-permute-start.11 = (f32[128,256]{1,0:T(8,128)S(1)}, f32[128,256]{1,0:T(8,128)S(1)}, u32[]{:S(2)}, u32[]{:S(2)}) collective-permute-start(f32[128,256]{1,0:T(8,128)S(1)} %get-tuple-element.76.pa), channel_id=1, source_target_pairs={{0,1},{1,0},{2,3},{3,2},{4,5},{5,4},{6,7},{7,6},{8,9},{9,8},{10,11... | collective-permute-start | bytes 393224 | tf_op jit(solution)/shard_map/ppermute | solution.py:278
  82.0 28.3 %collective-permute-start.17 = (f32[2,128,512]{2,1,0:T(8,128)S(1)}, f32[2,128,512]{2,1,0:T(8,128)S(1)}, u32[]{:S(2)}, u32[]{:S(2)}) collective-permute-start(f32[2,128,512]{2,1,0:T(8,128)S(1)} %pad_maximum_fusion.3), channel_id=1, source_target_pairs={{0,24},{8,0},{16,8},{24,16},{1,25},{9,1},{17,9},{25,17},{2,26},{10... | collective-permute-start | bytes 1572872 | tf_op jit(solution)/shard_map/ppermute | solution.py:274
  83.0 27.3 %collective-permute-start.18 = (f32[2,128,512]{2,1,0:T(8,128)S(1)}, f32[2,128,512]{2,1,0:T(8,128)S(1)}, u32[]{:S(2)}, u32[]{:S(2)}) collective-permute-start(f32[2,128,512]{2,1,0:T(8,128)S(1)} %pad_maximum_fusion.4), channel_id=1, source_target_pairs={{0,16},{8,24},{16,0},{24,8},{1,17},{9,25},{17,1},{25,9},{2,18},{10... | collective-permute-start | bytes 1572872 | tf_op jit(solution)/shard_map/ppermute | solution.py:274
  91.1 5.1 %collective-permute-start.12 = (f32[128,256]{1,0:T(8,128)S(1)}, f32[128,256]{1,0:T(8,128)S(1)}, u32[]{:S(2)}, u32[]{:S(2)}) collective-permute-start(f32[128,256]{1,0:T(8,128)S(1)} %get-tuple-element.80.pa), channel_id=1, source_target_pairs={{0,1},{1,0},{2,3},{3,2},{4,5},{5,4},{6,7},{7,6},{8,9},{9,8},{10,11... | collective-permute-start | bytes 393224 | tf_op jit(solution)/shard_map/ppermute | solution.py:278
  91.5 18.9 %collective-permute-start.19 = (f32[2,128,512]{2,1,0:T(8,128)S(1)}, f32[2,128,512]{2,1,0:T(8,128)S(1)}, u32[]{:S(2)}, u32[]{:S(2)}) collective-permute-start(f32[2,128,512]{2,1,0:T(8,128)S(1)} %pad_maximum_fusion.5), channel_id=1, source_target_pairs={{0,8},{8,16},{16,24},{24,0},{1,9},{9,17},{17,25},{25,1},{2,10},{10... | collective-permute-start | bytes 1572872 | tf_op jit(solution)/shard_map/ppermute | solution.py:274
  100.3 5.2 %collective-permute-start.13 = (f32[128,256]{1,0:T(8,128)S(1)}, f32[128,256]{1,0:T(8,128)S(1)}, u32[]{:S(2)}, u32[]{:S(2)}) collective-permute-start(f32[128,256]{1,0:T(8,128)S(1)} %get-tuple-element.82.pa), channel_id=1, source_target_pairs={{0,1},{1,0},{2,3},{3,2},{4,5},{5,4},{6,7},{7,6},{8,9},{9,8},{10,11... | collective-permute-start | bytes 393224 | tf_op jit(solution)/shard_map/ppermute | solution.py:278
  105.6 7.6 %collective-permute-start.16 = (f32[128,256]{1,0:T(8,128)S(1)}, f32[128,256]{1,0:T(8,128)S(1)}, u32[]{:S(2)}, u32[]{:S(2)}) collective-permute-start(f32[128,256]{1,0:T(8,128)S(1)} %last_update.1), channel_id=1, source_target_pairs={{0,8},{8,16},{16,24},{24,0},{1,9},{9,17},{17,25},{25,1},{2,10},{10... | collective-permute-start | bytes 393224 | tf_op jit(solution)/shard_map/ppermute | solution.py:274
  106.3 7.0 %collective-permute-start.15 = (f32[128,256]{1,0:T(8,128)S(1)}, f32[128,256]{1,0:T(8,128)S(1)}, u32[]{:S(2)}, u32[]{:S(2)}) collective-permute-start(f32[128,256]{1,0:T(8,128)S(1)} %last_update.1), channel_id=1, source_target_pairs={{0,16},{8,24},{16,0},{24,8},{1,17},{9,25},{17,1},{25,9},{2,18},{10... | collective-permute-start | bytes 393224 | tf_op jit(solution)/shard_map/ppermute | solution.py:274
  110.3 6.2 %collective-permute-start.14 = (f32[128,256]{1,0:T(8,128)S(1)}, f32[128,256]{1,0:T(8,128)S(1)}, u32[]{:S(2)}, u32[]{:S(2)}) collective-permute-start(f32[128,256]{1,0:T(8,128)S(1)} %last_update.1), channel_id=1, source_target_pairs={{0,24},{8,0},{16,8},{24,16},{1,25},{9,1},{17,9},{25,17},{2,26},{10... | collective-permute-start | bytes 393224 | tf_op jit(solution)/shard_map/ppermute | solution.py:274
  116.6 3.5 %collective-permute-start.21 = (f32[4,128,512]{2,1,0:T(8,128)S(1)}, f32[4,128,512]{2,1,0:T(8,128)S(1)}, u32[]{:S(2)}, u32[]{:S(2)}) collective-permute-start(f32[4,128,512]{2,1,0:T(8,128)S(1)} %pad_maximum_fusion.1), channel_id=1, source_target_pairs={{0,4},{4,0},{1,5},{5,1},{2,6},{6,2},{3,7},{7,3},{8,12},{12,8},{9,1... | collective-permute-start | bytes 3145736 | tf_op jit(solution)/shard_map/ppermute | solution.py:278
  116.8 3.4 %collective-permute-start.20 = (f32[4,128,256]{2,1,0:T(8,128)S(1)}, f32[4,128,256]{2,1,0:T(8,128)S(1)}, u32[]{:S(2)}, u32[]{:S(2)}) collective-permute-start(f32[4,128,256]{2,1,0:T(8,128)S(1)} %pad_maximum_fusion.6.own_vectors), channel_id=1, source_target_pairs={{0,4},{4,0},{1,5},{5,1},{2,6},{6,2},{3,7},{7,3},{8,12},{12,8},{9,1... | collective-permute-start | bytes 1572872 | tf_op jit(solution)/shard_map/ppermute | solution.py:278
  121.9 19.7 %all-to-all-start.1 = ((f32[4,8,64,128]{3,2,1,0:T(8,128)}), f32[4,8,64,128]{3,2,1,0:T(8,128)S(1)}, u32[]{:S(2)}, u32[]{:S(2)}) async-start(f32[4,8,64,128]{3,2,1,0:T(8,128)} %bitcast.29), calls=%async_computation.1 | async-start | bytes 2097152 | tf_op jit(solution)/shard_map/all_to_all | solution.py:467
  126.4 7.8 %collective-permute-start.22 = (f32[128,64]{0,1:T(8,128)S(1)}, f32[128,64]{0,1:T(8,128)S(1)}, u32[]{:S(2)}, u32[]{:S(2)}) collective-permute-start(f32[128,64]{0,1:T(8,128)S(1)} %dynamic-slice_bitcast_fusion.1), channel_id=1, source_target_pairs={{0,2},{1,3},{2,0},{3,1},{4,6},{5,7},{6,4},{7,5},{8,10},{9,11},{10,... | collective-permute-start | bytes 98312 | tf_op jit(solution)/shard_map/ppermute | solution.py:278
  142.4 18.2 %all-to-all-start.2 = ((f32[8,64,128]{2,1,0:T(8,128)}), f32[8,64,128]{2,1,0:T(8,128)S(1)}, u32[]{:S(2)}, u32[]{:S(2)}) async-start(f32[8,64,128]{2,1,0:T(8,128)} %reduce_sum.18), calls=%async_computation.2 | async-start | bytes 524288 | tf_op jit(solution)/shard_map/all_to_all | solution.py:471

commit v7 on v6

--- a/solution.py
+++ b/solution.py
@@ -289,9 +289,9 @@
 XC = 0
 NP = 'y'
 XS = 'perm'
-CHUNKS = (56,8)
 YS = 'perm'
 DT = 'after'
+CHUNKS = (56,8)
 
 
 def everyone(value, axis, size):
@@ -312,6 +312,9 @@
     inside = y // 2 == parity
     strip = RANK // 4
     tie = lax.optimization_barrier
+
+    copies = jnp.broadcast_to(items.T[None], (8, strip, TILE))
+    copies, factors_in, tile_user = tie((copies, factors_in, tile_user))
 
     lev = levels[0].reshape(32, 2, HALF, TILE)
     other = pick(lev, 1 - half, 1)
@@ -331,7 +334,8 @@
     high = jnp.where(half == 0, got[:strip], kept)
     pair = jnp.stack([low, high])
     next_pair = flip(pair, "rep", 4, 1)
-    panel = everyone(items.T, ("zh", "rep"), 8).reshape(2, RANK, TILE)
+    panel = lax.all_to_all(copies, ("zh", "rep"), split_axis=0, concat_axis=0, tiled=True)
+    panel = panel.reshape(2, RANK, TILE)
     if NP == "z":
         panel, pair, next_pair, got, *parts = tie((panel, pair, next_pair, got, *parts))
     else:

time: 162 us -> 161 us (level)
  waiting for transfers between devices: 83.3 us -> 79.8 us
  starting transfers between devices: 50.1 us -> 51.8 us
    all_to_all x1, waiting for transfers between devices: 9.12 us -> 2.3 us  [per_device(): lax.all_to_all(copies, ('zh', 'rep'), split_axis=0, concat_axis=0, tiled=...]
    ppermute x11, waiting for transfers between devices: 23.9 us -> 27.5 us  [flip(): return lax.ppermute(value, axis, [(i, i ^ bit) for i in range(size)])]
    all_to_all x1, starting transfers between devices: 6.67 us -> 8.47 us  [per_device(): lax.all_to_all(copies, ('zh', 'rep'), split_axis=0, concat_axis=0, tiled=...]
    all_to_all x1, starting transfers between devices: 7.22 us -> 8.89 us  [per_device(): lax.all_to_all(summed, ('zh', 'rep'), split_axis=0, concat_axis=0, tiled=...]
  transfers between devices with their start and end apart: 26 -> 26, of which waited for: 20 -> 21; matrix products, arithmetic and copies ran while one was open for 4% -> 4% of each run, Pallas kernels for 7% -> 7%
where the time goes in v7:
time: 161 us; the launch traced here: 160 us
  waiting for transfers between devices  79.8 us (50%)
  starting transfers between devices  51.8 us (32%)
  Pallas kernels  17.6 us (11%)
  local copies, waits for them, and re-layouts  6.61 us (4%)
  other arithmetic  3.37 us (2%)
    ppermute x11, waiting for transfers between devices, flip(): return lax.ppermute(value, axis, [(i, i ^ bit) for i in range(size)])  27.5 us
    ppermute x9, waiting for transfers between devices, shift(): lax.ppermute(value, axis, [(i, (i + by) % size) for i in range(size)])  25.3 us
    ppermute x11, starting transfers between devices, flip(): return lax.ppermute(value, axis, [(i, i ^ bit) for i in range(size)])  12.1 us
    all_to_all x1, waiting for transfers between devices, per_device(): lax.all_to_all(summed, ('zh', 'rep'), split_axis=0, concat_axis=0, tiled=...  11 us
    ppermute x9, starting transfers between devices, shift(): lax.ppermute(value, axis, [(i, (i + by) % size) for i in range(size)])  10 us
    all_to_all x1, starting transfers between devices, per_device(): lax.all_to_all(summed, ('zh', 'rep'), split_axis=0, concat_axis=0, tiled=...  8.89 us
    all_to_all x1, starting transfers between devices, per_device(): lax.all_to_all(copies, ('zh', 'rep'), split_axis=0, concat_axis=0, tiled=...  8.47 us
    ppermute x3, starting transfers between devices, along_y(): return lax.ppermute(value, ('y', 'rep'), pairs)  8.28 us
  transfers between devices with their start and end apart: 26, of which 21 were waited for; matrix products, arithmetic and copies ran while one was open for 4% of the time, Pallas kernels for 7%

profile of v7, /device:TPU:6, one launch (start us, length us, event | category | flops | bytes accessed | tf_op | source)
XLA Modules:
  0.0 160.1 jit_solution(1285953708156720961)
XLA Ops:
  0.6 1.5 broadcast_in_dim.2
  2.1 8.5 %all-to-all-start = ((f32[8,64,128]{2,1,0:T(8,128)}), f32[8,64,128]{2,1,0:T(8,128)S(1)}, u32[]{:S(2)}, u32[]{:S(2)}) async-start(f32[8,64,128]{2,1,0:T(8,128)} %broadcast_in_dim.2), calls=%async_computation | async-start | bytes 524288 | tf_op jit(solution)/shard_map/all_to_all | solution.py:337
  12.4 3.0 %collective-permute-start = (f32[72,128]{1,0:T(8,128)S(1)}, f32[72,128]{1,0:T(8,128)S(1)}, u32[]{:S(2)}, u32[]{:S(2)}) collective-permute-start(f32[72,128]{1,0:T(8,128)S(1)} %select_maximum_fusion), channel_id=1, source_target_pairs={{0,2},{1,3},{2,0},{3,1},{4,6},{5,7},{6,4},{7,5},{8,10},{9,11},{10,... | collective-permute-start | bytes 110600 | tf_op jit(solution)/shard_map/ppermute | solution.py:278
  17.9 2.6 %collective-permute-done = f32[72,128]{1,0:T(8,128)S(1)} collective-permute-done((f32[72,128]{1,0:T(8,128)S(1)}, f32[72,128]{1,0:T(8,128)S(1)}, u32[]{:S(2)}, u32[]{:S(2)}) %collective-permute-start) | collective-permute-done | bytes 36896 | tf_op jit(solution)/shard_map/ppermute | solution.py:278
  20.6 2.3 %all-to-all-done = f32[8,64,128]{2,1,0:T(8,128)S(1)} async-done(((f32[8,64,128]{2,1,0:T(8,128)}), f32[8,64,128]{2,1,0:T(8,128)S(1)}, u32[]{:S(2)}, u32[]{:S(2)}) %all-to-all-start) | async-done | bytes 262176 | tf_op jit(solution)/shard_map/all_to_all | solution.py:337
  22.9 4.9 %collective-permute-start.3 = (f32[2,256,128]{2,1,0:T(8,128)S(1)}, f32[2,256,128]{2,1,0:T(8,128)S(1)}, u32[]{:S(2)}, u32[]{:S(2)}) collective-permute-start(f32[2,256,128]{2,1,0:T(8,128)S(1)} %bitcast.66), channel_id=1, source_target_pairs={{0,192},{2,194},{64,128},{66,130},{129,65},{131,67},{193,1},{195,3... | collective-permute-start | bytes 786440 | tf_op jit(solution)/shard_map/ppermute | solution.py:306
  27.8 2.0 %collective-permute-start.2 = (f32[2,256,128]{2,1,0:T(8,128)S(1)}, f32[2,256,128]{2,1,0:T(8,128)S(1)}, u32[]{:S(2)}, u32[]{:S(2)}) collective-permute-start(f32[2,256,128]{2,1,0:T(8,128)S(1)} %bitcast.67), channel_id=1, source_target_pairs={{0,64},{2,66},{64,0},{66,2},{129,193},{131,195},{193,129},{195,131... | collective-permute-start | bytes 786440 | tf_op jit(solution)/shard_map/ppermute | solution.py:306
  31.7 6.4 %collective-permute-done.2 = f32[2,256,128]{2,1,0:T(8,128)S(1)} collective-permute-done((f32[2,256,128]{2,1,0:T(8,128)S(1)}, f32[2,256,128]{2,1,0:T(8,128)S(1)}, u32[]{:S(2)}, u32[]{:S(2)}) %collective-permute-start.2) | collective-permute-done | bytes 262176 | tf_op jit(solution)/shard_map/ppermute | solution.py:306
  40.8 2.1 %collective-permute-start.4 = (f32[4,256,128]{2,1,0:T(8,128)S(1)}, f32[4,256,128]{2,1,0:T(8,128)S(1)}, u32[]{:S(2)}, u32[]{:S(2)}) collective-permute-start(f32[4,256,128]{2,1,0:T(8,128)S(1)} %bitcast.64), channel_id=1, source_target_pairs={{0,8},{8,16},{16,24},{24,0},{1,9},{9,17},{17,25},{25,1},{2,10},{10... | collective-permute-start | bytes 1572872 | tf_op jit(solution)/shard_map/ppermute | solution.py:274
  42.9 1.6 %collective-permute-start.7 = (f32[2,64,128]{2,1,0:T(8,128)S(1)}, f32[2,64,128]{2,1,0:T(8,128)S(1)}, u32[]{:S(2)}, u32[]{:S(2)}) collective-permute-start(f32[2,64,128]{2,1,0:T(8,128)S(1)} %pad_maximum_fusion.9), channel_id=1, source_target_pairs={{0,1},{1,0},{2,3},{3,2},{4,5},{5,4},{6,7},{7,6},{8,9},{9,8},{10,11... | collective-permute-start | bytes 196616 | tf_op jit(solution)/shard_map/ppermute | solution.py:278
  44.5 17.2 %collective-permute-done.6 = f32[4,256,128]{2,1,0:T(8,128)S(1)} collective-permute-done((f32[4,256,128]{2,1,0:T(8,128)S(1)}, f32[4,256,128]{2,1,0:T(8,128)S(1)}, u32[]{:S(2)}, u32[]{:S(2)}) %collective-permute-start.6) | collective-permute-done | bytes 524320 | tf_op jit(solution)/shard_map/ppermute | solution.py:274
  62.6 3.6 %collective-permute-done.8 = s32[32,56,128]{2,1,0:T(8,128)S(1)} collective-permute-done((s32[32,56,128]{2,1,0:T(8,128)}, s32[32,56,128]{2,1,0:T(8,128)S(1)}, u32[]{:S(2)}, u32[]{:S(2)}) %collective-permute-start.8) | collective-permute-done | bytes 917536 | tf_op jit(solution)/shard_map/ppermute | solution.py:278
  67.0 3.4 %collective-permute-done.9.far = f32[4,4,256,128]{3,2,1,0:T(8,128)} collective-permute-done((f32[4,4,256,128]{3,2,1,0:T(8,128)S(1)}, f32[4,4,256,128]{3,2,1,0:T(8,128)}, u32[]{:S(2)}, u32[]{:S(2)}) %collective-permute-start.9) | collective-permute-done | bytes 2097184 | tf_op jit(solution)/shard_map/ppermute | solution.py:278
  70.4 3.8 %first_scores.1 = (bf16[4,256,512]{2,1,0:T(8,128)(2,1)S(1)}, bf16[4,256,512]{2,1,0:T(8,128)(2,1)S(1)}, bf16[4,256,512]{2,1,0:T(8,128)(2,1)S(1)}, bf16[4,256,512]...) custom-call(f32[256,128]{1,0:T(8,128)S(1)} %bitcast.61, ...), custom_call_target="tpu_custom_call" | custom-call | flops 805306368 | bytes 10485760 | tf_op jit(solution)/shard_map/first_scores/pallas_call | solution.py:213
  74.2 1.4 collective-permute-done.10
  75.6 4.1 %first_apply.1 = (bf16[4,128,512]{2,1,0:T(8,128)(2,1)S(1)}, bf16[4,128,512]{2,1,0:T(8,128)(2,1)S(1)}, f32[4,128,512]{2,1,0:T(8,128)S(1)}, f32[4,128,512]{2,1,0:T(8,128)S(1)}, f32[128,256]{1,0:T(8,128)S(1)}) custom-call(s32[67]{0:T(128)S(1)} %concatenate.9.scal, f32[4,128,512]{2,1,0:T(8,128)S(1)} %get-tuple-element.74.refs_0_, ...), custom_call_target="tpu_custom_call" | custom-call | flops 805306368 | bytes 12582912 | tf_op jit(solution)/shard_map/first_apply/pallas_call | solution.py:241
  82.1 3.1 %collective-permute-done.11.pb = f32[128,256]{1,0:T(8,128)S(1)} collective-permute-done((f32[128,256]{1,0:T(8,128)S(1)}, f32[128,256]{1,0:T(8,128)S(1)}, u32[]{:S(2)}, u32[]{:S(2)}) %collective-permute-start.11) | collective-permute-done | bytes 131104 | tf_op jit(solution)/shard_map/ppermute | solution.py:278
  85.2 3.9 %second_apply.1 = (f32[128,256]{1,0:T(8,128)S(1)}, f32[128,256]{1,0:T(8,128)S(1)}) custom-call(f32[128,256]{1,0:T(8,128)S(1)} %get-tuple-element.82.pa, f32[128,256]{1,0:T(8,128)S(1)} %collective-permute-done.11.pb, f32[128,256]{1,0:T(8,128)S(1)} %get-tuple-element.83.x0, bf16[4,256,512]{2,1,0:T(8,128)(2,1)S(1)} %get-tuple-element.76.refs_2_.refs_0_, ...), custom_call_target="tpu_custom_call" | custom-call | flops 1610612736 | bytes 6291456 | tf_op jit(solution)/shard_map/second_apply/pallas_call | solution.py:260
  90.3 3.8 %collective-permute-done.12.pb = f32[128,256]{1,0:T(8,128)S(1)} collective-permute-done((f32[128,256]{1,0:T(8,128)S(1)}, f32[128,256]{1,0:T(8,128)S(1)}, u32[]{:S(2)}, u32[]{:S(2)}) %collective-permute-start.12) | collective-permute-done | bytes 131104 | tf_op jit(solution)/shard_map/ppermute | solution.py:278
  94.1 4.1 %third_apply.1 = (f32[128,256]{1,0:T(8,128)S(1)}, f32[128,256]{1,0:T(8,128)S(1)}, f32[128,256]{1,0:T(8,128)S(1)}, f32[128,256]{1,0:T(8,128)S(1)}) custom-call(f32[128,256]{1,0:T(8,128)S(1)} %get-tuple-element.86.pa, f32[128,256]{1,0:T(8,128)S(1)} %collective-permute-done.12.pb, f32[128,256]{1,0:T(8,128)S(1)} %get-tuple-element.87.resid, ...), custom_call_target="tpu_custom_call" | custom-call | flops 1610612736 | bytes 6291456 | tf_op jit(solution)/shard_map/third_apply/pallas_call | solution.py:260
  98.7 4.7 %collective-permute-done.13.pb = f32[128,256]{1,0:T(8,128)S(1)} collective-permute-done((f32[128,256]{1,0:T(8,128)S(1)}, f32[128,256]{1,0:T(8,128)S(1)}, u32[]{:S(2)}, u32[]{:S(2)}) %collective-permute-start.13) | collective-permute-done | bytes 131104 | tf_op jit(solution)/shard_map/ppermute | solution.py:278
  104.1 2.4 %collective-permute-start.15 = (f32[128,256]{1,0:T(8,128)S(1)}, f32[128,256]{1,0:T(8,128)S(1)}, u32[]{:S(2)}, u32[]{:S(2)}) collective-permute-start(f32[128,256]{1,0:T(8,128)S(1)} %last_update.1), channel_id=1, source_target_pairs={{0,16},{8,24},{16,0},{24,8},{1,17},{9,25},{17,1},{25,9},{2,18},{10... | collective-permute-start | bytes 393224 | tf_op jit(solution)/shard_map/ppermute | solution.py:274
  108.3 2.8 %collective-permute-done.16 = f32[128,256]{1,0:T(8,128)S(1)} collective-permute-done((f32[128,256]{1,0:T(8,128)S(1)}, f32[128,256]{1,0:T(8,128)S(1)}, u32[]{:S(2)}, u32[]{:S(2)}) %collective-permute-start.16) | collective-permute-done | bytes 131104 | tf_op jit(solution)/shard_map/ppermute | solution.py:274
  111.2 2.8 %collective-permute-done.14 = f32[128,256]{1,0:T(8,128)S(1)} collective-permute-done((f32[128,256]{1,0:T(8,128)S(1)}, f32[128,256]{1,0:T(8,128)S(1)}, u32[]{:S(2)}, u32[]{:S(2)}) %collective-permute-start.14) | collective-permute-done | bytes 131104 | tf_op jit(solution)/shard_map/ppermute | solution.py:274
  114.9 2.8 %collective-permute-done.20.far_vectors = f32[4,128,256]{2,1,0:T(8,128)S(1)} collective-permute-done((f32[4,128,256]{2,1,0:T(8,128)S(1)}, f32[4,128,256]{2,1,0:T(8,128)S(1)}, u32[]{:S(2)}, u32[]{:S(2)}) %collective-permute-start.20) | collective-permute-done | bytes 524320 | tf_op jit(solution)/shard_map/ppermute | solution.py:278
  117.6 1.7 %rhs_terms.1 = f32[2,4,256,128]{3,2,1,0:T(8,128)} custom-call(f32[4,128,256]{2,1,0:T(8,128)S(1)} %pad_maximum_fusion.6.own_vectors, f32[4,128,256]{2,1,0:T(8,128)S(1)} %collective-permute-done.20.far_vectors, f32[4,128,512]{2,1,0:T(8,128)S(1)} %get-tuple-element.92.own, f32[4,128,512]{2,1,0:T(8,128)S(1)} %collective-permute-done.21.got, ...), custom_call_target="tpu_custom_call" | custom-call | flops 536870912 | bytes 4194304 | tf_op jit(solution)/shard_map/rhs_terms/pallas_call | solution.py:428
  119.4 4.0 %all-to-all-start.1 = ((f32[4,8,64,128]{3,2,1,0:T(8,128)}), f32[4,8,64,128]{3,2,1,0:T(8,128)S(1)}, u32[]{:S(2)}, u32[]{:S(2)}) async-start(f32[4,8,64,128]{3,2,1,0:T(8,128)} %bitcast.29), calls=%async_computation.1 | async-start | bytes 2097152 | tf_op jit(solution)/shard_map/all_to_all | solution.py:471
  123.5 5.5 %collective-permute-start.22 = (f32[128,64]{0,1:T(8,128)S(1)}, f32[128,64]{0,1:T(8,128)S(1)}, u32[]{:S(2)}, u32[]{:S(2)}) collective-permute-start(f32[128,64]{0,1:T(8,128)S(1)} %dynamic-slice_bitcast_fusion.1), channel_id=1, source_target_pairs={{0,2},{1,3},{2,0},{3,1},{4,6},{5,7},{6,4},{7,5},{8,10},{9,11},{10,... | collective-permute-start | bytes 98312 | tf_op jit(solution)/shard_map/ppermute | solution.py:278
  129.0 2.1 %collective-permute-done.22 = f32[128,64]{0,1:T(8,128)S(1)} collective-permute-done((f32[128,64]{0,1:T(8,128)S(1)}, f32[128,64]{0,1:T(8,128)S(1)}, u32[]{:S(2)}, u32[]{:S(2)}) %collective-permute-start.22) | collective-permute-done | bytes 32800 | tf_op jit(solution)/shard_map/ppermute | solution.py:278
  132.3 6.4 %all-to-all-done.1 = f32[4,8,64,128]{3,2,1,0:T(8,128)S(1)} async-done(((f32[4,8,64,128]{3,2,1,0:T(8,128)}), f32[4,8,64,128]{3,2,1,0:T(8,128)S(1)}, u32[]{:S(2)}, u32[]{:S(2)}) %all-to-all-start.1) | async-done | bytes 1048608 | tf_op jit(solution)/shard_map/all_to_all | solution.py:471
  139.5 8.9 %all-to-all-start.2 = ((f32[8,64,128]{2,1,0:T(8,128)}), f32[8,64,128]{2,1,0:T(8,128)S(1)}, u32[]{:S(2)}, u32[]{:S(2)}) async-start(f32[8,64,128]{2,1,0:T(8,128)} %reduce_sum.18), calls=%async_computation.2 | async-start | bytes 524288 | tf_op jit(solution)/shard_map/all_to_all | solution.py:475
  148.4 11.0 %all-to-all-done.2 = f32[8,64,128]{2,1,0:T(8,128)S(1)} async-done(((f32[8,64,128]{2,1,0:T(8,128)}), f32[8,64,128]{2,1,0:T(8,128)S(1)}, u32[]{:S(2)}, u32[]{:S(2)}) %all-to-all-start.2) | async-done | bytes 262176 | tf_op jit(solution)/shard_map/all_to_all | solution.py:475
  (72 shorter events, 20.7 us)
Async XLA Ops:
  2.1 20.7 %all-to-all-start = ((f32[8,64,128]{2,1,0:T(8,128)}), f32[8,64,128]{2,1,0:T(8,128)S(1)}, u32[]{:S(2)}, u32[]{:S(2)}) async-start(f32[8,64,128]{2,1,0:T(8,128)} %broadcast_in_dim.2), calls=%async_computation | async-start | bytes 524288 | tf_op jit(solution)/shard_map/all_to_all | solution.py:337
  12.4 8.1 %collective-permute-start = (f32[72,128]{1,0:T(8,128)S(1)}, f32[72,128]{1,0:T(8,128)S(1)}, u32[]{:S(2)}, u32[]{:S(2)}) collective-permute-start(f32[72,128]{1,0:T(8,128)S(1)} %select_maximum_fusion), channel_id=1, source_target_pairs={{0,2},{1,3},{2,0},{3,1},{4,6},{5,7},{6,4},{7,5},{8,10},{9,11},{10,... | collective-permute-start | bytes 110600 | tf_op jit(solution)/shard_map/ppermute | solution.py:278
  20.5 2.3 %copy-start.1 = (f32[72,128]{1,0:T(8,128)}, f32[72,128]{1,0:T(8,128)S(1)}, u32[]{:S(2)}) copy-start(f32[72,128]{1,0:T(8,128)S(1)} %collective-permute-done) | copy-start | bytes 110596
  22.9 8.8 %collective-permute-start.3 = (f32[2,256,128]{2,1,0:T(8,128)S(1)}, f32[2,256,128]{2,1,0:T(8,128)S(1)}, u32[]{:S(2)}, u32[]{:S(2)}) collective-permute-start(f32[2,256,128]{2,1,0:T(8,128)S(1)} %bitcast.66), channel_id=1, source_target_pairs={{0,192},{2,194},{64,128},{66,130},{129,65},{131,67},{193,1},{195,3... | collective-permute-start | bytes 786440 | tf_op jit(solution)/shard_map/ppermute | solution.py:306
  27.8 10.3 %collective-permute-start.2 = (f32[2,256,128]{2,1,0:T(8,128)S(1)}, f32[2,256,128]{2,1,0:T(8,128)S(1)}, u32[]{:S(2)}, u32[]{:S(2)}) collective-permute-start(f32[2,256,128]{2,1,0:T(8,128)S(1)} %bitcast.67), channel_id=1, source_target_pairs={{0,64},{2,66},{64,0},{66,2},{129,193},{131,195},{193,129},{195,131... | collective-permute-start | bytes 786440 | tf_op jit(solution)/shard_map/ppermute | solution.py:306
  29.8 8.8 %collective-permute-start.1 = (f32[2,256,128]{2,1,0:T(8,128)S(1)}, f32[2,256,128]{2,1,0:T(8,128)S(1)}, u32[]{:S(2)}, u32[]{:S(2)}) collective-permute-start(f32[2,256,128]{2,1,0:T(8,128)S(1)} %bitcast.68), channel_id=1, source_target_pairs={{0,128},{2,130},{64,192},{66,194},{129,1},{131,3},{193,65},{195,67... | collective-permute-start | bytes 786440 | tf_op jit(solution)/shard_map/ppermute | solution.py:306
  31.2 35.0 %collective-permute-start.8 = (s32[32,56,128]{2,1,0:T(8,128)}, s32[32,56,128]{2,1,0:T(8,128)S(1)}, u32[]{:S(2)}, u32[]{:S(2)}) collective-permute-start(s32[32,56,128]{2,1,0:T(8,128)} %slice.74), channel_id=1, source_target_pairs={{0,2},{1,3},{2,0},{3,1},{4,6},{5,7},{6,4},{7,5},{8,10},{9,11},{10,... | collective-permute-start | bytes 2752520 | tf_op jit(solution)/shard_map/ppermute | solution.py:278
  38.8 23.0 %collective-permute-start.6 = (f32[4,256,128]{2,1,0:T(8,128)S(1)}, f32[4,256,128]{2,1,0:T(8,128)S(1)}, u32[]{:S(2)}, u32[]{:S(2)}) collective-permute-start(f32[4,256,128]{2,1,0:T(8,128)S(1)} %bitcast.62), channel_id=1, source_target_pairs={{0,24},{8,0},{16,8},{24,16},{1,25},{9,1},{17,9},{25,17},{2,26},{10... | collective-permute-start | bytes 1572872 | tf_op jit(solution)/shard_map/ppermute | solution.py:274
  39.7 22.0 %collective-permute-start.5 = (f32[4,256,128]{2,1,0:T(8,128)S(1)}, f32[4,256,128]{2,1,0:T(8,128)S(1)}, u32[]{:S(2)}, u32[]{:S(2)}) collective-permute-start(f32[4,256,128]{2,1,0:T(8,128)S(1)} %bitcast.63), channel_id=1, source_target_pairs={{0,16},{8,24},{16,0},{24,8},{1,17},{9,25},{17,1},{25,9},{2,18},{10... | collective-permute-start | bytes 1572872 | tf_op jit(solution)/shard_map/ppermute | solution.py:274
  40.8 21.6 %collective-permute-start.4 = (f32[4,256,128]{2,1,0:T(8,128)S(1)}, f32[4,256,128]{2,1,0:T(8,128)S(1)}, u32[]{:S(2)}, u32[]{:S(2)}) collective-permute-start(f32[4,256,128]{2,1,0:T(8,128)S(1)} %bitcast.64), channel_id=1, source_target_pairs={{0,8},{8,16},{16,24},{24,0},{1,9},{9,17},{17,25},{25,1},{2,10},{10... | collective-permute-start | bytes 1572872 | tf_op jit(solution)/shard_map/ppermute | solution.py:274
  42.9 19.6 %collective-permute-start.7 = (f32[2,64,128]{2,1,0:T(8,128)S(1)}, f32[2,64,128]{2,1,0:T(8,128)S(1)}, u32[]{:S(2)}, u32[]{:S(2)}) collective-permute-start(f32[2,64,128]{2,1,0:T(8,128)S(1)} %pad_maximum_fusion.9), channel_id=1, source_target_pairs={{0,1},{1,0},{2,3},{3,2},{4,5},{5,4},{6,7},{7,6},{8,9},{9,8},{10,11... | collective-permute-start | bytes 196616 | tf_op jit(solution)/shard_map/ppermute | solution.py:278
  62.4 4.5 %copy-start.2 = (s32[1,32]{1,0:T(1,128)S(1)}, s32[1,32]{1,0:T(1,128)}, u32[]{:S(2)}) copy-start(s32[1,32]{1,0:T(1,128)} %param.8) | copy-start | bytes 388
  66.1 4.3 %collective-permute-start.9 = (f32[4,4,256,128]{3,2,1,0:T(8,128)S(1)}, f32[4,4,256,128]{3,2,1,0:T(8,128)}, u32[]{:S(2)}, u32[]{:S(2)}) collective-permute-start(f32[4,4,256,128]{3,2,1,0:T(8,128)S(1)} %pad_maximum_fusion.own), channel_id=1, source_target_pairs={{0,4},{4,0},{1,5},{5,1},{2,6},{6,2},{3,7},{7,3},{8,12},{12,8},{9,1... | collective-permute-start | bytes 6291464 | tf_op jit(solution)/shard_map/ppermute | solution.py:278
  66.2 9.4 %collective-permute-start.10 = (s32[32,8,128]{2,1,0:T(8,128)S(1)}, s32[32,8,128]{2,1,0:T(8,128)S(1)}, u32[]{:S(2)}, u32[]{:S(2)}) collective-permute-start(s32[32,8,128]{2,1,0:T(8,128)S(1)} %slice.75), channel_id=1, source_target_pairs={{0,2},{1,3},{2,0},{3,1},{4,6},{5,7},{6,4},{7,5},{8,10},{9,11},{10,... | collective-permute-start | bytes 393224 | tf_op jit(solution)/shard_map/ppermute | solution.py:278
  70.4 5.2 %copy-start = (s32[1,32,128,128]{3,2,1,0:T(8,128)S(1)}, s32[1,32,128,128]{3,2,1,0:T(8,128)}, u32[]{:S(2)}) copy-start(s32[1,32,128,128]{3,2,1,0:T(8,128)} %param.9) | copy-start | bytes 6291460
  79.6 5.6 %collective-permute-start.11 = (f32[128,256]{1,0:T(8,128)S(1)}, f32[128,256]{1,0:T(8,128)S(1)}, u32[]{:S(2)}, u32[]{:S(2)}) collective-permute-start(f32[128,256]{1,0:T(8,128)S(1)} %get-tuple-element.82.pa), channel_id=1, source_target_pairs={{0,1},{1,0},{2,3},{3,2},{4,5},{5,4},{6,7},{7,6},{8,9},{9,8},{10,11... | collective-permute-start | bytes 393224 | tf_op jit(solution)/shard_map/ppermute | solution.py:278
  80.0 27.8 %collective-permute-start.17 = (f32[2,128,512]{2,1,0:T(8,128)S(1)}, f32[2,128,512]{2,1,0:T(8,128)S(1)}, u32[]{:S(2)}, u32[]{:S(2)}) collective-permute-start(f32[2,128,512]{2,1,0:T(8,128)S(1)} %pad_maximum_fusion.3), channel_id=1, source_target_pairs={{0,24},{8,0},{16,8},{24,16},{1,25},{9,1},{17,9},{25,17},{2,26},{10... | collective-permute-start | bytes 1572872 | tf_op jit(solution)/shard_map/ppermute | solution.py:274
  80.9 26.9 %collective-permute-start.18 = (f32[2,128,512]{2,1,0:T(8,128)S(1)}, f32[2,128,512]{2,1,0:T(8,128)S(1)}, u32[]{:S(2)}, u32[]{:S(2)}) collective-permute-start(f32[2,128,512]{2,1,0:T(8,128)S(1)} %pad_maximum_fusion.4), channel_id=1, source_target_pairs={{0,16},{8,24},{16,0},{24,8},{1,17},{9,25},{17,1},{25,9},{2,18},{10... | collective-permute-start | bytes 1572872 | tf_op jit(solution)/shard_map/ppermute | solution.py:274
  89.1 5.1 %collective-permute-start.12 = (f32[128,256]{1,0:T(8,128)S(1)}, f32[128,256]{1,0:T(8,128)S(1)}, u32[]{:S(2)}, u32[]{:S(2)}) collective-permute-start(f32[128,256]{1,0:T(8,128)S(1)} %get-tuple-element.86.pa), channel_id=1, source_target_pairs={{0,1},{1,0},{2,3},{3,2},{4,5},{5,4},{6,7},{7,6},{8,9},{9,8},{10,11... | collective-permute-start | bytes 393224 | tf_op jit(solution)/shard_map/ppermute | solution.py:278
  89.5 18.9 %collective-permute-start.19 = (f32[2,128,512]{2,1,0:T(8,128)S(1)}, f32[2,128,512]{2,1,0:T(8,128)S(1)}, u32[]{:S(2)}, u32[]{:S(2)}) collective-permute-start(f32[2,128,512]{2,1,0:T(8,128)S(1)} %pad_maximum_fusion.5), channel_id=1, source_target_pairs={{0,8},{8,16},{16,24},{24,0},{1,9},{9,17},{17,25},{25,1},{2,10},{10... | collective-permute-start | bytes 1572872 | tf_op jit(solution)/shard_map/ppermute | solution.py:274
  98.2 5.2 %collective-permute-start.13 = (f32[128,256]{1,0:T(8,128)S(1)}, f32[128,256]{1,0:T(8,128)S(1)}, u32[]{:S(2)}, u32[]{:S(2)}) collective-permute-start(f32[128,256]{1,0:T(8,128)S(1)} %get-tuple-element.88.pa), channel_id=1, source_target_pairs={{0,1},{1,0},{2,3},{3,2},{4,5},{5,4},{6,7},{7,6},{8,9},{9,8},{10,11... | collective-permute-start | bytes 393224 | tf_op jit(solution)/shard_map/ppermute | solution.py:278
  103.6 7.6 %collective-permute-start.16 = (f32[128,256]{1,0:T(8,128)S(1)}, f32[128,256]{1,0:T(8,128)S(1)}, u32[]{:S(2)}, u32[]{:S(2)}) collective-permute-start(f32[128,256]{1,0:T(8,128)S(1)} %last_update.1), channel_id=1, source_target_pairs={{0,8},{8,16},{16,24},{24,0},{1,9},{9,17},{17,25},{25,1},{2,10},{10... | collective-permute-start | bytes 393224 | tf_op jit(solution)/shard_map/ppermute | solution.py:274
  104.1 7.0 %collective-permute-start.15 = (f32[128,256]{1,0:T(8,128)S(1)}, f32[128,256]{1,0:T(8,128)S(1)}, u32[]{:S(2)}, u32[]{:S(2)}) collective-permute-start(f32[128,256]{1,0:T(8,128)S(1)} %last_update.1), channel_id=1, source_target_pairs={{0,16},{8,24},{16,0},{24,8},{1,17},{9,25},{17,1},{25,9},{2,18},{10... | collective-permute-start | bytes 393224 | tf_op jit(solution)/shard_map/ppermute | solution.py:274
  107.8 6.2 %collective-permute-start.14 = (f32[128,256]{1,0:T(8,128)S(1)}, f32[128,256]{1,0:T(8,128)S(1)}, u32[]{:S(2)}, u32[]{:S(2)}) collective-permute-start(f32[128,256]{1,0:T(8,128)S(1)} %last_update.1), channel_id=1, source_target_pairs={{0,24},{8,0},{16,8},{24,16},{1,25},{9,1},{17,9},{25,17},{2,26},{10... | collective-permute-start | bytes 393224 | tf_op jit(solution)/shard_map/ppermute | solution.py:274
  114.1 3.5 %collective-permute-start.21 = (f32[4,128,512]{2,1,0:T(8,128)S(1)}, f32[4,128,512]{2,1,0:T(8,128)S(1)}, u32[]{:S(2)}, u32[]{:S(2)}) collective-permute-start(f32[4,128,512]{2,1,0:T(8,128)S(1)} %pad_maximum_fusion.1), channel_id=1, source_target_pairs={{0,4},{4,0},{1,5},{5,1},{2,6},{6,2},{3,7},{7,3},{8,12},{12,8},{9,1... | collective-permute-start | bytes 3145736 | tf_op jit(solution)/shard_map/ppermute | solution.py:278
  114.3 3.4 %collective-permute-start.20 = (f32[4,128,256]{2,1,0:T(8,128)S(1)}, f32[4,128,256]{2,1,0:T(8,128)S(1)}, u32[]{:S(2)}, u32[]{:S(2)}) collective-permute-start(f32[4,128,256]{2,1,0:T(8,128)S(1)} %pad_maximum_fusion.6.own_vectors), channel_id=1, source_target_pairs={{0,4},{4,0},{1,5},{5,1},{2,6},{6,2},{3,7},{7,3},{8,12},{12,8},{9,1... | collective-permute-start | bytes 1572872 | tf_op jit(solution)/shard_map/ppermute | solution.py:278
  119.4 19.4 %all-to-all-start.1 = ((f32[4,8,64,128]{3,2,1,0:T(8,128)}), f32[4,8,64,128]{3,2,1,0:T(8,128)S(1)}, u32[]{:S(2)}, u32[]{:S(2)}) async-start(f32[4,8,64,128]{3,2,1,0:T(8,128)} %bitcast.29), calls=%async_computation.1 | async-start | bytes 2097152 | tf_op jit(solution)/shard_map/all_to_all | solution.py:471
  123.5 7.7 %collective-permute-start.22 = (f32[128,64]{0,1:T(8,128)S(1)}, f32[128,64]{0,1:T(8,128)S(1)}, u32[]{:S(2)}, u32[]{:S(2)}) collective-permute-start(f32[128,64]{0,1:T(8,128)S(1)} %dynamic-slice_bitcast_fusion.1), channel_id=1, source_target_pairs={{0,2},{1,3},{2,0},{3,1},{4,6},{5,7},{6,4},{7,5},{8,10},{9,11},{10,... | collective-permute-start | bytes 98312 | tf_op jit(solution)/shard_map/ppermute | solution.py:278
  139.5 19.9 %all-to-all-start.2 = ((f32[8,64,128]{2,1,0:T(8,128)}), f32[8,64,128]{2,1,0:T(8,128)S(1)}, u32[]{:S(2)}, u32[]{:S(2)}) async-start(f32[8,64,128]{2,1,0:T(8,128)} %reduce_sum.18), calls=%async_computation.2 | async-start | bytes 524288 | tf_op jit(solution)/shard_map/all_to_all | solution.py:475
